TPU v7x, 32 devices: a whole 2x2x4 slice. The times are simulated.
32 devices in a mesh: dp: 8 (over y, x, core), mp: 4 (over z).
Axes of the slice: x: 2, y: 2, z: 4, core: 2. Of those that a mesh axis runs over, the one named last changes fastest.
Arguments:
- image: bfloat16 [8, 1024, 1024], P('dp'), may hold values from -6 to 6
- text: bfloat16 [8, 128, 1024], P('dp'), may hold values from -6 to 6
- grad_out: bfloat16 [8, 1024, 1024], P('dp'), may hold values from -6 to 6
- lengths: int32 [8], P('dp'), may hold values from 8 to 128, as said below
- ln1_gain: float32 [1024], replicated, may hold values from 0.5 to 1.5
- ln1_bias: float32 [1024], replicated, may hold values from -1.5 to 1.5
- self_qkv: bfloat16 [1024, 3, 1024], P(None, None, 'mp'), may hold values from -0.1875 to 0.1875
- self_out: bfloat16 [1024, 1024], P('mp'), may hold values from -0.75 to 0.75
- ln2_gain: float32 [1024], replicated, may hold values from 0.5 to 1.5
- ln2_bias: float32 [1024], replicated, may hold values from -1.5 to 1.5
- cross_q: bfloat16 [1024, 1024], P(None, 'mp'), may hold values from -0.1875 to 0.1875
- cross_kv: bfloat16 [1024, 2, 1024], P(None, None, 'mp'), may hold values from -0.1875 to 0.1875
- cross_out: bfloat16 [1024, 1024], P('mp'), may hold values from -0.5 to 0.5
- ln3_gain: float32 [1024], replicated, may hold values from 0.5 to 1.5
- ln3_bias: float32 [1024], replicated, may hold values from -1.5 to 1.5
- mlp_in: bfloat16 [1024, 4096], P(None, 'mp'), may hold values from -0.1875 to 0.1875
- mlp_in_bias: float32 [4096], P('mp'), may hold values from -2.5 to 2.5
- mlp_out: bfloat16 [4096, 1024], P('mp'), may hold values from -0.09375 to 0.09375
- mlp_out_bias: float32 [1024], replicated, may hold values from -1.5 to 1.5
Outputs:
- out: bfloat16 [8, 1024, 1024], P('dp', 'mp')
- image_grad: float32 [8, 1024, 1024], P('dp', 'mp')
- text_grad: float32 [8, 128, 1024], P('dp', 'mp')
- ln1_gain_grad: float32 [1024], replicated
- ln1_bias_grad: float32 [1024], replicated
- self_qkv_grad: float32 [1024, 3, 1024], P(None, None, 'mp')
- self_out_grad: float32 [1024, 1024], P('mp')
- ln2_gain_grad: float32 [1024], replicated
- ln2_bias_grad: float32 [1024], replicated
- cross_q_grad: float32 [1024, 1024], P(None, 'mp')
- cross_kv_grad: float32 [1024, 2, 1024], P(None, None, 'mp')
- cross_out_grad: float32 [1024, 1024], P('mp')
- ln3_gain_grad: float32 [1024], replicated
- ln3_bias_grad: float32 [1024], replicated
- mlp_in_grad: float32 [1024, 4096], P(None, 'mp')
- mlp_in_bias_grad: float32 [4096], P('mp')
- mlp_out_grad: float32 [4096, 1024], P('mp')
- mlp_out_bias_grad: float32 [1024], replicated
Inputs may be any that keep to these rules, and one draw needn't show every extreme that they name: `lengths`: the number of leading text slots that item i's prompt fills; the other slots are padding. Some item has 8 and some item has 128.
All inputs are finite; a program needn't handle non-finite values.
Results may differ from a plain program's by a relative error of at most 0.023.
Values may be sent and summed in bfloat16 or wider, within the bound.
A program may use at most 192 MiB of HBM per device.

v0:
```python
from functools import partial

import jax
import jax.numpy as jnp
from jax import lax
from jax.sharding import PartitionSpec as P

HEAD_DIM = 64


epsilon = 1e-05


def own_rows(value):
    count = value.shape[1] // lax.axis_size("mp")
    return lax.dynamic_slice_in_dim(value, lax.axis_index("mp") * count, count, 1)


def local_rows(value):
    return own_rows(value)


def norm_parts(value):
    center = value - jnp.mean(value, axis=-1, keepdims=True)
    inverse = lax.rsqrt(jnp.mean(center * center, axis=-1, keepdims=True) + epsilon)
    return (center * inverse, inverse)


def norm_back(grad, normal, inverse, gain):
    scaled = grad * gain
    return inverse * (
        scaled
        - jnp.mean(scaled, axis=-1, keepdims=True)
        - normal * jnp.mean(scaled * normal, axis=-1, keepdims=True)
    )


def add_branch(branch_part, residual):
    total = lax.psum_scatter(branch_part, "mp", scatter_dimension=1, tiled=True)
    return residual + total


def spread_normed(residual, gain, shift):
    normal, inverse = norm_parts(residual)
    normed = (normal * gain + shift).astype(jnp.bfloat16)
    spread = lax.all_gather(normed, "mp", axis=1, tiled=True)
    return (spread, normal, inverse)


def input_grad_sum(branch_part):
    total = lax.psum_scatter(branch_part, "mp", scatter_dimension=1, tiled=True)
    return total


def spread_grad(residual_grad):
    rounded = residual_grad.astype(jnp.bfloat16)
    spread = lax.all_gather(rounded, "mp", axis=1, tiled=True)
    return spread


def query_blocks(rows):
    block = min(512, rows)
    return [(start, start + block) for start in range(0, rows, block)]


def causal_mask(start, stop):
    return (
        lax.iota(jnp.int32, stop - start)[:, None] + start >= lax.iota(jnp.int32, stop)[None, :]
    )[None]


def masked_scores(query, keys, allowed):
    scores = jnp.einsum(
        "iqhe,ikhe->ihqk", query, keys, preferred_element_type=jnp.float32
    ) * HEAD_DIM ** (-0.5)
    return jnp.where(allowed[:, None], scores, -1e30)


def attend_forward(query, keys, values, allowed):
    scores = masked_scores(query, keys, allowed)
    largest = jnp.max(scores, axis=-1, keepdims=True)
    powers = jnp.exp(scores - largest)
    total = jnp.sum(powers, axis=-1, keepdims=True)
    weights = (powers / total).astype(jnp.bfloat16)
    mixed = jnp.einsum("ihqk,ikhe->iqhe", weights, values, preferred_element_type=jnp.float32)
    return (mixed.astype(jnp.bfloat16), largest + jnp.log(total))


def attend_backward(query, keys, values, allowed, log_total, grad_mixed):
    weights = jnp.exp(masked_scores(query, keys, allowed) - log_total)
    grad_weights = jnp.einsum(
        "iqhe,ikhe->ihqk", grad_mixed, values, preferred_element_type=jnp.float32
    )
    grad_scores = weights * (grad_weights - jnp.sum(weights * grad_weights, axis=-1, keepdims=True))
    grad_raw = (grad_scores * HEAD_DIM ** (-0.5)).astype(jnp.bfloat16)
    grad_query = jnp.einsum("ihqk,ikhe->iqhe", grad_raw, keys, preferred_element_type=jnp.float32)
    grad_keys = jnp.einsum("ihqk,iqhe->ikhe", grad_raw, query, preferred_element_type=jnp.float32)
    grad_values = jnp.einsum(
        "ihqk,iqhe->ikhe",
        weights.astype(jnp.bfloat16),
        grad_mixed,
        preferred_element_type=jnp.float32,
    )
    return (grad_query, grad_keys, grad_values)


def self_forward(projected):
    mixed_parts = []
    totals = []
    for start, stop in query_blocks(projected.shape[1]):
        mixed, log_total = attend_forward(
            projected[:, start:stop, 0],
            projected[:, :stop, 1],
            projected[:, :stop, 2],
            causal_mask(start, stop),
        )
        mixed_parts.append(mixed)
        totals.append(log_total)
    return (jnp.concatenate(mixed_parts, axis=1), totals)


def self_backward(projected, totals, grad_mixed):
    shape = projected.shape
    grad_keys = jnp.zeros((shape[0], shape[1], shape[3], shape[4]), jnp.float32)
    grad_values = jnp.zeros((shape[0], shape[1], shape[3], shape[4]), jnp.float32)
    query_parts = []
    for index, (start, stop) in enumerate(query_blocks(shape[1])):
        part_query, part_keys, part_values = attend_backward(
            projected[:, start:stop, 0],
            projected[:, :stop, 1],
            projected[:, :stop, 2],
            causal_mask(start, stop),
            totals[index],
            grad_mixed[:, start:stop],
        )
        query_parts.append(part_query)
        grad_keys = grad_keys.at[:, :stop].add(part_keys)
        grad_values = grad_values.at[:, :stop].add(part_values)
    stacked = jnp.stack([jnp.concatenate(query_parts, axis=1), grad_keys, grad_values], axis=2)
    return stacked.astype(jnp.bfloat16).reshape(shape[0], shape[1], 3 * shape[3] * shape[4])


def cross_forward(query, text_proj, allowed):
    mixed_parts = []
    totals = []
    for start, stop in query_blocks(query.shape[1]):
        mixed, log_total = attend_forward(
            query[:, start:stop], text_proj[:, :, 0], text_proj[:, :, 1], allowed
        )
        mixed_parts.append(mixed)
        totals.append(log_total)
    return (jnp.concatenate(mixed_parts, axis=1), totals)


def cross_backward(query, text_proj, allowed, totals, grad_mixed):
    shape = text_proj.shape
    grad_keys = jnp.zeros((shape[0], shape[1], shape[3], shape[4]), jnp.float32)
    grad_values = jnp.zeros((shape[0], shape[1], shape[3], shape[4]), jnp.float32)
    query_parts = []
    for index, (start, stop) in enumerate(query_blocks(query.shape[1])):
        part_query, part_keys, part_values = attend_backward(
            query[:, start:stop],
            text_proj[:, :, 0],
            text_proj[:, :, 1],
            allowed,
            totals[index],
            grad_mixed[:, start:stop],
        )
        query_parts.append(part_query)
        grad_keys = grad_keys + part_keys
        grad_values = grad_values + part_values
    grad_query = jnp.concatenate(query_parts, axis=1).astype(jnp.bfloat16)
    grad_text = jnp.stack([grad_keys, grad_values], axis=2).astype(jnp.bfloat16)
    return (
        grad_query.reshape(query.shape[0], query.shape[1], shape[3] * shape[4]),
        grad_text.reshape(shape[0], shape[1], 2 * shape[3] * shape[4]),
    )


def body(
    image,
    text,
    grad_out,
    lengths,
    ln1_gain,
    ln1_bias,
    self_qkv,
    self_out,
    ln2_gain,
    ln2_bias,
    cross_q,
    cross_kv,
    cross_out,
    ln3_gain,
    ln3_bias,
    mlp_in,
    mlp_in_bias,
    mlp_out,
    mlp_out_bias,
):
    items, rows, width = image.shape
    slots = text.shape[1]
    local = self_out.shape[0]
    heads = local // HEAD_DIM
    joint_weight = self_qkv.reshape(width, 3 * local)
    text_weight = cross_kv.reshape(width, 2 * local)
    image_full = image.astype(jnp.float32)
    normal1, inverse1 = norm_parts(image_full)
    normed1 = (normal1 * ln1_gain + ln1_bias).astype(jnp.bfloat16)
    projected = jnp.einsum("isd,dc->isc", normed1, joint_weight, preferred_element_type=jnp.float32)
    projected = projected.astype(jnp.bfloat16).reshape(items, rows, 3, heads, HEAD_DIM)
    self_mixed, self_totals = self_forward(projected)
    self_mixed = self_mixed.reshape(items, rows, local)
    residual = add_branch(
        jnp.einsum("isc,cd->isd", self_mixed, self_out, preferred_element_type=jnp.float32),
        local_rows(image_full),
    )
    normed2, normal2, inverse2 = spread_normed(residual, ln2_gain, ln2_bias)
    cross_query = jnp.einsum("isd,dc->isc", normed2, cross_q, preferred_element_type=jnp.float32)
    cross_query = cross_query.astype(jnp.bfloat16).reshape(items, rows, heads, HEAD_DIM)
    text_proj = jnp.einsum("itd,dc->itc", text, text_weight, preferred_element_type=jnp.float32)
    text_proj = text_proj.astype(jnp.bfloat16).reshape(items, slots, 2, heads, HEAD_DIM)
    filled = (lax.iota(jnp.int32, slots)[None, :] < lengths[:, None])[:, None, :]
    cross_mixed, cross_totals = cross_forward(cross_query, text_proj, filled)
    cross_mixed = cross_mixed.reshape(items, rows, local)
    residual = add_branch(
        jnp.einsum("isc,cd->isd", cross_mixed, cross_out, preferred_element_type=jnp.float32),
        residual,
    )
    normed3, normal3, inverse3 = spread_normed(residual, ln3_gain, ln3_bias)
    hidden = (
        jnp.einsum("isd,df->isf", normed3, mlp_in, preferred_element_type=jnp.float32) + mlp_in_bias
    )
    active, gelu_back = jax.vjp(partial(jax.nn.gelu, approximate=False), hidden)
    active = active.astype(jnp.bfloat16)
    output = (
        add_branch(
            jnp.einsum("isf,fd->isd", active, mlp_out, preferred_element_type=jnp.float32), residual
        )
        + mlp_out_bias
    )
    result = output.astype(jnp.bfloat16)
    residual_grad = local_rows(grad_out.astype(jnp.float32))
    out_bias_part = jnp.sum(residual_grad, axis=(0, 1))
    mlp_out_grad = jnp.einsum("isf,isd->fd", active, grad_out, preferred_element_type=jnp.float32)
    grad_active = jnp.einsum("isd,fd->isf", grad_out, mlp_out, preferred_element_type=jnp.float32)
    grad_hidden = gelu_back(grad_active)[0].astype(jnp.bfloat16)
    mlp_in_grad = jnp.einsum(
        "isd,isf->df", normed3, grad_hidden, preferred_element_type=jnp.float32
    )
    in_bias_grad = jnp.sum(grad_hidden.astype(jnp.float32), axis=(0, 1))
    grad_normed3 = input_grad_sum(
        jnp.einsum("isf,df->isd", grad_hidden, mlp_in, preferred_element_type=jnp.float32)
    )
    gain3_part = jnp.sum(grad_normed3 * normal3, axis=(0, 1))
    shift3_part = jnp.sum(grad_normed3, axis=(0, 1))
    residual_grad = residual_grad + norm_back(grad_normed3, normal3, inverse3, ln3_gain)
    spread = spread_grad(residual_grad)
    cross_out_grad = jnp.einsum(
        "isc,isd->cd", cross_mixed, spread, preferred_element_type=jnp.float32
    )
    grad_cross_mixed = jnp.einsum(
        "isd,cd->isc", spread, cross_out, preferred_element_type=jnp.float32
    )
    grad_cross_mixed = grad_cross_mixed.astype(jnp.bfloat16).reshape(items, rows, heads, HEAD_DIM)
    grad_query, grad_text_proj = cross_backward(
        cross_query, text_proj, filled, cross_totals, grad_cross_mixed
    )
    cross_q_grad = jnp.einsum(
        "isd,isc->dc", normed2, grad_query, preferred_element_type=jnp.float32
    )
    cross_kv_grad = jnp.einsum(
        "itd,itc->dc", text, grad_text_proj, preferred_element_type=jnp.float32
    ).reshape(width, 2, local)
    query_part = jnp.einsum("isc,dc->isd", grad_query, cross_q, preferred_element_type=jnp.float32)
    text_part = jnp.einsum(
        "itc,dc->itd", grad_text_proj, text_weight, preferred_element_type=jnp.float32
    )
    grad_normed2, text_grad = (
        lax.psum_scatter(query_part, "mp", scatter_dimension=1, tiled=True),
        lax.psum_scatter(text_part, "mp", scatter_dimension=1, tiled=True),
    )
    gain2_part = jnp.sum(grad_normed2 * normal2, axis=(0, 1))
    shift2_part = jnp.sum(grad_normed2, axis=(0, 1))
    residual_grad = residual_grad + norm_back(grad_normed2, normal2, inverse2, ln2_gain)
    spread = spread_grad(residual_grad)
    self_out_grad = jnp.einsum(
        "isc,isd->cd", self_mixed, spread, preferred_element_type=jnp.float32
    )
    grad_self_mixed = jnp.einsum(
        "isd,cd->isc", spread, self_out, preferred_element_type=jnp.float32
    )
    grad_self_mixed = grad_self_mixed.astype(jnp.bfloat16).reshape(items, rows, heads, HEAD_DIM)
    grad_projected = self_backward(projected, self_totals, grad_self_mixed)
    self_qkv_grad = jnp.einsum(
        "isd,isc->dc", normed1, grad_projected, preferred_element_type=jnp.float32
    ).reshape(width, 3, local)
    grad_normed1 = input_grad_sum(
        jnp.einsum("isc,dc->isd", grad_projected, joint_weight, preferred_element_type=jnp.float32)
    )
    normal1_rows = local_rows(normal1)
    inverse1_rows = local_rows(inverse1)
    gain1_part = jnp.sum(grad_normed1 * normal1_rows, axis=(0, 1))
    shift1_part = jnp.sum(grad_normed1, axis=(0, 1))
    image_grad = residual_grad + norm_back(grad_normed1, normal1_rows, inverse1_rows, ln1_gain)
    (
        self_qkv_grad,
        self_out_grad,
        cross_q_grad,
        cross_kv_grad,
        cross_out_grad,
        mlp_in_grad,
        in_bias_grad,
        mlp_out_grad,
    ) = (
        lax.psum(self_qkv_grad.astype(jnp.bfloat16), "dp").astype(jnp.float32),
        lax.psum(self_out_grad.astype(jnp.bfloat16), "dp").astype(jnp.float32),
        lax.psum(cross_q_grad.astype(jnp.bfloat16), "dp").astype(jnp.float32),
        lax.psum(cross_kv_grad.astype(jnp.bfloat16), "dp").astype(jnp.float32),
        lax.psum(cross_out_grad.astype(jnp.bfloat16), "dp").astype(jnp.float32),
        lax.psum(mlp_in_grad.astype(jnp.bfloat16), "dp").astype(jnp.float32),
        lax.psum(in_bias_grad.astype(jnp.bfloat16), "dp").astype(jnp.float32),
        lax.psum(mlp_out_grad.astype(jnp.bfloat16), "dp").astype(jnp.float32),
    )
    gain1, shift1, gain2, shift2, gain3, shift3, out_bias_grad = lax.psum(
        (gain1_part, shift1_part, gain2_part, shift2_part, gain3_part, shift3_part, out_bias_part),
        ("dp", "mp"),
    )
    return (
        result,
        image_grad,
        text_grad,
        gain1,
        shift1,
        self_qkv_grad,
        self_out_grad,
        gain2,
        shift2,
        cross_q_grad,
        cross_kv_grad,
        cross_out_grad,
        gain3,
        shift3,
        mlp_in_grad,
        in_bias_grad,
        mlp_out_grad,
        out_bias_grad,
    )


def solution(mesh):
    in_specs = (
        P("dp", None, None),
        P("dp", None, None),
        P("dp", None, None),
        P("dp"),
        P(),
        P(),
        P(None, None, "mp"),
        P("mp", None),
        P(),
        P(),
        P(None, "mp"),
        P(None, None, "mp"),
        P("mp", None),
        P(),
        P(),
        P(None, "mp"),
        P("mp"),
        P("mp", None),
        P(),
    )
    out_specs = (
        P("dp", "mp", None),
        P("dp", "mp", None),
        P("dp", "mp", None),
        P(),
        P(),
        P(None, None, "mp"),
        P("mp", None),
        P(),
        P(),
        P(None, "mp"),
        P(None, None, "mp"),
        P("mp", None),
        P(),
        P(),
        P(None, "mp"),
        P("mp"),
        P("mp", None),
        P(),
    )
    return jax.shard_map(body, mesh=mesh, in_specs=in_specs, out_specs=out_specs, check_vma=False)
```

profile of v0, /device:TPU:0, one launch (start us, length us, event | category | flops | bytes accessed | tf_op | source)
XLA Modules:
  0.0 1011.4 jit_solution(5812767606807532860)
XLA Ops:
  11.7 2.6 copy.53
  14.8 4.2 fusion.95
  23.9 2.5 fusion.165
  30.2 2.8 convolution_bitcast_fusion.5
  33.3 4.1 convert_element_type.240
  37.4 75.2 %reduce-scatter.8.cloned.1.call-done = f32[1,256,1024]{2,1,0:T(8,128)} async-done(((f32[1,1024,1024]{2,1,0:T(8,128)}), f32[1,256,1024]{2,1,0:T(8,128)}) %reduce-scatter.8.cloned.1.call-update) | async-done | bytes 1048592 | tf_op jit(solution)/shard_map/reduce_scatter | solution.py:39
  120.5 41.8 %all-gather.5.cloned.1.call-done = bf16[1,1024,1024]{2,1,0:T(8,128)(2,1)} async-done(((bf16[1,256,1024]{2,1,0:T(8,128)(2,1)}), bf16[1,1024,1024]{2,1,0:T(8,128)(2,1)}) %all-gather.5.cloned.1.call-update) | async-done | bytes 2097168 | tf_op jit(solution)/shard_map/all_gather | solution.py:46
  162.3 2.4 fusion.128
  169.3 2.8 convolution_bitcast_fusion.4
  172.1 75.6 %reduce-scatter.10.cloned.1.call-done = f32[1,256,1024]{2,1,0:T(8,128)} async-done(((f32[1,1024,1024]{2,1,0:T(8,128)}), f32[1,256,1024]{2,1,0:T(8,128)}) %reduce-scatter.10.cloned.1.call-update) | async-done | bytes 1048592 | tf_op jit(solution)/shard_map/reduce_scatter | solution.py:39
  251.8 46.6 %all-gather.7.cloned.1.call-done = bf16[1,1024,1024]{2,1,0:T(8,128)(2,1)} async-done(((bf16[1,256,1024]{2,1,0:T(8,128)(2,1)}), bf16[1,1024,1024]{2,1,0:T(8,128)(2,1)}) %all-gather.7.cloned.1.call-update) | async-done | bytes 2097168 | tf_op jit(solution)/shard_map/all_gather | solution.py:46
  298.4 13.4 %multiply_convert_fusion.2 = (bf16[1024,1024]{1,0:T(8,128)(2,1)}, f32[1024,1024]{1,0:T(8,128)S(1)}, f32[1024,1024]{1,0:T(8,128)S(1)}) fusion(f32[1024]{0:T(1024)} %param.47, bf16[1024,1024]{1,0:T(8,128)(2,1)S(1)} %copy-done, bf16[1,1024,1024]{2,1,0:T(8,128)(2,1)} %all-gather.7.cloned.1.call-done), kind=kOutput, calls=%fused_computation.25 | convolution fusion | flops 2216689664 | bytes 14684160 | tf_op jit(solution)/shard_map/isd,df->isf/dot_general | solution.py:232
  311.8 4.7 fusion.242
  317.8 4.4 convolution_bitcast_fusion.2
  323.8 5.9 convolution_bitcast_fusion.3
  329.8 68.0 %reduce-scatter.14.cloned.1.call-done = f32[1,256,1024]{2,1,0:T(8,128)} async-done(((f32[1,1024,1024]{2,1,0:T(8,128)}), f32[1,256,1024]{2,1,0:T(8,128)}) %reduce-scatter.14.cloned.1.call-update) | async-done | bytes 1048592 | tf_op jit(solution)/shard_map/reduce_scatter | solution.py:51
  400.2 77.8 %reduce-scatter.12.cloned.1.call-done = f32[1,256,1024]{2,1,0:T(8,128)} async-done(((f32[1,1024,1024]{2,1,0:T(8,128)}), f32[1,256,1024]{2,1,0:T(8,128)}) %reduce-scatter.12.cloned.1.call-update) | async-done | bytes 1048592 | tf_op jit(solution)/shard_map/reduce_scatter | solution.py:39
  478.0 4.2 fusion.235
  482.2 11.3 %reduce-scatter.16.cloned.1.call-start = ((), (), s32[]{:S(2)}) async-start(), calls=%async_computation.14 | async-start | bytes 5242880 | tf_op jit(solution)/shard_map/reduce_scatter | solution.py:280
  494.7 34.1 %all-gather.9.cloned.1.call-done = bf16[1,1024,1024]{2,1,0:T(8,128)(2,1)} async-done(((bf16[1,256,1024]{2,1,0:T(8,128)(2,1)}), bf16[1,1024,1024]{2,1,0:T(8,128)(2,1)}) %all-gather.9.cloned.1.call-update) | async-done | bytes 2097168 | tf_op jit(solution)/shard_map/all_gather | solution.py:57
  528.8 2.4 fusion.134
  533.8 2.9 convolution_convert_fusion.2
  536.7 2.9 convolution_convert_fusion.1
  539.6 4.0 convolution_bitcast_fusion.1
  543.7 75.5 %reduce-scatter.16.cloned.1.call-done = f32[1,256,1024]{2,1,0:T(8,128)} async-done(((f32[1,1024,1024]{2,1,0:T(8,128)}), f32[1,256,1024]{2,1,0:T(8,128)}) %reduce-scatter.16.cloned.1.call-update) | async-done | bytes 1048592 | tf_op jit(solution)/shard_map/reduce_scatter | solution.py:280
  621.6 3.1 fusion.234
  626.0 6.1 fusion.92
  632.1 3.8 fusion.89
  642.3 2.6 fusion.131
  646.4 24.8 %all-gather.11.cloned.1.call-done = bf16[1,1024,1024]{2,1,0:T(8,128)(2,1)} async-done(((bf16[1,256,1024]{2,1,0:T(8,128)(2,1)}), bf16[1,1024,1024]{2,1,0:T(8,128)(2,1)}) %all-gather.11.cloned.1.call-update) | async-done | bytes 2097168 | tf_op jit(solution)/shard_map/all_gather | solution.py:57
  673.6 3.7 fusion.203
  677.3 5.6 fusion.199
  682.9 7.9 fusion.148
  690.9 8.2 fusion.151
  699.1 3.0 fusion.154
  702.1 18.0 %fusion.157 = bf16[1,512,4,64]{1,3,2,0:T(8,128)(2,1)} fusion(f32[4,512,1024]{2,1,0:T(8,128)} %fusion.199, f32[4,512,1024]{2,1,0:T(8,128)} %copy-done.8, f32[4,512]{1,0:T(4,128)S(1)} %copy-done.72, pred[512,1024]{1,0:T(8,128)(4,1)S(1)} %copy-done.20, bf16[1,1024,3,4,64]{1,4,3,2,0:T(8,128)(2,1)} %bitcast.317), kind=kOutput, calls=%fused_computation.134 | convolution fusion | flops 291507200 | bytes 35405824 | tf_op jit(solution)/shard_map/ihqk,ikhe->iqhe/dot_general | solution.py:96
  720.1 18.0 %fusion.119 = bf16[1,1024,1,4,64]{1,4,3,2,0:T(8,128)(2,1)S(1)} fusion(f32[4,512,1024]{2,1,0:T(8,128)} %fusion.199, f32[4,512,1024]{2,1,0:T(8,128)} %copy-done.8, f32[4,512]{1,0:T(4,128)S(1)} %copy-done.72, pred[512,1024]{1,0:T(8,128)(4,1)S(1)} %copy-done.20, f32[1,512,4,64]{1,3,2,0:T(8,128)S(1)} %fusion.151, bf16[1,1024,3,4,64]{1,4,3,2,0:T(8,128)(2,1)} %bitcast.318), kind=kOutput, calls=%fused_computation.117 | convolution fusion | flops 292031488 | bytes 35930112 | tf_op jit(solution)/shard_map/ihqk,iqhe->ikhe/dot_general | solution.py:97
  738.0 4.8 fusion.125
  745.1 3.5 fusion.98
  750.4 5.7 convolution_bitcast_fusion
  758.5 2.5 subtract_multiply_fusion
  761.1 14.6 %psum.117 = bf16[1024]{0:T(1024)(128)(2,1)S(1)} all-reduce(bf16[1024]{0:T(1024)(128)(2,1)S(1)} %copy-done.76), channel_id=1, replica_groups=mesh['dp'=8,'mp'=4] {'dp'}, use_global_device_ids=true, to_apply=%region_50.51 | all-reduce | flops 1024 | bytes 4096 | tf_op jit(solution)/shard_map/psum | solution.py:322
  776.3 101.8 %all-reduce.6.cloned.1.call-done = (bf16[1024,2,256]{0,2,1:T(8,128)(2,1)}, bf16[1024,3,256]{2,0,1:T(8,128)(2,1)}, bf16[256,1024]{1,0:T(8,128)(2,1)}, bf16[1024,2...) async-done(((bf16[1024,2,256]{0,2,1:T(8,128)(2,1)}, bf16[1024,3,256]{2,0,1:T(8,128)(2,1)}, ...) | async-done | bytes 8388624 | tf_op jit(solution)/shard_map/psum | solution.py:319
  878.1 4.2 convert_element_type.295
  882.3 2.5 convert_element_type.298
  894.4 63.1 %reduce-scatter.18.cloned.1.call-done = f32[1,256,1024]{2,1,0:T(8,128)} async-done(((f32[1,1024,1024]{2,1,0:T(8,128)}), f32[1,256,1024]{2,1,0:T(8,128)}) %reduce-scatter.18.cloned.1.call-update) | async-done | bytes 1048592 | tf_op jit(solution)/shard_map/reduce_scatter | solution.py:51
  959.5 41.8 %all-reduce.2 = (f32[1024]{0:T(1024)}, f32[1024]{0:T(1024)}, f32[1024]{0:T(1024)}, f32[1024]{0:T(1024)}, f32[1024]{0:T(1024)}, /*index=5*/f32[1024]{0:T(1024)}, f32[1024]{0:T(1024)}) all-reduce(f32[1024]{0:T(1024)S(1)} %get-tuple-element.118, f32[1024]{0:T(1024)S(1)} %get-tuple-element.129, ...), channel_id=1, replica_groups=mesh['dp'=8,'mp'=4] {'dp','mp'}, use_global_device_ids=true, to_apply=%region_32.33 | all-reduce | flops 7168 | bytes 57344 | tf_op jit(solution)/shard_map/psum | solution.py:325
  1001.3 2.8 multiply_add_fusion
  (271 shorter events, 71.1 us)
Async XLA Ops:
  7.2 291.2 %copy-start = (bf16[1024,1024]{1,0:T(8,128)(2,1)S(1)}, bf16[1024,1024]{1,0:T(8,128)(2,1)}, u32[]{:S(2)}) copy-start(bf16[1024,1024]{1,0:T(8,128)(2,1)} %param.46) | copy-start | bytes 6291460
  7.2 7.5 copy-start.70
  7.2 105.4 %reduce-scatter.8.cloned.1.call-start = ((), (), s32[]{:S(2)}) async-start(), calls=%async_computation.7 | async-start | bytes 5242880 | tf_op jit(solution)/shard_map/reduce_scatter | solution.py:39
  14.7 8.3 copy-start.19
  19.0 9.0 copy-start.32
  33.0 129.3 %all-gather.5.cloned.1.call-start = ((), (), s32[]{:S(2)}) async-start(), calls=%async_computation.8 | async-start | bytes 2621440 | tf_op jit(solution)/shard_map/all_gather | solution.py:46
  33.3 81.3 %copy-start.37 = (f32[1024]{0:T(1024)S(1)}, f32[1024]{0:T(1024)}, u32[]{:S(2)}) copy-start(f32[1024]{0:T(1024)} %param.39) | copy-start | bytes 12292
  33.3 81.3 %copy-start.73 = (f32[1024]{0:T(1024)S(1)}, f32[1024]{0:T(1024)}, u32[]{:S(2)}) copy-start(f32[1024]{0:T(1024)} %param.40) | copy-start | bytes 12292
  37.4 80.8 %copy-start.26 = (bf16[1,128,1024]{2,1,0:T(8,128)(2,1)S(1)}, bf16[1,128,1024]{2,1,0:T(8,128)(2,1)}, u32[]{:S(2)}) copy-start(bf16[1,128,1024]{2,1,0:T(8,128)(2,1)} %param.32) | copy-start | bytes 786436
  114.6 50.1 %copy-start.61 = (f32[256]{0:T(256)}, f32[256]{0:T(256)S(1)}, u32[]{:S(2)}) copy-start(f32[256]{0:T(256)S(1)} %add_rsqrt_fusion.2) | copy-start | bytes 3076
  115.7 132.0 %reduce-scatter.10.cloned.1.call-start = ((), (), s32[]{:S(2)}) async-start(), calls=%async_computation.9 | async-start | bytes 5242880 | tf_op jit(solution)/shard_map/reduce_scatter | solution.py:39
  119.3 46.8 %copy-start.31 = (bf16[128,512]{0,1:T(8,128)(2,1)S(1)}, bf16[128,512]{0,1:T(8,128)(2,1)}, u32[]{:S(2)}) copy-start(bf16[128,512]{0,1:T(8,128)(2,1)} %copy.55) | copy-start | bytes 393220
  172.0 78.6 %copy-start.36 = (f32[1024]{0:T(1024)S(1)}, f32[1024]{0:T(1024)}, u32[]{:S(2)}) copy-start(f32[1024]{0:T(1024)} %param.44) | copy-start | bytes 12292
  172.1 126.3 %all-gather.7.cloned.1.call-start = ((), (), s32[]{:S(2)}) async-start(), calls=%async_computation.10 | async-start | bytes 2621440 | tf_op jit(solution)/shard_map/all_gather | solution.py:46
  251.7 146.1 %reduce-scatter.14.cloned.1.call-start = ((), (), s32[]{:S(2)}) async-start(), calls=%async_computation.12 | async-start | bytes 5242880 | tf_op jit(solution)/shard_map/reduce_scatter | solution.py:51
  298.3 13.4 %copy-start.35 = (bf16[1,1024,1024]{2,1,0:T(8,128)(2,1)S(1)}, bf16[1,1024,1024]{2,1,0:T(8,128)(2,1)}, u32[]{:S(2)}) copy-start(bf16[1,1024,1024]{2,1,0:T(8,128)(2,1)} %param.33) | copy-start | bytes 6291460
  298.3 13.4 %copy-start.77 = (bf16[1024,1024]{1,0:T(8,128)(2,1)S(1)}, bf16[1024,1024]{1,0:T(8,128)(2,1)}, u32[]{:S(2)}) copy-start(bf16[1024,1024]{1,0:T(8,128)(2,1)} %param.48) | copy-start | bytes 6291460
  298.4 13.4 %copy-start.83 = (f32[1024]{0:T(1024)S(1)}, f32[1024]{0:T(1024)}, u32[]{:S(2)}) copy-start(f32[1024]{0:T(1024)} %param.47) | copy-start | bytes 12292
  322.2 155.8 %reduce-scatter.12.cloned.1.call-start = ((), (), s32[]{:S(2)}) async-start(), calls=%async_computation.11 | async-start | bytes 5242880 | tf_op jit(solution)/shard_map/reduce_scatter | solution.py:39
  329.7 68.1 %copy-start.4 = (f32[1,256,1024]{2,1,0:T(8,128)S(1)}, f32[1,256,1024]{2,1,0:T(8,128)}, u32[]{:S(2)}) copy-start(f32[1,256,1024]{2,1,0:T(8,128)} %copy-done.3) | copy-start | bytes 3145732
  329.7 68.1 %copy-start.58 = (f32[256]{0:T(256)S(1)}, f32[256]{0:T(256)}, u32[]{:S(2)}) copy-start(f32[256]{0:T(256)} %copy-done.57) | copy-start | bytes 3076
  329.7 68.1 %copy-start.64 = (f32[256]{0:T(256)S(1)}, f32[256]{0:T(256)}, u32[]{:S(2)}) copy-start(f32[256]{0:T(256)} %copy-done.63) | copy-start | bytes 3076
  329.7 148.3 %copy-start.75 = (f32[1024]{0:T(1024)S(1)}, f32[1024]{0:T(1024)}, u32[]{:S(2)}) copy-start(f32[1024]{0:T(1024)} %param.49) | copy-start | bytes 12292
  329.7 163.7 %copy-start.43 = (f32[4,512]{1,0:T(4,128)S(1)}, f32[4,512]{1,0:T(4,128)}, u32[]{:S(2)}) copy-start(f32[4,512]{1,0:T(4,128)} %copy-done.42) | copy-start | bytes 24580
  329.7 163.7 %copy-start.47 = (f32[4,512]{1,0:T(4,128)S(1)}, f32[4,512]{1,0:T(4,128)}, u32[]{:S(2)}) copy-start(f32[4,512]{1,0:T(4,128)} %copy-done.46) | copy-start | bytes 24580
  329.8 164.3 %copy-start.45 = (f32[4,512]{1,0:T(4,128)S(1)}, f32[4,512]{1,0:T(4,128)}, u32[]{:S(2)}) copy-start(f32[4,512]{1,0:T(4,128)} %copy-done.44) | copy-start | bytes 24580
  329.8 164.3 %copy-start.49 = (f32[4,512]{1,0:T(4,128)S(1)}, f32[4,512]{1,0:T(4,128)}, u32[]{:S(2)}) copy-start(f32[4,512]{1,0:T(4,128)} %copy-done.48) | copy-start | bytes 24580
  329.8 199.0 %all-gather.9.cloned.1.call-start = ((), (), s32[]{:S(2)}) async-start(), calls=%async_computation.13 | async-start | bytes 2621440 | tf_op jit(solution)/shard_map/all_gather | solution.py:57
  482.2 137.1 %reduce-scatter.16.cloned.1.call-start = ((), (), s32[]{:S(2)}) async-start(), calls=%async_computation.14 | async-start | bytes 5242880 | tf_op jit(solution)/shard_map/reduce_scatter | solution.py:280
  494.7 39.1 %copy-start.10 = (f32[4,512,128]{1,2,0:T(8,128)S(1)}, f32[4,512,128]{1,2,0:T(8,128)}, u32[]{:S(2)}) copy-start(f32[4,512,128]{1,2,0:T(8,128)} %copy-done.9) | copy-start | bytes 3145732
  494.7 42.0 %copy-start.12 = (f32[4,512,128]{1,2,0:T(8,128)S(1)}, f32[4,512,128]{1,2,0:T(8,128)}, u32[]{:S(2)}) copy-start(f32[4,512,128]{1,2,0:T(8,128)} %copy-done.11) | copy-start | bytes 3145732
  539.6 79.6 %copy-start.62 = (f32[256]{0:T(256)S(1)}, f32[256]{0:T(256)}, u32[]{:S(2)}) copy-start(f32[256]{0:T(256)} %copy-done.61) | copy-start | bytes 3076
  543.6 81.1 %copy-start.39 = (f32[4,512]{1,0:T(4,128)S(1)}, f32[4,512]{1,0:T(4,128)}, u32[]{:S(2)}) copy-start(f32[4,512]{1,0:T(4,128)} %copy-done.38) | copy-start | bytes 24580
  543.6 81.1 %copy-start.41 = (f32[4,512]{1,0:T(4,128)S(1)}, f32[4,512]{1,0:T(4,128)}, u32[]{:S(2)}) copy-start(f32[4,512]{1,0:T(4,128)} %copy-done.40) | copy-start | bytes 24580
  543.6 81.7 %copy-start.54 = (f32[4,512]{1,0:T(4,128)S(1)}, f32[4,512]{1,0:T(4,128)}, u32[]{:S(2)}) copy-start(f32[4,512]{1,0:T(4,128)} %copy-done.53) | copy-start | bytes 24580
  543.6 81.7 %copy-start.56 = (f32[4,512]{1,0:T(4,128)S(1)}, f32[4,512]{1,0:T(4,128)}, u32[]{:S(2)}) copy-start(f32[4,512]{1,0:T(4,128)} %copy-done.55) | copy-start | bytes 24580
  543.7 127.6 %all-gather.11.cloned.1.call-start = ((), (), s32[]{:S(2)}) async-start(), calls=%async_computation.15 | async-start | bytes 2621440 | tf_op jit(solution)/shard_map/all_gather | solution.py:57
  624.7 253.4 %all-reduce.6.cloned.1.call-start = ((), (), s32[]{:S(2)}) async-start(), calls=%async_computation.18 | async-start | bytes 16777216 | tf_op jit(solution)/shard_map/psum | solution.py:319
  642.3 29.0 %copy-start.30 = (bf16[256,1024]{1,0:T(8,128)(2,1)S(1)}, bf16[256,1024]{1,0:T(8,128)(2,1)}, u32[]{:S(2)}) copy-start(bf16[256,1024]{1,0:T(8,128)(2,1)} %param.38) | copy-start | bytes 1572868
  750.1 207.5 %reduce-scatter.18.cloned.1.call-start = ((), (), s32[]{:S(2)}) async-start(), calls=%async_computation.16 | async-start | bytes 5242880 | tf_op jit(solution)/shard_map/reduce_scatter | solution.py:51
  756.0 248.1 %reduce-scatter.20.cloned.1.call-start = ((), (), s32[]{:S(2)}) async-start(), calls=%async_computation.17 | async-start | bytes 655360 | tf_op jit(solution)/shard_map/reduce_scatter | solution.py:281
  888.9 70.6 %copy-start.65 = (f32[1024]{0:T(1024)S(1)}, f32[1024]{0:T(1024)}, u32[]{:S(2)}) copy-start(f32[1024]{0:T(1024)} %get-tuple-element.120) | copy-start | bytes 12292
  888.9 70.6 %copy-start.66 = (f32[1024]{0:T(1024)S(1)}, f32[1024]{0:T(1024)}, u32[]{:S(2)}) copy-start(f32[1024]{0:T(1024)} %get-tuple-element.127) | copy-start | bytes 12292
  888.9 70.6 %copy-start.67 = (f32[1024]{0:T(1024)S(1)}, f32[1024]{0:T(1024)}, u32[]{:S(2)}) copy-start(f32[1024]{0:T(1024)} %get-tuple-element.154) | copy-start | bytes 12292
  888.9 70.6 %copy-start.68 = (f32[1024]{0:T(1024)S(1)}, f32[1024]{0:T(1024)}, u32[]{:S(2)}) copy-start(f32[1024]{0:T(1024)} %get-tuple-element.122) | copy-start | bytes 12292
  888.9 70.6 %copy-start.69 = (f32[1024]{0:T(1024)S(1)}, f32[1024]{0:T(1024)}, u32[]{:S(2)}) copy-start(f32[1024]{0:T(1024)} %get-tuple-element.128) | copy-start | bytes 12292
  888.9 112.4 %copy-start.13 = (f32[1,256,1024]{2,1,0:T(8,128)S(1)}, f32[1,256,1024]{2,1,0:T(8,128)}, u32[]{:S(2)}) copy-start(f32[1,256,1024]{2,1,0:T(8,128)} %get-tuple-element.145) | copy-start | bytes 3145732
  890.0 114.1 %copy-start.1 = (bf16[1024,1024]{1,0:T(8,128)(2,1)S(1)}, bf16[1024,1024]{1,0:T(8,128)(2,1)}, u32[]{:S(2)}) copy-start(bf16[1024,1024]{1,0:T(8,128)(2,1)} %param.46) | copy-start | bytes 6291460
  (54 other events, 160.8 us)
Sparse Core Ops, SparseCore 0:
  33.1 79.4 reduce-scatter.7
  115.8 46.4 all-gather.4
  172.2 75.4 reduce-scatter.9
  251.9 46.4 all-gather.6
  322.3 75.4 reduce-scatter.13
  400.7 77.2 reduce-scatter.11
  482.3 46.4 all-gather.8
  543.7 75.4 reduce-scatter.15
  624.8 46.4 all-gather.10
  750.2 127.8 all-reduce.5
  880.4 77.0 reduce-scatter.17
  960.3 22.3 reduce-scatter.19
where the time goes:
time: 1020 us; the launch traced here: 1010 us
  waiting for transfers between devices  685 us (67%)
  matrix products  168 us (16%)
  blocking collectives  56.4 us (6%)
  other arithmetic  55 us (5%)
  local copies, waits for them, and re-layouts  19.2 us (2%)
  between operations  16.3 us (2%)
  starting transfers between devices  12.2 us (1%)
    reduce_scatter x3, waiting for transfers between devices, add_branch(): total = lax.psum_scatter(branch_part, 'mp', scatter_dimension=1, tiled=True)  229 us
    reduce_scatter x2, waiting for transfers between devices, input_grad_sum(): total = lax.psum_scatter(branch_part, 'mp', scatter_dimension=1, tiled=True)  131 us
    psum x1, waiting for transfers between devices, body(): lax.psum(cross_kv_grad.astype(jnp.bfloat16), 'dp').astype(jnp.float32)  102 us
    all_gather x2, waiting for transfers between devices, spread_normed(): spread = lax.all_gather(normed, 'mp', axis=1, tiled=True)  88.4 us
    reduce_scatter x1, waiting for transfers between devices, body(): lax.psum_scatter(query_part, 'mp', scatter_dimension=1, tiled=True)  75.5 us
    all_gather x2, waiting for transfers between devices, spread_grad(): spread = lax.all_gather(rounded, 'mp', axis=1, tiled=True)  58.9 us
    psum x1, blocking collectives, body(): lax.psum((gain1_part, shift1_part, gain2_part, shift2_part, gain3_part, s...  41.8 us
    dot_general x4, matrix products, attend_backward(): jnp.einsum('ihqk,ikhe->iqhe', grad_raw, keys, preferred_element_type=jnp....  31.7 us
  transfers between devices with their start and end apart: 12, of which 11 were waited for; matrix products, arithmetic and copies ran while one was open for 7% of the time, Pallas kernels for 0%

commit v1 on v0

v1 whole, which is shorter than its diff:
```python
from functools import partial

import jax
import jax.numpy as jnp
from jax import lax
from jax.experimental import pallas as pl
from jax.experimental.pallas import tpu as pltpu
from jax.sharding import PartitionSpec as P

HEAD_DIM = 64
PAIR = 2 * HEAD_DIM
EPSILON = 1e-05
SCALE = HEAD_DIM ** (-0.5)
MASKED = -1e30
BF = jnp.bfloat16
F32 = jnp.float32
MESH = pl.DeviceIdType.MESH
VMEM_LIMIT = 56 << 20


def nn(a, b):
    return lax.dot_general(a, b, (((1,), (0,)), ((), ())), preferred_element_type=F32)


def nt(a, b):
    return lax.dot_general(a, b, (((1,), (1,)), ((), ())), preferred_element_type=F32)


def tn(a, b):
    return lax.dot_general(a, b, (((0,), (0,)), ((), ())), preferred_element_type=F32)


def norm_parts(value):
    center = value - jnp.mean(value, axis=-1, keepdims=True)
    inverse = lax.rsqrt(jnp.mean(center * center, axis=-1, keepdims=True) + EPSILON)
    return center * inverse, inverse


def half_masks():
    lane = lax.broadcasted_iota(jnp.int32, (1, PAIR), 1)
    first = jnp.where(lane < HEAD_DIM, 1.0, 0.0)
    return first, 1.0 - first


def stack_heads(pair, scale=None):
    first, second = half_masks()
    if scale is not None:
        first, second = first * scale, second * scale
    wide = pair.astype(F32)
    return jnp.concatenate([wide * first, wide * second], axis=0).astype(BF)


def fold_heads(stacked):
    rows = stacked.shape[1] // 2
    both = jnp.concatenate([stacked[:HEAD_DIM, :rows], stacked[HEAD_DIM:, rows:]], axis=0)
    return both.T


def causal(tile_keys, tile_rows):
    key = lax.broadcasted_iota(jnp.int32, (tile_keys, tile_rows), 0)
    row = lax.broadcasted_iota(jnp.int32, (tile_keys, tile_rows), 1)
    both = key <= row
    return jnp.concatenate([both, both], axis=1)


class Place:
    def __init__(self, sizes):
        self.n = sizes["mp"]
        self.dp = sizes["dp"]
        self.share = sizes["share"]
        self.d = lax.axis_index("dp")
        self.m = lax.axis_index("mp")
        self.core = lax.rem(self.d, 2)
        self.partner = (self.d + 1 - 2 * self.core, self.m)
        self.member = lax.rem(self.d, self.share)
        self.chip = self.member // 2
        self.base = self.d - self.member
        self.piece = self.core * (self.share // 2) + self.chip

    def along(self, offset):
        return lax.rem(self.m + offset, self.n)

    def peer(self, offset):
        return (self.d, self.along(offset))

    def chip_peer(self, offset):
        chip = lax.rem(self.chip + offset, self.share // 2)
        return (self.base + 2 * chip + self.core, self.m), self.core * (self.share // 2) + chip


def barrier(devices):
    sem = pltpu.get_barrier_semaphore()
    for device in devices:
        pl.semaphore_signal(sem, inc=1, device_id=device, device_id_type=MESH)
    pl.semaphore_wait(sem, len(devices))


class Gather:
    def __init__(self, place, own, full, offsets, slot_of, sems):
        self.place, self.own, self.full, self.offsets, self.slot_of = place, own, full, offsets, slot_of
        self.rows = own.shape[0]
        self.count = self.rows // place.share
        self.sems = sems

    def rows_of(self, slot, piece, pieces=1):
        start = pl.multiple_of(piece * self.count, self.count)
        return self.full.at[slot, pl.ds(start, pieces * self.count), :]

    def first(self, index):
        place, offset = self.place, self.offsets[index]
        start = pl.multiple_of(place.piece * self.count, self.count)
        return pltpu.make_async_remote_copy(
            src_ref=self.own.at[pl.ds(start, self.count), :],
            dst_ref=self.rows_of(self.slot_of(place.m), place.piece),
            send_sem=self.sems[0].at[index, 0],
            recv_sem=self.sems[1].at[index, 0],
            device_id=place.peer(offset),
            device_id_type=MESH,
        )

    def slot(self, index):
        place = self.place
        return self.slot_of(place.along(place.n - self.offsets[index]))

    def second(self, index, hop):
        place = self.place
        device, _ = place.chip_peer(hop)
        block = self.rows_of(self.slot(index), place.piece)
        return pltpu.make_async_remote_copy(
            src_ref=block,
            dst_ref=block,
            send_sem=self.sems[0].at[index, hop],
            recv_sem=self.sems[1].at[index, hop],
            device_id=device,
            device_id_type=MESH,
        )

    def third(self, index):
        place = self.place
        half = place.share // 2
        block = self.rows_of(self.slot(index), place.core * half, half)
        return pltpu.make_async_remote_copy(
            src_ref=block,
            dst_ref=block,
            send_sem=self.sems[0].at[index, half],
            recv_sem=self.sems[1].at[index, half],
            device_id=place.partner,
            device_id_type=MESH,
        )

    def local(self):
        return pltpu.make_async_copy(self.own, self.full.at[self.slot_of(self.place.m)], self.sems[2])

    def step(self, number):
        hops = range(1, self.place.share // 2)
        for index in range(len(self.offsets)):
            if number == 0:
                self.first(index).start()
            elif number == 1:
                self.first(index).wait_recv()
                for hop in hops:
                    self.second(index, hop).start()
            elif number == 2:
                for hop in hops:
                    self.second(index, hop).wait_recv()
                self.third(index).start()
            else:
                self.third(index).wait()
                self.first(index).wait_send()
                for hop in hops:
                    self.second(index, hop).wait_send()
        if number == 0:
            self.local().start()
        if number == 3:
            self.local().wait()


def attend_block(projected, mixed, totals, i, hp, size, local):
    rows = pl.ds(pl.multiple_of(i * size, size), size)
    column = pl.multiple_of(hp * PAIR, PAIR)
    query = stack_heads(projected[rows, pl.ds(column, PAIR)], SCALE)

    def tile(j, carry, diagonal):
        largest, total, acc = carry
        keys = pl.ds(pl.multiple_of(j * size, size), size)
        key = projected[keys, pl.ds(column + local, PAIR)]
        value = projected[keys, pl.ds(column + 2 * local, PAIR)]
        scores = nt(key, query)
        if diagonal:
            scores = jnp.where(causal(size, size), scores, MASKED)
        top = jnp.maximum(largest, jnp.max(scores, axis=0, keepdims=True))
        powers = jnp.exp(scores - top)
        shrink = jnp.exp(largest - top)
        total = total * shrink + jnp.sum(powers, axis=0, keepdims=True)
        acc = acc * shrink + tn(value, powers.astype(BF))
        return top, total, acc

    carry = (
        jnp.full((1, 2 * size), MASKED, F32),
        jnp.zeros((1, 2 * size), F32),
        jnp.zeros((PAIR, 2 * size), F32),
    )
    carry = tile(i, carry, True)
    largest, total, acc = lax.fori_loop(0, i, lambda j, c: tile(j, c, False), carry)
    mixed[rows, pl.ds(column, PAIR)] = fold_heads(acc / total).astype(BF)
    totals[hp, i] = largest + jnp.log(total)


def attention_kernel(
    sizes,
    image, gain, shift, qkv, text, kv, so, cq, co, mi, mo,
    projected, normed, mixed, totals, mixed_rows, text_proj, so_full, cq_full, co_full, mi_full, mo_full,
    text_own, small_send, small_recv, small_own, wide_send, wide_recv, wide_own,
    mix_send, mix_recv, mix_own, text_send, text_recv, text_local,
):
    place = Place(sizes)
    n, share = place.n, place.share
    rows = image.shape[0]
    size = rows // n
    local = so.shape[0]
    offsets = list(range(1, n))
    greet = [place.peer(k) for k in offsets]
    greet += [place.chip_peer(k)[0] for k in range(1, share // 2)]
    greet.append(place.partner)
    barrier(greet)

    small = [
        Gather(place, own, full, offsets, lambda s: s, (small_send.at[t], small_recv.at[t], small_own.at[t]))
        for t, (own, full) in enumerate(((so, so_full), (cq, cq_full), (co, co_full)))
    ]
    wide = [
        Gather(place, own, full, list(range(2, n, 2)), lambda s: s // 2, (wide_send.at[t], wide_recv.at[t], wide_own.at[t]))
        for t, (own, full) in enumerate(((mi, mi_full), (mo, mo_full)))
    ]
    for item in small + wide:
        item.step(0)

    def project(i, _):
        block = pl.ds(pl.multiple_of(i * size, size), size)
        normal, _ = norm_parts(image[block, :].astype(F32))
        row = (normal * gain[...] + shift[...]).astype(BF)
        normed[block, :] = row
        projected[block, :] = nn(row, qkv[...]).astype(BF)
        return 0

    lax.fori_loop(0, n, project, 0)
    text_own[...] = nn(text[...], kv[...]).astype(BF)

    def text_copy(k):
        return pltpu.make_async_remote_copy(
            src_ref=text_own, dst_ref=text_proj.at[place.m],
            send_sem=text_send.at[k], recv_sem=text_recv.at[k],
            device_id=place.peer(k), device_id_type=MESH,
        )

    for k in offsets:
        text_copy(k).start()
    text_keep = pltpu.make_async_copy(text_own, text_proj.at[place.m], text_local)
    text_keep.start()

    def mix_copy(i):
        gap = lax.rem(i - place.m + n, n)
        block = pl.ds(pl.multiple_of(i * size, size), size)
        return pltpu.make_async_remote_copy(
            src_ref=mixed.at[block, :], dst_ref=mixed_rows.at[place.m],
            send_sem=mix_send.at[gap], recv_sem=mix_recv.at[gap],
            device_id=(place.d, i), device_id_type=MESH,
        )

    def mix_keep():
        block = pl.ds(pl.multiple_of(place.m * size, size), size)
        return pltpu.make_async_copy(mixed.at[block, :], mixed_rows.at[place.m], mix_own)

    plan = [(small[0], 1), (small[1], 1), (small[0], 2), (small[2], 1), (small[1], 2), (small[2], 2)]
    plan += [(wide[0], 1), (wide[1], 1), (wide[0], 2), (wide[1], 2)]
    each = -(-len(plan) // n)
    for i in range(n):
        lax.fori_loop(0, local // PAIR, lambda hp, _: (attend_block(projected, mixed, totals, i, hp, size, local), 0)[1], 0)

        @pl.when(place.m != i)
        def _():
            mix_copy(i).start()

        @pl.when(place.m == i)
        def _():
            mix_keep().start()

        for item, number in plan[i * each : (i + 1) * each]:
            item.step(number)

    for item in small + wide:
        item.step(3)
    for k in offsets:
        text_copy(k).wait()
    text_keep.wait()
    for k in offsets:
        mix_copy(place.along(k)).wait()
    mix_keep().wait()


def share_of(local, dp):
    share = dp
    while (local // share) % 16:
        share //= 2
    return share


def attention(sizes, image, gain, shift, qkv, text, kv, so, cq, co, mi, mo):
    n, share = sizes["mp"], sizes["share"]
    rows, width = image.shape
    slots = text.shape[0]
    local, hidden = so.shape[0], mi.shape[1]
    size = rows // n
    pairs = local // PAIR
    hops = share // 2 + 1
    half = max(n // 2, 1)
    vmem, hbm = pl.BlockSpec(memory_space=pltpu.VMEM), pl.BlockSpec(memory_space=pl.ANY)
    dma = pltpu.SemaphoreType.DMA
    return pl.pallas_call(
        partial(attention_kernel, sizes),
        out_shape=[
            jax.ShapeDtypeStruct((rows, 3 * local), BF),
            jax.ShapeDtypeStruct((rows, width), BF),
            jax.ShapeDtypeStruct((rows, local), BF),
            jax.ShapeDtypeStruct((pairs, n, 1, 2 * size), F32),
            jax.ShapeDtypeStruct((n, size, local), BF),
            jax.ShapeDtypeStruct((n, slots, 2 * local), BF),
            jax.ShapeDtypeStruct((n, local, width), BF),
            jax.ShapeDtypeStruct((n, width, local), BF),
            jax.ShapeDtypeStruct((n, local, width), BF),
            jax.ShapeDtypeStruct((half, width, hidden), BF),
            jax.ShapeDtypeStruct((half, hidden, width), BF),
        ],
        in_specs=[vmem] * 6 + [hbm] * 5,
        out_specs=[vmem] * 4 + [hbm] * 7,
        scratch_shapes=[
            pltpu.VMEM((slots, 2 * local), BF),
            dma((3, n - 1, hops)), dma((3, n - 1, hops)), dma((3,)),
            dma((2, half - 1, hops)), dma((2, half - 1, hops)), dma((2,)),
            dma((n,)), dma((n,)), dma(()),
            dma((n,)), dma((n,)), dma(()),
        ],
        compiler_params=pltpu.CompilerParams(collective_id=1, has_side_effects=True, vmem_limit_bytes=VMEM_LIMIT),
        cost_estimate=pl.CostEstimate(flops=6 << 30, bytes_accessed=32 << 20, transcendentals=4 << 20),
    )(image, gain, shift, qkv, text, kv, so, cq, co, mi, mo)


def row_norm(value, gain, shift):
    normal, inverse = norm_parts(value)
    return (normal * gain + shift).astype(BF), normal, inverse


def norm_back(grad, normal, inverse, gain):
    scaled = grad * gain
    return inverse * (
        scaled
        - jnp.mean(scaled, axis=-1, keepdims=True)
        - normal * jnp.mean(scaled * normal, axis=-1, keepdims=True)
    )


def swap_pairs(value, n):
    return lax.ppermute(value, "mp", [(s, s + 1 - 2 * (s % 2)) for s in range(n)])


def split_heads(value):
    return value.reshape(value.shape[0], -1, HEAD_DIM)


def middle(n, image_rows, grad_rows, grad_pair, length, mixed_rows, text_proj, so, cq, co, mi, mo, in_bias, out_bias,
           gain2, shift2, gain3, shift3):
    size, width = image_rows.shape
    local = so.shape[1]
    mixed = jnp.concatenate(list(mixed_rows), axis=1)
    so, co = so.reshape(-1, width), co.reshape(-1, width)
    cq = jnp.concatenate(list(cq), axis=1)
    first = image_rows + nn(mixed, so)
    n2, normal2, inverse2 = row_norm(first, gain2, shift2)
    query = split_heads(nn(n2, cq).astype(BF))
    keys = split_heads(jnp.concatenate([t[:, :local] for t in text_proj], axis=1))
    values = split_heads(jnp.concatenate([t[:, local:] for t in text_proj], axis=1))
    scores = jnp.einsum("qhe,khe->hqk", query, keys, preferred_element_type=F32) * SCALE
    scores = jnp.where(lax.iota(jnp.int32, keys.shape[0]) < length, scores, MASKED)
    weights = jax.nn.softmax(scores, axis=-1)
    rounded = weights.astype(BF)
    cross = jnp.einsum("hqk,khe->qhe", rounded, values, preferred_element_type=F32).astype(BF).reshape(size, -1)
    second = first + nn(cross, co)
    n3, normal3, inverse3 = row_norm(second, gain3, shift3)
    n3_pair = jnp.stack([n3, swap_pairs(n3, n)])
    hidden = jnp.einsum("psd,kdf->pksf", n3_pair, mi, preferred_element_type=F32) + in_bias[None, :, None, :]
    active, gelu_back = jax.vjp(partial(jax.nn.gelu, approximate=False), hidden)
    active = active.astype(BF)
    out_part = jnp.einsum("pksf,kfd->psd", active, mo, preferred_element_type=F32)
    out = second + out_part[0] + swap_pairs(out_part[1].astype(BF), n).astype(F32) + out_bias
    grad_active = jnp.einsum("psd,kfd->pksf", grad_pair, mo, preferred_element_type=F32)
    grad_hidden = gelu_back(grad_active)[0].astype(BF)
    mo_grad = jnp.einsum("pksf,psd->kfd", active, grad_pair, preferred_element_type=F32)
    mi_grad = jnp.einsum("psd,pksf->kdf", n3_pair, grad_hidden, preferred_element_type=F32)
    in_bias_grad = jnp.sum(grad_hidden.astype(F32), axis=(0, 2))
    dn3_part = jnp.einsum("pksf,kdf->psd", grad_hidden, mi, preferred_element_type=F32)
    dn3 = dn3_part[0] + swap_pairs(dn3_part[1].astype(BF), n).astype(F32)
    residual = grad_rows + norm_back(dn3, normal3, inverse3, gain3)
    r2 = residual.astype(BF)
    co_grad = tn(cross, r2)
    dcross = split_heads(nt(r2, co).astype(BF))
    dweights = jnp.einsum("qhe,khe->hqk", dcross, values, preferred_element_type=F32)
    dscores = weights * (dweights - jnp.sum(weights * dweights, axis=-1, keepdims=True)) * SCALE
    dscores = dscores.astype(BF)
    dquery = jnp.einsum("hqk,khe->qhe", dscores, keys, preferred_element_type=F32).astype(BF).reshape(size, -1)
    dkeys = jnp.einsum("hqk,qhe->khe", dscores, query, preferred_element_type=F32).reshape(keys.shape[0], -1)
    dvalues = jnp.einsum("hqk,qhe->khe", rounded, dcross, preferred_element_type=F32).reshape(keys.shape[0], -1)
    dtext = jnp.concatenate(
        [t[:, g * local : (g + 1) * local] for g in range(n) for t in (dkeys, dvalues)], axis=1
    ).astype(BF)
    cq_grad = tn(n2, dquery)
    dn2 = nt(dquery, cq)
    residual = residual + norm_back(dn2, normal2, inverse2, gain2)
    r1 = residual.astype(BF)
    so_grad = tn(mixed, r1)
    dmixed = nt(r1, so).astype(BF)
    dmixed = jnp.stack([dmixed[:, g * local : (g + 1) * local] for g in range(n)])
    dmixed = lax.all_to_all(dmixed, "mp", 0, 0)
    vectors = [
        jnp.sum(dn2 * normal2, axis=0), jnp.sum(dn2, axis=0), jnp.sum(dn3 * normal3, axis=0), jnp.sum(dn3, axis=0),
        jnp.sum(grad_rows, axis=0),
    ]
    return (out.astype(BF), residual, dmixed.reshape(-1, local), dtext, so_grad, cq_grad, co_grad, mi_grad, mo_grad,
            in_bias_grad, vectors)


def attention_back(n, projected, totals, dmixed, local):
    rows = projected.shape[0]
    heads = local // HEAD_DIM
    q, k, v = (split_heads(projected[:, t * local : (t + 1) * local]) for t in range(3))
    size = rows // n
    log_total = totals.reshape(heads // 2, n, 2, size).transpose(0, 2, 1, 3).reshape(heads, rows)
    scores = jnp.einsum("qhe,khe->hqk", q, k, preferred_element_type=F32) * SCALE
    keep = lax.iota(jnp.int32, rows)[:, None] >= lax.iota(jnp.int32, rows)[None, :]
    weights = jnp.exp(jnp.where(keep, scores, MASKED) - log_total[:, :, None])
    do = split_heads(dmixed)
    dweights = jnp.einsum("qhe,khe->hqk", do, v, preferred_element_type=F32)
    dscores = weights * (dweights - jnp.sum(weights * dweights, axis=-1, keepdims=True)) * SCALE
    dscores = dscores.astype(BF)
    dq = jnp.einsum("hqk,khe->qhe", dscores, k, preferred_element_type=F32)
    dk = jnp.einsum("hqk,qhe->khe", dscores, q, preferred_element_type=F32)
    dv = jnp.einsum("hqk,qhe->khe", weights.astype(BF), do, preferred_element_type=F32)
    return jnp.concatenate([t.reshape(rows, local) for t in (dq, dk, dv)], axis=1).astype(BF)


def body(sizes, image, text, grad_out, lengths, gain1, shift1, qkv, so, gain2, shift2, cq, kv, co, gain3, shift3, mi,
         in_bias, mo, out_bias):
    n = sizes["mp"]
    image, text, grad_out = image[0], text[0], grad_out[0]
    rows, width = image.shape
    size = rows // n
    local = so.shape[0]
    m = lax.axis_index("mp")
    sizes = dict(sizes, share=share_of(local, sizes["dp"]))
    qkv, kv = qkv.reshape(width, 3 * local), kv.reshape(width, 2 * local)
    own = lambda value: lax.dynamic_slice_in_dim(value, m * size, size, 0)
    (projected, normed1, mixed, totals, mixed_rows, text_proj, so_full, cq_full, co_full, mi_full, mo_full) = attention(
        sizes, image, gain1[None], shift1[None], qkv, text, kv, so, cq, co, mi, mo)
    bias_full = lax.all_gather(in_bias, "mp").reshape(n // 2, 2, -1)[:, m % 2]
    image_rows = own(image).astype(F32)
    grad_rows = own(grad_out)
    other = lax.dynamic_slice_in_dim(grad_out, (m + 1 - 2 * (m % 2)) * size, size, 0)
    (out, residual, dmixed, dtext, so_grad, cq_grad, co_grad, mi_grad, mo_grad, in_bias_grad, vectors) = middle(
        n, image_rows, grad_rows.astype(F32), jnp.stack([grad_rows, other]), lengths[0], mixed_rows, text_proj,
        so_full, cq_full, co_full, mi_full, mo_full, bias_full, out_bias, gain2, shift2, gain3, shift3)
    dprojected = attention_back(n, projected, totals, dmixed, local)
    qkv_grad = tn(normed1, dprojected)
    dn1 = lax.psum_scatter(nt(dprojected, qkv).astype(BF), "mp", scatter_dimension=0, tiled=True).astype(F32)
    normal1, inverse1 = norm_parts(image_rows)
    image_grad = residual + norm_back(dn1, normal1, inverse1, gain1)
    dtext = lax.psum_scatter(dtext, "mp", scatter_dimension=1, tiled=True)
    kv_grad = tn(text, dtext)
    text_grad = lax.psum_scatter(nt(dtext, kv).astype(BF), "mp", scatter_dimension=0, tiled=True).astype(F32)
    scatter = lambda value, dim: lax.psum_scatter(value.astype(BF), "mp", scatter_dimension=dim, tiled=True)
    so_grad, co_grad, cq_grad = scatter(so_grad, 0), scatter(co_grad, 0), scatter(cq_grad, 1)

    def own_shard(value):
        total = jnp.zeros((n,) + value.shape[1:], F32)
        for j in range(n // 2):
            total = lax.dynamic_update_index_in_dim(total, value[j], 2 * j + m % 2, 0)
        return lax.psum_scatter(total.astype(BF), "mp", scatter_dimension=0, tiled=True)[0]

    mi_grad, mo_grad, in_bias_grad = own_shard(mi_grad), own_shard(mo_grad), own_shard(in_bias_grad)
    total = lambda value: lax.psum(value.astype(BF), "dp").astype(F32)
    vectors = [jnp.sum(dn1 * normal1, axis=0), jnp.sum(dn1, axis=0)] + vectors
    g1, s1, g2, s2, g3, s3, ob = lax.psum(tuple(vectors), ("dp", "mp"))
    return (
        out[None], image_grad[None], text_grad[None], g1, s1, total(qkv_grad).reshape(width, 3, local), total(so_grad),
        g2, s2, total(cq_grad), total(kv_grad).reshape(width, 2, local), total(co_grad), g3, s3, total(mi_grad),
        total(in_bias_grad), total(mo_grad), ob,
    )


def solution(mesh):
    rows3, rows2, rows1 = P(None, None, "mp"), P(None, "mp"), P("mp")
    item = P("dp", None, None)
    in_specs = (item, item, item, P("dp"), P(), P(), rows3, P("mp", None), P(), P(), rows2, rows3, P("mp", None), P(), P(),
                rows2, rows1, P("mp", None), P())
    split = P("dp", "mp", None)
    out_specs = (split, split, split, P(), P(), rows3, P("mp", None), P(), P(), rows2, rows3, P("mp", None), P(), P(),
                 rows2, rows1, P("mp", None), P())
    sizes = dict(mesh.shape)
    return jax.shard_map(partial(body, sizes), mesh=mesh, in_specs=in_specs, out_specs=out_specs, check_vma=False)
```

time: 1020 us -> 983 us (0.964)
  waiting for transfers between devices: 685 us -> 454 us
  Pallas kernels: 0 us -> 187 us
  local copies, waits for them, and re-layouts: 19.2 us -> 49.7 us
  blocking collectives: 56.4 us -> 85.5 us
  other arithmetic: 55 us -> 28.2 us
  matrix products: 168 us -> 149 us
    pallas_call x0 -> x1, Pallas kernels: none -> 187 us  [attention(): pl.pallas_call(partial(attention_kernel, sizes), out_shape=[jax.ShapeDtyp...]
    all_gather x4 -> x0, waiting for transfers between devices: 147 us -> none  [the longest x2 88.4 us: spread_normed(): spread = lax.all_gather(normed, 'mp', axis=1, tiled=True)]
    reduce_scatter x7 -> x8, waiting for transfers between devices: 435 us -> 343 us  [the longest x2 294 us: own_shard(): lax.psum_scatter(total.astype(BF), 'mp', scatter_dimension=0, tiled=True)[0]]
    dot_general x45 -> x29, matrix products: 168 us -> 146 us  [the longest x1 24 us: attention_back(): dk = jnp.einsum('hqk,qhe->khe', dscores, q, preferred_element_type=F32)]
    all_gather x0 -> x1, blocking collectives: none -> 20.9 us  [body(): bias_full = lax.all_gather(in_bias, 'mp').reshape(n // 2, 2, -1)[:, m % 2]]
    convert_element_type x14 -> x7, other arithmetic: 28.3 us -> 10.7 us  [the longest x6 10.5 us: body(): total = lambda value: lax.psum(value.astype(BF), 'dp').astype(F32)]
    ppermute x0 -> x3, waiting for transfers between devices: none -> 16 us  [swap_pairs(): lax.ppermute(value, 'mp', [(s, s + 1 - 2 * (s % 2)) for s in range(n)])]
    slice x0 -> x10, local copies, waits for them, and re-layouts: none -> 14.4 us  [the longest x4 9.24 us: own_shard(): total = lax.dynamic_update_index_in_dim(total, value[j], 2 * j + m % 2, 0)]
  transfers between devices with their start and end apart: 12 -> 13, of which waited for: 11 -> 8; matrix products, arithmetic and copies ran while one was open for 7% -> 16% of each run, Pallas kernels for 0% -> 0%
where the time goes in v1:
time: 983 us; the launch traced here: 975 us
  waiting for transfers between devices  454 us (46%)
  Pallas kernels  187 us (19%)
  matrix products  149 us (15%)
  blocking collectives  85.5 us (9%)
  local copies, waits for them, and re-layouts  49.7 us (5%)
  other arithmetic  28.2 us (3%)
  between operations  16.1 us (2%)
    reduce_scatter x2, waiting for transfers between devices, own_shard(): lax.psum_scatter(total.astype(BF), 'mp', scatter_dimension=0, tiled=True)[0]  294 us
    pallas_call x1, Pallas kernels, attention(): pl.pallas_call(partial(attention_kernel, sizes), out_shape=[jax.ShapeDtyp...  187 us
    psum x1, waiting for transfers between devices, body(): total = lambda value: lax.psum(value.astype(BF), 'dp').astype(F32)  89.9 us
    psum x1, blocking collectives, body(): g1, s1, g2, s2, g3, s3, ob = lax.psum(tuple(vectors), ('dp', 'mp'))  41.3 us
    reduce_scatter x1, waiting for transfers between devices, body(): lax.psum_scatter(nt(dprojected, qkv).astype(BF), 'mp', scatter_dimension=...  40 us
    dot_general x1, matrix products, attention_back(): dk = jnp.einsum('hqk,qhe->khe', dscores, q, preferred_element_type=F32)  24 us
    dot_general x1, matrix products, attention_back(): dq = jnp.einsum('hqk,khe->qhe', dscores, k, preferred_element_type=F32)  23.3 us
    all_gather x1, blocking collectives, body(): bias_full = lax.all_gather(in_bias, 'mp').reshape(n // 2, 2, -1)[:, m % 2]  20.9 us
  transfers between devices with their start and end apart: 13, of which 8 were waited for; matrix products, arithmetic and copies ran while one was open for 16% of the time, Pallas kernels for 0%

profile of v1, /device:TPU:0, one launch (start us, length us, event | category | flops | bytes accessed | tf_op | source)
XLA Modules:
  0.0 975.5 jit_solution(11962423650086716001)
XLA Ops:
  11.9 186.5 %shard_map.322 = (bf16[1024,768]{1,0:T(8,128)(2,1)}, bf16[1024,1024]{1,0:T(8,128)(2,1)}, bf16[1024,256]{1,0:T(8,128)(2,1)}, f32[2,4,1,512]{3,2,1,0:T(1,128)}, bf...) custom-call(bf16[1024,1024]{1,0:T(8,128)(2,1)} %bitcast.337, ...), custom_call_target="tpu_custom_call" | custom-call | flops 6442450944 | bytes 33554432 | tf_op jit(solution)/shard_map/pallas_call | solution.py:319
  199.6 2.6 fusion.144
  206.4 2.2 fusion.145
  208.6 2.0 convolution_convert_fusion.6
  212.8 20.9 %all-gather = f32[4096]{0:T(1024)S(1)} all-gather(f32[1024]{0:T(1024)S(1)} %copy-done.63), channel_id=2, replica_groups=mesh['dp'=8,'mp'=4] {'mp'}, dimensions={0}, use_global_device_ids=true | all-gather | bytes 20480 | tf_op jit(solution)/shard_map/all_gather | solution.py:463
  237.6 13.1 %fusion.31 = (bf16[2,2,256,1024]{3,2,0,1:T(8,128)(2,1)S(1)}, f32[2,2,256,1024]{3,2,0,1:T(8,128)S(1)}, f32[2,1024,2,256]{1,3,2,0:T(8,128)S(1)}) fusion(f32[2,1024]{1,0:T(2,128)} %bitcast.370, bf16[1,256,1024]{2,1,0:T(8,128)(2,1)} %bitcast.29, bf16[1,256,1024]{2,1,0:T(8,128)(2,1)S(1)} %fusion.181, bf16[2,1024,1024]{2,1,0:T(8,128)(2,1)} %get-tuple-element.33), kind=kOutput, calls=%fused_computation.38 | convolution fusion | flops 2218786816 | bytes 15736832 | tf_op jit(solution)/shard_map/psd,kdf->pksf/dot_general | solution.py:390
  250.8 5.2 convert_reduce_fusion
  255.9 2.4 fusion.59
  258.5 2.3 fusion.56
  261.0 2.1 collective-permute-start.1
  263.0 10.3 %collective-permute-done.2 = bf16[256,1024]{1,0:T(8,128)(2,1)S(1)} collective-permute-done((bf16[256,1024]{1,0:T(8,128)(2,1)S(1)}, bf16[256,1024]{1,0:T(8,128)(2,1)S(1)}, u32[]{:S(2)}, u32[]{:S(2)}) %collective-permute-start.2) | collective-permute-done | bytes 524320 | tf_op jit(solution)/shard_map/ppermute | solution.py:363
  274.4 5.7 collective-permute-done.1
  284.3 2.8 convolution_convert_fusion.11
  287.1 4.3 fusion.81
  292.5 4.3 fusion.69
  296.8 2.9 convolution_convert_fusion.1
  299.9 3.1 multiply_reduce_fusion.3
  304.0 2.1 convolution_convert_fusion.2
  308.4 4.1 convolution_bitcast_fusion.1
  312.5 2.4 fusion.137
  314.9 2.9 copy.115
  317.8 3.9 copy.116
  321.7 4.3 broadcast.140.clone
  331.1 4.0 convolution_bitcast_fusion
  335.0 4.3 broadcast.140.clone.1
  342.4 2.7 fusion.138
  346.8 3.5 all-to-all-start
  354.4 9.4 subtract_exponential_fusion
  363.8 4.6 all-to-all-done
  369.1 8.3 fusion.148
  377.4 23.3 %fusion.72 = bf16[4,64,1024]{2,1,0:T(8,128)(2,1)} fusion(bf16[1024,4,64]{0,2,1:T(8,128)(2,1)S(1)} %bitcast.355, f32[4,1024,1024]{1,2,0:T(8,128)} %subtract_exponential_fusion, f32[4,1024,1024]{1,2,0:T(8,128)} %fusion.148), kind=kOutput, calls=%fused_computation.93 | convolution fusion | flops 558109696 | bytes 34603008 | tf_op jit(solution)/shard_map/hqk,khe->qhe/dot_general | solution.py:444
  400.7 8.6 fusion.66
  409.4 2.1 convolution_convert_fusion.10
  411.8 24.0 %fusion.75 = bf16[4,64,1024]{2,1,0:T(8,128)(2,1)} fusion(bf16[1024,4,64]{0,2,1:T(8,128)(2,1)} %bitcast.353, f32[4,1024,1024]{1,2,0:T(8,128)} %subtract_exponential_fusion, f32[4,1024,1024]{1,2,0:T(8,128)} %fusion.148), kind=kOutput, calls=%fused_computation.94 | convolution fusion | flops 558109696 | bytes 34603008 | tf_op jit(solution)/shard_map/hqk,qhe->khe/dot_general | solution.py:445
  435.8 4.4 convolution_convert_fusion.3
  440.2 3.8 convolution_convert_fusion.4
  448.0 9.2 reduce-scatter.19.cloned.1.call-done
  457.2 146.1 %reduce-scatter.21.cloned.1.call-done = bf16[1,1024,1024]{2,1,0:T(8,128)(2,1)} async-done(((bf16[4,1024,1024]{2,1,0:T(8,128)(2,1)}), bf16[1,1024,1024]{2,1,0:T(8,128)(2,1)}) %reduce-scatter.21.cloned.1.call-update) | async-done | bytes 2097168 | tf_op jit(solution)/shard_map/reduce_scatter | solution.py:485
  603.4 147.6 %reduce-scatter.23.cloned.1.call-done = bf16[1,1024,1024]{2,1,0:T(8,128)(2,1)} async-done(((bf16[4,1024,1024]{2,1,0:T(8,128)(2,1)}), bf16[1,1024,1024]{2,1,0:T(8,128)(2,1)}) %reduce-scatter.23.cloned.1.call-update) | async-done | bytes 2097168 | tf_op jit(solution)/shard_map/reduce_scatter | solution.py:485
  753.2 11.3 %all-reduce = bf16[4,1024]{1,0:T(4,128)(2,1)S(1)} all-reduce(bf16[4,1024]{1,0:T(4,128)(2,1)S(1)} %dynamic_update_slice.23), channel_id=10, replica_groups=mesh['dp'=8,'mp'=4] {'mp'}, use_global_device_ids=true, to_apply=%region_42.43.clone | all-reduce | flops 4096 | bytes 16384
  765.2 12.0 %psum.117 = bf16[1024]{0:T(1024)(128)(2,1)S(1)} all-reduce(bf16[1024]{0:T(1024)(128)(2,1)S(1)} %dynamic-slice_reduce_fusion), channel_id=1, replica_groups=mesh['dp'=8,'mp'=4] {'dp'}, use_global_device_ids=true, to_apply=%region_43.44 | all-reduce | flops 1024 | bytes 4096 | tf_op jit(solution)/shard_map/psum | solution.py:488
  779.3 40.0 %reduce-scatter.9.cloned.1.call-done = bf16[256,1024]{1,0:T(8,128)(2,1)} async-done(((bf16[1024,1024]{1,0:T(8,128)(2,1)}), bf16[256,1024]{1,0:T(8,128)(2,1)}) %reduce-scatter.9.cloned.1.call-update) | async-done | bytes 524304 | tf_op jit(solution)/shard_map/reduce_scatter | solution.py:472
  821.0 41.3 %all-reduce.1 = (f32[1024]{0:T(1024)}, f32[1024]{0:T(1024)}, f32[1024]{0:T(1024)}, f32[1024]{0:T(1024)}, f32[1024]{0:T(1024)}, /*index=5*/f32[1024]{0:T(1024)}, f32[1024]{0:T(1024)}) all-reduce(f32[1024]{0:T(1024)S(1)} %get-tuple-element.41, f32[1024]{0:T(1024)S(1)} %get-tuple-element.49, ...), channel_id=1, replica_groups=mesh['dp'=8,'mp'=4] {'dp','mp'}, use_global_device_ids=true, to_apply=%region_20.21 | all-reduce | flops 7168 | bytes 57344 | tf_op jit(solution)/shard_map/psum | solution.py:490
  862.3 2.4 fusion.87
  864.7 89.9 %all-reduce.5.cloned.1.call-done = (bf16[1024,3,256]{2,0,1:T(8,128)(2,1)}, bf16[256,1024]{1,0:T(8,128)(2,1)}, bf16[1024,256]{1,0:T(8,128)(2,1)}, bf16[1024,2,256...) async-done(((bf16[1024,3,256]{2,0,1:T(8,128)(2,1)}, bf16[256,1024]{1,0:T(8,128)(2,1)}, ...) | async-done | bytes 8388624 | tf_op jit(solution)/shard_map/psum | solution.py:488
  954.6 4.2 convert_element_type.181
  958.8 2.5 convert_element_type.186
  963.2 2.0 reshape.215
  (258 shorter events, 55.5 us)
Async XLA Ops:
  7.2 402.1 %reduce-scatter.11.cloned.1.call-start = ((), (), s32[]{:S(2)}) async-start(), calls=%async_computation.10 | async-start | bytes 655360 | tf_op jit(solution)/shard_map/reduce_scatter | solution.py:475
  9.1 189.4 %copy-start.3 = (bf16[1024,3,256]{0,2,1:T(8,128)(2,1)}, bf16[1024,3,256]{0,2,1:T(8,128)(2,1)S(1)}, u32[]{:S(2)}) copy-start(bf16[1024,3,256]{0,2,1:T(8,128)(2,1)S(1)} %copy.94) | copy-start | bytes 4718596
  199.6 4.5 copy-start.55
  199.6 4.5 copy-start.62
  205.5 5.1 copy-start.44
  212.2 25.4 %collective-permute-start = (bf16[256,1024]{1,0:T(8,128)(2,1)S(1)}, bf16[256,1024]{1,0:T(8,128)(2,1)}, u32[]{:S(2)}, u32[]{:S(2)}) collective-permute-start(bf16[256,1024]{1,0:T(8,128)(2,1)S(1)} %add_convert_fusion), channel_id=1, source_target_pairs={{0,1},{1,0},{2,3},{3,2},{4,5},{5,4},{6,7},{7,6},{8,9},{9,8},{10,11... | collective-permute-start | bytes 1572872 | tf_op jit(solution)/shard_map/ppermute | solution.py:363
  236.1 44.1 %copy-start.14 = (bf16[1,256,1024]{2,1,0:T(8,128)(2,1)}, bf16[1,256,1024]{2,1,0:T(8,128)(2,1)S(1)}, u32[]{:S(2)}) copy-start(bf16[1,256,1024]{2,1,0:T(8,128)(2,1)S(1)} %get-tuple-element.65) | copy-start | bytes 1572868
  237.3 13.4 %copy-start.30 = (bf16[1,256,1024]{2,1,0:T(8,128)(2,1)}, bf16[1,256,1024]{2,1,0:T(8,128)(2,1)S(1)}, u32[]{:S(2)}) copy-start(bf16[1,256,1024]{2,1,0:T(8,128)(2,1)S(1)} %constant_dynamic-slice_fusion) | copy-start | bytes 1572868
  237.6 13.1 %copy-start.25 = (bf16[1,256,1024]{2,1,0:T(8,128)(2,1)}, bf16[1,256,1024]{2,1,0:T(8,128)(2,1)S(1)}, u32[]{:S(2)}) copy-start(bf16[1,256,1024]{2,1,0:T(8,128)(2,1)S(1)} %fusion.181) | copy-start | bytes 1572868
  237.6 13.1 %copy-start.61 = (f32[2,1,1024]{2,0,1:T(2,128)S(1)}, f32[2,1,1024]{2,0,1:T(2,128)}, u32[]{:S(2)}) copy-start(f32[2,1,1024]{2,0,1:T(2,128)} %copy.135) | copy-start | bytes 24580
  237.6 13.1 %copy-start.71 = (bf16[2,1024,1024]{2,1,0:T(8,128)(2,1)S(1)}, bf16[2,1024,1024]{2,1,0:T(8,128)(2,1)}, u32[]{:S(2)}) copy-start(bf16[2,1024,1024]{2,1,0:T(8,128)(2,1)} %get-tuple-element.34) | copy-start | bytes 12582916
  250.7 7.8 copy-start.68
  250.8 5.2 copy-start.70
  258.4 14.9 %collective-permute-start.2 = (bf16[256,1024]{1,0:T(8,128)(2,1)S(1)}, bf16[256,1024]{1,0:T(8,128)(2,1)S(1)}, u32[]{:S(2)}, u32[]{:S(2)}) collective-permute-start(bf16[256,1024]{1,0:T(8,128)(2,1)S(1)} %fusion.104), channel_id=1, source_target_pairs={{0,1},{1,0},{2,3},{3,2},{4,5},{5,4},{6,7},{7,6},{8,9},{9,8},{10,11... | collective-permute-start | bytes 1572872 | tf_op jit(solution)/shard_map/ppermute | solution.py:363
  258.5 21.7 %copy-start.66 = (f32[1024]{0:T(1024)S(1)}, f32[1024]{0:T(1024)}, u32[]{:S(2)}) copy-start(f32[1024]{0:T(1024)} %param.37) | copy-start | bytes 12292
  260.9 20.5 %copy-start.1 = (bf16[4,256,1024]{2,1,0:T(8,128)(2,1)S(1)}, bf16[4,256,1024]{2,1,0:T(8,128)(2,1)}, u32[]{:S(2)}) copy-start(bf16[4,256,1024]{2,1,0:T(8,128)(2,1)} %get-tuple-element.32) | copy-start | bytes 6291460
  261.0 19.2 %collective-permute-start.1 = (bf16[256,1024]{1,0:T(8,128)(2,1)S(1)}, bf16[256,1024]{1,0:T(8,128)(2,1)S(1)}, u32[]{:S(2)}, u32[]{:S(2)}) collective-permute-start(bf16[256,1024]{1,0:T(8,128)(2,1)S(1)} %fusion.103), channel_id=1, source_target_pairs={{0,1},{1,0},{2,3},{3,2},{4,5},{5,4},{6,7},{7,6},{8,9},{9,8},{10,11... | collective-permute-start | bytes 1572872 | tf_op jit(solution)/shard_map/ppermute | solution.py:363
  287.1 4.3 copy-start.46
  287.1 5.4 copy-start.45
  292.4 4.4 copy-start.56
  292.4 4.4 copy-start.58
  292.4 4.4 copy-start.60
  292.5 155.6 %reduce-scatter.17.cloned.1.call-start = ((), (), s32[]{:S(2)}) async-start(), calls=%async_computation.13 | async-start | bytes 2621440 | tf_op jit(solution)/shard_map/reduce_scatter | solution.py:478
  299.8 148.2 %reduce-scatter.15.cloned.1.call-start = ((), (), s32[]{:S(2)}) async-start(), calls=%async_computation.12 | async-start | bytes 2621440 | tf_op jit(solution)/shard_map/reduce_scatter | solution.py:478
  306.1 151.2 %reduce-scatter.19.cloned.1.call-start = ((), (), s32[]{:S(2)}) async-start(), calls=%async_computation.14 | async-start | bytes 2621440 | tf_op jit(solution)/shard_map/reduce_scatter | solution.py:478
  308.2 295.2 %reduce-scatter.21.cloned.1.call-start = ((), (), s32[]{:S(2)}) async-start(), calls=%async_computation.15 | async-start | bytes 10485760 | tf_op jit(solution)/shard_map/reduce_scatter | solution.py:485
  329.9 421.1 %reduce-scatter.23.cloned.1.call-start = ((), (), s32[]{:S(2)}) async-start(), calls=%async_computation.16 | async-start | bytes 10485760 | tf_op jit(solution)/shard_map/reduce_scatter | solution.py:485
  345.9 7.2 copy-start.13
  345.9 8.2 copy-start.12
  345.9 8.4 copy-start.53
  346.8 21.6 %all-to-all-start = ((bf16[4,256,256]{2,1,0:T(8,128)(2,1)}), bf16[4,256,256]{2,1,0:T(8,128)(2,1)S(1)}, u32[]{:S(2)}, u32[]{:S(2)}) async-start(bf16[4,256,256]{2,1,0:T(8,128)(2,1)} %pad_maximum_fusion.5), calls=%async_computation | async-start | bytes 1048576 | tf_op jit(solution)/shard_map/all_to_all | solution.py:422
  350.3 427.5 %reduce-scatter.13.cloned.1.call-start = ((), (), s32[]{:S(2)}) async-start(), calls=%async_computation.11 | async-start | bytes 327680 | tf_op jit(solution)/shard_map/reduce_scatter | solution.py:477
  354.3 9.5 copy-start.28
  369.1 8.3 copy-start.29
  400.7 8.6 copy-start.5
  411.5 24.3 %copy-start.4 = (bf16[1024,3,256]{0,2,1:T(8,128)(2,1)S(1)}, bf16[1024,3,256]{0,2,1:T(8,128)(2,1)}, u32[]{:S(2)}) copy-start(bf16[1024,3,256]{0,2,1:T(8,128)(2,1)} %copy-done.3) | copy-start | bytes 4718596
  411.5 407.8 %reduce-scatter.9.cloned.1.call-start = ((), (), s32[]{:S(2)}) async-start(), calls=%async_computation.9 | async-start | bytes 2621440 | tf_op jit(solution)/shard_map/reduce_scatter | solution.py:472
  440.2 514.4 %all-reduce.5.cloned.1.call-start = ((), (), s32[]{:S(2)}) async-start(), calls=%async_computation.17 | async-start | bytes 16777216 | tf_op jit(solution)/shard_map/psum | solution.py:488
  440.2 5.4 copy-start.43
  440.2 5.4 copy-start.47
  750.9 68.4 %copy-start.50 = (f32[1024]{0:T(1024)S(1)}, f32[1024]{0:T(1024)}, u32[]{:S(2)}) copy-start(f32[1024]{0:T(1024)} %param.23) | copy-start | bytes 12292
  751.0 70.0 %copy-start.51 = (f32[1024]{0:T(1024)S(1)}, f32[1024]{0:T(1024)}, u32[]{:S(2)}) copy-start(f32[1024]{0:T(1024)} %get-tuple-element.64) | copy-start | bytes 12292
  751.0 70.0 %copy-start.52 = (f32[1024]{0:T(1024)S(1)}, f32[1024]{0:T(1024)}, u32[]{:S(2)}) copy-start(f32[1024]{0:T(1024)} %get-tuple-element.43) | copy-start | bytes 12292
  751.0 70.0 %copy-start.64 = (f32[1024]{0:T(1024)S(1)}, f32[1024]{0:T(1024)}, u32[]{:S(2)}) copy-start(f32[1024]{0:T(1024)} %get-tuple-element.44) | copy-start | bytes 12292
  751.0 70.0 %copy-start.65 = (f32[1024]{0:T(1024)S(1)}, f32[1024]{0:T(1024)}, u32[]{:S(2)}) copy-start(f32[1024]{0:T(1024)} %get-tuple-element.47) | copy-start | bytes 12292
  954.6 4.2 copy-start.6
  958.8 4.4 copy-start.17
  961.3 5.1 copy-start.21
  (38 other events, 78.6 us)
Sparse Core Ops, SparseCore 0:
  292.5 20.7 reduce-scatter.10
  316.2 46.9 reduce-scatter.16
  366.2 45.0 reduce-scatter.14
  414.0 43.1 reduce-scatter.18
  459.6 143.7 reduce-scatter.20
  605.7 145.1 reduce-scatter.22
  753.9 20.4 reduce-scatter.12
  777.2 42.0 reduce-scatter.8
  825.4 129.1 all-reduce.4

commit v2 on v1

--- a/solution.py
+++ b/solution.py
@@ -169,10 +169,10 @@
                 self.first(index).wait_send()
                 for hop in hops:
                     self.second(index, hop).wait_send()
-        if number == 0:
-            self.local().start()
-        if number == 3:
-            self.local().wait()
+
+    def finish(self):
+        self.step(3)
+        self.local().wait()
 
 
 def attend_block(projected, mixed, totals, i, hp, size, local):
@@ -206,23 +206,83 @@
     totals[hp, i] = largest + jnp.log(total)
 
 
-def attention_kernel(
+def share_of(local, dp):
+    share = dp
+    while (local // share) % 16:
+        share //= 2
+    return share
+
+
+def norm_back(grad, normal, inverse, gain):
+    scaled = grad * gain
+    return inverse * (
+        scaled
+        - jnp.mean(scaled, axis=-1, keepdims=True)
+        - normal * jnp.mean(scaled * normal, axis=-1, keepdims=True)
+    )
+
+
+def add_rows(ref, index, value):
+    ref[pl.ds(index, 1), :] += jnp.sum(value, axis=0, keepdims=True)
+
+
+def in_chunks(total, chunk, step):
+    def run(i, _):
+        step(pl.ds(pl.multiple_of(i * chunk, chunk), chunk))
+        return 0
+
+    lax.fori_loop(0, total // chunk, run, 0)
+
+
+def cross_pair(query, text_proj, length, idx, local):
+    per = local // PAIR
+    g, hp = idx // per, lax.rem(idx, per)
+    near = pl.multiple_of(hp * PAIR, PAIR)
+    column = pl.multiple_of(idx * PAIR, PAIR)
+    stacked = stack_heads(query[:, pl.ds(column, PAIR)], SCALE)
+    key = text_proj[g, :, pl.ds(near, PAIR)]
+    value = text_proj[g, :, pl.ds(near + local, PAIR)]
+    scores = nt(key, stacked)
+    slot = lax.broadcasted_iota(jnp.int32, scores.shape, 0)
+    return g, near, column, stacked, key, value, jnp.where(slot < length, scores, MASKED)
+
+
+ROWS_AT_ONCE = 32
+
+
+def layer_kernel(
     sizes,
-    image, gain, shift, qkv, text, kv, so, cq, co, mi, mo,
-    projected, normed, mixed, totals, mixed_rows, text_proj, so_full, cq_full, co_full, mi_full, mo_full,
-    text_own, small_send, small_recv, small_own, wide_send, wide_recv, wide_own,
-    mix_send, mix_recv, mix_own, text_send, text_recv, text_local,
+    image, gain1, shift1, qkv, text, kv, length, gain2, shift2, gain3, shift3, in_bias, out_bias,
+    so, cq, co, mi, mo, grad_out,
+    projected, normed, mixed, totals, out, residual, dmixed, dtext, so_grad, cq_grad, co_grad, mi_grad, mo_grad,
+    bias_grad, vectors,
+    mixed_rows, text_proj, so_full, cq_full, co_full, mi_full, mo_full, bias_full,
+    grad_pair, mixed_all, first, second, work, grad2, out_part,
+    n2, query, cross, cross_totals, dquery, n3_pair, active, dhidden,
+    dn3_send, dn3_recv, out_send, out_recv, r2, dcross, r1, dmixed_send, dtext_send, dtext_recv,
+    text_own, so_keep, co_keep, small_send, small_recv, small_own, wide_send, wide_recv, wide_own,
+    mix_send, mix_recv, mix_own, text_send, text_recv, bias_send, bias_recv, load_sem,
+    pair_send, pair_recv, dmix_send, dmix_recv, dtext_ssem, dtext_rsem, store_sem,
 ):
     place = Place(sizes)
     n, share = place.n, place.share
-    rows = image.shape[0]
+    rows, width = image.shape
     size = rows // n
-    local = so.shape[0]
+    local, hidden = so.shape[0], mi.shape[1]
+    half = n // 2
     offsets = list(range(1, n))
+    parity = lax.rem(place.m, 2)
+    mate = (place.d, place.m + 1 - 2 * parity)
+    mine = place.m // 2
     greet = [place.peer(k) for k in offsets]
     greet += [place.chip_peer(k)[0] for k in range(1, share // 2)]
     greet.append(place.partner)
     barrier(greet)
+
+    def remote(src, dst, send, recv, device):
+        return pltpu.make_async_remote_copy(
+            src_ref=src, dst_ref=dst, send_sem=send, recv_sem=recv, device_id=device, device_id_type=MESH
+        )
 
     small = [
         Gather(place, own, full, offsets, lambda s: s, (small_send.at[t], small_recv.at[t], small_own.at[t]))
@@ -232,47 +292,58 @@
         Gather(place, own, full, list(range(2, n, 2)), lambda s: s // 2, (wide_send.at[t], wide_recv.at[t], wide_own.at[t]))
         for t, (own, full) in enumerate(((mi, mi_full), (mo, mo_full)))
     ]
+    for item in small:
+        item.step(0)
     for item in small + wide:
-        item.step(0)
+        item.local().start()
+
+    def block_of(index):
+        return pl.ds(pl.multiple_of(index * size, size), size)
+
+    own_rows = block_of(place.m)
+    loads = [
+        pltpu.make_async_copy(grad_out.at[own_rows, :], grad_pair.at[0], load_sem.at[0]),
+        pltpu.make_async_copy(grad_out.at[block_of(mate[1]), :], grad_pair.at[1], load_sem.at[1]),
+    ]
+    for load in loads:
+        load.start()
+    bias_full[mine] = in_bias[...]
+
+    def bias_copy(k):
+        return remote(in_bias, bias_full.at[mine], bias_send.at[k], bias_recv.at[k], place.peer(2 * k))
+
+    for k in range(1, half):
+        bias_copy(k).start()
 
     def project(i, _):
-        block = pl.ds(pl.multiple_of(i * size, size), size)
-        normal, _ = norm_parts(image[block, :].astype(F32))
-        row = (normal * gain[...] + shift[...]).astype(BF)
-        normed[block, :] = row
-        projected[block, :] = nn(row, qkv[...]).astype(BF)
+        block = block_of(i)
+
+        def norm(chunk):
+            at = pl.ds(pl.multiple_of(i * size + chunk.start, ROWS_AT_ONCE), ROWS_AT_ONCE)
+            normal, _ = norm_parts(image[at, :].astype(F32))
+            normed[at, :] = (normal * gain1[...] + shift1[...]).astype(BF)
+
+        in_chunks(size, ROWS_AT_ONCE, norm)
+        projected[block, :] = nn(normed[block, :], qkv[...]).astype(BF)
         return 0
 
     lax.fori_loop(0, n, project, 0)
     text_own[...] = nn(text[...], kv[...]).astype(BF)
+    text_proj[place.m] = text_own[...]
 
     def text_copy(k):
-        return pltpu.make_async_remote_copy(
-            src_ref=text_own, dst_ref=text_proj.at[place.m],
-            send_sem=text_send.at[k], recv_sem=text_recv.at[k],
-            device_id=place.peer(k), device_id_type=MESH,
-        )
+        return remote(text_own, text_proj.at[place.m], text_send.at[k], text_recv.at[k], place.peer(k))
 
     for k in offsets:
         text_copy(k).start()
-    text_keep = pltpu.make_async_copy(text_own, text_proj.at[place.m], text_local)
-    text_keep.start()
 
     def mix_copy(i):
         gap = lax.rem(i - place.m + n, n)
-        block = pl.ds(pl.multiple_of(i * size, size), size)
-        return pltpu.make_async_remote_copy(
-            src_ref=mixed.at[block, :], dst_ref=mixed_rows.at[place.m],
-            send_sem=mix_send.at[gap], recv_sem=mix_recv.at[gap],
-            device_id=(place.d, i), device_id_type=MESH,
-        )
-
-    def mix_keep():
-        block = pl.ds(pl.multiple_of(place.m * size, size), size)
-        return pltpu.make_async_copy(mixed.at[block, :], mixed_rows.at[place.m], mix_own)
-
+        return remote(mixed.at[block_of(i), :], mixed_rows.at[place.m], mix_send.at[gap], mix_recv.at[gap], (place.d, i))
+
+    mix_keep = pltpu.make_async_copy(mixed.at[own_rows, :], mixed_rows.at[place.m], mix_own)
     plan = [(small[0], 1), (small[1], 1), (small[0], 2), (small[2], 1), (small[1], 2), (small[2], 2)]
-    plan += [(wide[0], 1), (wide[1], 1), (wide[0], 2), (wide[1], 2)]
+    plan += [(wide[0], 0), (wide[1], 0)]
     each = -(-len(plan) // n)
     for i in range(n):
         lax.fori_loop(0, local // PAIR, lambda hp, _: (attend_block(projected, mixed, totals, i, hp, size, local), 0)[1], 0)
@@ -283,29 +354,238 @@
 
         @pl.when(place.m == i)
         def _():
-            mix_keep().start()
+            mix_keep.start()
 
         for item, number in plan[i * each : (i + 1) * each]:
             item.step(number)
 
-    for item in small + wide:
-        item.step(3)
+    for k in offsets:
+        mix_copy(place.along(k)).wait()
+    mix_keep.wait()
+    small[0].finish()
+    for g in range(n):
+        mixed_all[:, g * local : (g + 1) * local] = mixed_rows[g]
+    first[...] = nn(mixed_all[...], so_full[...].reshape(n * local, width))
+
+    def first_norm(chunk):
+        at = pl.ds(pl.multiple_of(place.m * size + chunk.start, ROWS_AT_ONCE), ROWS_AT_ONCE)
+        value = image[at, :].astype(F32) + first[chunk, :]
+        first[chunk, :] = value
+        n2[chunk, :] = (norm_parts(value)[0] * gain2[...] + shift2[...]).astype(BF)
+
+    in_chunks(size, ROWS_AT_ONCE, first_norm)
+    small[1].finish()
+    for g in range(n):
+        query[:, g * local : (g + 1) * local] = nn(n2[...], cq_full[g]).astype(BF)
     for k in offsets:
         text_copy(k).wait()
-    text_keep.wait()
+    for item in wide:
+        item.step(1)
+    limit = length[0, 0]
+    all_pairs = n * local // PAIR
+
+    def cross_forward(idx, _):
+        g, near, column, stacked, key, value, scores = cross_pair(query, text_proj, limit, idx, local)
+        largest = jnp.max(scores, axis=0, keepdims=True)
+        powers = jnp.exp(scores - largest)
+        total = jnp.sum(powers, axis=0, keepdims=True)
+        cross_totals[idx] = largest + jnp.log(total)
+        cross[:, pl.ds(column, PAIR)] = fold_heads(tn(value, (powers / total).astype(BF))).astype(BF)
+        return 0
+
+    lax.fori_loop(0, all_pairs, cross_forward, 0)
+    small[2].finish()
+    second[...] = nn(cross[...], co_full[...].reshape(n * local, width))
+
+    def second_norm(chunk):
+        value = first[chunk, :] + second[chunk, :]
+        second[chunk, :] = value
+        n3_pair[0, chunk, :] = (norm_parts(value)[0] * gain3[...] + shift3[...]).astype(BF)
+
+    in_chunks(size, ROWS_AT_ONCE, second_norm)
+
+    n3_copy = remote(n3_pair.at[0], n3_pair.at[1], pair_send.at[0], pair_recv.at[0], mate)
+    n3_copy.start()
+    for load in loads:
+        load.wait()
+    for k in range(1, half):
+        bias_copy(k).wait()
+    for item in wide:
+        item.local().wait()
+    step = min(256, hidden)
+
+    def feed(p, slot):
+        grads = grad_pair[p]
+
+        def chunk(c, _):
+            columns = pl.ds(pl.multiple_of(c * step, step), step)
+            value = nn(n3_pair[p], mi_full[slot, :, columns]) + bias_full[slot, :, columns]
+            inner = 0.5 * (1.0 + lax.erf(value * (0.5**0.5)))
+            slope = inner + value * jnp.exp(-0.5 * value * value) * ((2.0 * jnp.pi) ** -0.5)
+            active[slot, p, :, columns] = (value * inner).astype(BF)
+            dhidden[slot, p, :, columns] = (nt(grads, mo_full[slot, columns, :]) * slope).astype(BF)
+            return 0
+
+        lax.fori_loop(0, hidden // step, chunk, 0)
+
+    def sum_slots(term):
+        total = term(0)
+        for slot in range(1, half):
+            total += term(slot)
+        return total
+
+    feed(0, mine)
+    n3_copy.wait()
+    feed(1, mine)
+    for item in wide:
+        item.step(2)
+    for item in wide:
+        item.step(3)
+    others = [lax.rem(mine + k, half) for k in range(1, half)]
+    for slot in others:
+        feed(1, slot)
+    dn3_send[...] = sum_slots(lambda slot: nt(dhidden[slot, 1], mi_full[slot])).astype(BF)
+    dn3_copy = remote(dn3_send, dn3_recv, pair_send.at[1], pair_recv.at[1], mate)
+    dn3_copy.start()
+    out_send[...] = sum_slots(lambda slot: nn(active[slot, 1], mo_full[slot])).astype(BF)
+    out_copy = remote(out_send, out_recv, pair_send.at[2], pair_recv.at[2], mate)
+    out_copy.start()
+    for slot in others:
+        feed(0, slot)
+    work[...] = sum_slots(lambda slot: nt(dhidden[slot, 0], mi_full[slot]))
+    out_part[...] = sum_slots(lambda slot: nn(active[slot, 0], mo_full[slot]))
+    dn3_copy.wait()
+
+    vectors[...] = jnp.zeros_like(vectors)
+
+    def third_back(chunk):
+        grad = work[chunk, :] + dn3_recv[chunk, :].astype(F32)
+        normal, inverse = norm_parts(second[chunk, :])
+        above = grad_pair[0, chunk, :].astype(F32)
+        add_rows(vectors, 4, grad * normal)
+        add_rows(vectors, 5, grad)
+        add_rows(vectors, 6, above)
+        value = above + norm_back(grad, normal, inverse, gain3[...])
+        work[chunk, :] = value
+        r2[chunk, :] = value.astype(BF)
+
+    in_chunks(size, ROWS_AT_ONCE, third_back)
+    dcross[...] = nt(r2[...], co_full[...].reshape(n * local, width)).astype(BF)
+
+    def cross_back(idx, _):
+        g, near, column, stacked, key, value, scores = cross_pair(query, text_proj, limit, idx, local)
+        weights = jnp.exp(scores - cross_totals[idx])
+        above = stack_heads(dcross[:, pl.ds(column, PAIR)])
+        dweights = nt(value, above)
+        dscores = (weights * (dweights - jnp.sum(weights * dweights, axis=0, keepdims=True))).astype(BF)
+        dquery[:, pl.ds(column, PAIR)] = (fold_heads(tn(key, dscores)) * SCALE).astype(BF)
+        dtext_send[g, :, pl.ds(near, PAIR)] = nn(dscores, stacked).astype(BF)
+        dtext_send[g, :, pl.ds(near + local, PAIR)] = nn(weights.astype(BF), above).astype(BF)
+        return 0
+
+    lax.fori_loop(0, all_pairs, cross_back, 0)
+
+    def dtext_copy(k):
+        return remote(dtext_send.at[place.along(k)], dtext_recv.at[place.m], dtext_ssem.at[k], dtext_rsem.at[k], place.peer(k))
+
     for k in offsets:
-        mix_copy(place.along(k)).wait()
-    mix_keep().wait()
-
-
-def share_of(local, dp):
-    share = dp
-    while (local // share) % 16:
-        share //= 2
-    return share
-
-
-def attention(sizes, image, gain, shift, qkv, text, kv, so, cq, co, mi, mo):
+        dtext_copy(k).start()
+    def both(term):
+        total = term(0)
+        for g in range(1, n):
+            total += term(g)
+        return total
+
+    grad2[...] = both(lambda g: nt(dquery[:, g * local : (g + 1) * local], cq_full[g]))
+
+    def second_back(chunk):
+        grad = grad2[chunk, :]
+        normal, inverse = norm_parts(first[chunk, :])
+        add_rows(vectors, 2, grad * normal)
+        add_rows(vectors, 3, grad)
+        value = work[chunk, :] + norm_back(grad, normal, inverse, gain2[...])
+        residual[chunk, :] = value
+        r1[chunk, :] = value.astype(BF)
+
+    in_chunks(size, ROWS_AT_ONCE, second_back)
+
+    def dmix_copy(k):
+        return remote(dmixed_send.at[k], dmixed.at[own_rows, :], dmix_send.at[k], dmix_recv.at[k], place.peer(k))
+
+    for k in offsets:
+        dmixed_send[k] = nt(r1[...], so_full[place.along(k)]).astype(BF)
+        dmix_copy(k).start()
+    dmixed[own_rows, :] = nt(r1[...], so_full[place.m]).astype(BF)
+
+    tile = min(256, width)
+
+    def wide_grads(slot):
+        inner = n3_pair.shape[0] * size
+        hidden_grad = dhidden[slot].reshape(inner, hidden)
+        grads = grad_pair[...].reshape(inner, width)
+        bias_grad[slot] = jnp.sum(hidden_grad.astype(F32), axis=0, keepdims=True)
+
+        def into(t, _):
+            at = pl.ds(pl.multiple_of(t * tile, tile), tile)
+            mi_full[slot, at, :] = tn(n3_pair[:, :, at].reshape(inner, tile), hidden_grad).astype(BF)
+            return 0
+
+        lax.fori_loop(0, width // tile, into, 0)
+
+        def back(t, _):
+            at = pl.ds(pl.multiple_of(t * step, step), step)
+            mo_full[slot, at, :] = tn(active[slot, :, :, at].reshape(inner, step), grads).astype(BF)
+            return 0
+
+        lax.fori_loop(0, hidden // step, back, 0)
+
+    for slot in range(half):
+        wide_grads(slot)
+    stores = [
+        pltpu.make_async_copy(mi_full, mi_grad, store_sem.at[0]),
+        pltpu.make_async_copy(mo_full, mo_grad, store_sem.at[1]),
+    ]
+    for store in stores:
+        store.start()
+
+    def small_grad(left, right, keep, target, index):
+        def into(t, _):
+            at = pl.ds(pl.multiple_of(t * tile, tile), tile)
+            turned = left[:, at]
+            for g in range(n):
+                keep[g, at, :] = tn(turned, right[:, g * local : (g + 1) * local]).astype(BF)
+            return 0
+
+        lax.fori_loop(0, width // tile, into, 0)
+        copy = pltpu.make_async_copy(keep, target, store_sem.at[index])
+        copy.start()
+        stores.append(copy)
+
+    small_grad(n2, dquery, cq_full, cq_grad, 2)
+    small_grad(r1, mixed_all, so_keep, so_grad, 3)
+    small_grad(r2, cross, co_keep, co_grad, 4)
+
+    out_copy.wait()
+
+    def finish_out(chunk):
+        value = second[chunk, :] + out_part[chunk, :] + out_recv[chunk, :].astype(F32) + out_bias[...]
+        out[chunk, :] = value.astype(BF)
+
+    in_chunks(size, ROWS_AT_ONCE, finish_out)
+    for k in offsets:
+        dtext_copy(k).wait()
+    total = dtext_send[place.m].astype(F32)
+    for k in offsets:
+        total += dtext_recv[place.along(k)].astype(F32)
+    dtext[...] = total.astype(BF)
+    for k in offsets:
+        dmix_copy(k).wait()
+    for store in stores:
+        store.wait()
+
+
+def layer(sizes, image, gain1, shift1, qkv, text, kv, length, gain2, shift2, gain3, shift3, in_bias, out_bias,
+          so, cq, co, mi, mo, grad_out):
     n, share = sizes["mp"], sizes["share"]
     rows, width = image.shape
     slots = text.shape[0]
@@ -313,119 +593,51 @@
     size = rows // n
     pairs = local // PAIR
     hops = share // 2 + 1
-    half = max(n // 2, 1)
+    half = n // 2
     vmem, hbm = pl.BlockSpec(memory_space=pltpu.VMEM), pl.BlockSpec(memory_space=pl.ANY)
-    dma = pltpu.SemaphoreType.DMA
+    dma, mem = pltpu.SemaphoreType.DMA, pltpu.VMEM
+    shape = jax.ShapeDtypeStruct
+    few = max(half - 1, 1)
     return pl.pallas_call(
-        partial(attention_kernel, sizes),
+        partial(layer_kernel, sizes),
         out_shape=[
-            jax.ShapeDtypeStruct((rows, 3 * local), BF),
-            jax.ShapeDtypeStruct((rows, width), BF),
-            jax.ShapeDtypeStruct((rows, local), BF),
-            jax.ShapeDtypeStruct((pairs, n, 1, 2 * size), F32),
-            jax.ShapeDtypeStruct((n, size, local), BF),
-            jax.ShapeDtypeStruct((n, slots, 2 * local), BF),
-            jax.ShapeDtypeStruct((n, local, width), BF),
-            jax.ShapeDtypeStruct((n, width, local), BF),
-            jax.ShapeDtypeStruct((n, local, width), BF),
-            jax.ShapeDtypeStruct((half, width, hidden), BF),
-            jax.ShapeDtypeStruct((half, hidden, width), BF),
+            shape((rows, 3 * local), BF), shape((rows, width), BF), shape((rows, local), BF),
+            shape((pairs, n, 1, 2 * size), F32), shape((size, width), BF), shape((size, width), F32),
+            shape((rows, local), BF), shape((slots, 2 * local), BF),
+            shape((n, width, local), BF), shape((n, width, local), BF), shape((n, width, local), BF),
+            shape((half, width, hidden), BF), shape((half, hidden, width), BF),
+            shape((half, 1, hidden), F32), shape((8, width), F32),
         ],
-        in_specs=[vmem] * 6 + [hbm] * 5,
-        out_specs=[vmem] * 4 + [hbm] * 7,
+        in_specs=[vmem] * 6 + [pl.BlockSpec(memory_space=pltpu.SMEM)] + [vmem] * 6 + [hbm] * 6,
+        out_specs=[vmem] * 8 + [hbm] * 5 + [vmem] * 2,
         scratch_shapes=[
-            pltpu.VMEM((slots, 2 * local), BF),
+            mem((n, size, local), BF), mem((n, slots, 2 * local), BF),
+            mem((n, local, width), BF), mem((n, width, local), BF), mem((n, local, width), BF),
+            mem((half, width, hidden), BF), mem((half, hidden, width), BF), mem((half, 1, hidden), F32),
+            mem((2, size, width), BF), mem((size, n * local), BF),
+            mem((size, width), F32), mem((size, width), F32), mem((size, width), F32), mem((size, width), F32),
+            mem((size, width), F32),
+            mem((size, width), BF), mem((size, n * local), BF), mem((size, n * local), BF),
+            mem((n * pairs, 1, 2 * size), F32), mem((size, n * local), BF),
+            mem((2, size, width), BF), mem((half, 2, size, hidden), BF), mem((half, 2, size, hidden), BF),
+            mem((size, width), BF), mem((size, width), BF), mem((size, width), BF), mem((size, width), BF),
+            mem((size, width), BF), mem((size, n * local), BF), mem((size, width), BF),
+            mem((n, size, local), BF), mem((n, slots, 2 * local), BF), mem((n, slots, 2 * local), BF),
+            mem((slots, 2 * local), BF), mem((n, width, local), BF), mem((n, width, local), BF),
             dma((3, n - 1, hops)), dma((3, n - 1, hops)), dma((3,)),
-            dma((2, half - 1, hops)), dma((2, half - 1, hops)), dma((2,)),
+            dma((2, few, hops)), dma((2, few, hops)), dma((2,)),
             dma((n,)), dma((n,)), dma(()),
-            dma((n,)), dma((n,)), dma(()),
+            dma((n,)), dma((n,)), dma((half,)), dma((half,)), dma((2,)),
+            dma((3,)), dma((3,)), dma((n,)), dma((n,)), dma((n,)), dma((n,)), dma((5,)),
         ],
         compiler_params=pltpu.CompilerParams(collective_id=1, has_side_effects=True, vmem_limit_bytes=VMEM_LIMIT),
-        cost_estimate=pl.CostEstimate(flops=6 << 30, bytes_accessed=32 << 20, transcendentals=4 << 20),
-    )(image, gain, shift, qkv, text, kv, so, cq, co, mi, mo)
-
-
-def row_norm(value, gain, shift):
-    normal, inverse = norm_parts(value)
-    return (normal * gain + shift).astype(BF), normal, inverse
-
-
-def norm_back(grad, normal, inverse, gain):
-    scaled = grad * gain
-    return inverse * (
-        scaled
-        - jnp.mean(scaled, axis=-1, keepdims=True)
-        - normal * jnp.mean(scaled * normal, axis=-1, keepdims=True)
-    )
-
-
-def swap_pairs(value, n):
-    return lax.ppermute(value, "mp", [(s, s + 1 - 2 * (s % 2)) for s in range(n)])
+        cost_estimate=pl.CostEstimate(flops=22 << 30, bytes_accessed=48 << 20, transcendentals=8 << 20),
+    )(image, gain1, shift1, qkv, text, kv, length, gain2, shift2, gain3, shift3, in_bias, out_bias,
+      so, cq, co, mi, mo, grad_out)
 
 
 def split_heads(value):
     return value.reshape(value.shape[0], -1, HEAD_DIM)
-
-
-def middle(n, image_rows, grad_rows, grad_pair, length, mixed_rows, text_proj, so, cq, co, mi, mo, in_bias, out_bias,
-           gain2, shift2, gain3, shift3):
-    size, width = image_rows.shape
-    local = so.shape[1]
-    mixed = jnp.concatenate(list(mixed_rows), axis=1)
-    so, co = so.reshape(-1, width), co.reshape(-1, width)
-    cq = jnp.concatenate(list(cq), axis=1)
-    first = image_rows + nn(mixed, so)
-    n2, normal2, inverse2 = row_norm(first, gain2, shift2)
-    query = split_heads(nn(n2, cq).astype(BF))
-    keys = split_heads(jnp.concatenate([t[:, :local] for t in text_proj], axis=1))
-    values = split_heads(jnp.concatenate([t[:, local:] for t in text_proj], axis=1))
-    scores = jnp.einsum("qhe,khe->hqk", query, keys, preferred_element_type=F32) * SCALE
-    scores = jnp.where(lax.iota(jnp.int32, keys.shape[0]) < length, scores, MASKED)
-    weights = jax.nn.softmax(scores, axis=-1)
-    rounded = weights.astype(BF)
-    cross = jnp.einsum("hqk,khe->qhe", rounded, values, preferred_element_type=F32).astype(BF).reshape(size, -1)
-    second = first + nn(cross, co)
-    n3, normal3, inverse3 = row_norm(second, gain3, shift3)
-    n3_pair = jnp.stack([n3, swap_pairs(n3, n)])
-    hidden = jnp.einsum("psd,kdf->pksf", n3_pair, mi, preferred_element_type=F32) + in_bias[None, :, None, :]
-    active, gelu_back = jax.vjp(partial(jax.nn.gelu, approximate=False), hidden)
-    active = active.astype(BF)
-    out_part = jnp.einsum("pksf,kfd->psd", active, mo, preferred_element_type=F32)
-    out = second + out_part[0] + swap_pairs(out_part[1].astype(BF), n).astype(F32) + out_bias
-    grad_active = jnp.einsum("psd,kfd->pksf", grad_pair, mo, preferred_element_type=F32)
-    grad_hidden = gelu_back(grad_active)[0].astype(BF)
-    mo_grad = jnp.einsum("pksf,psd->kfd", active, grad_pair, preferred_element_type=F32)
-    mi_grad = jnp.einsum("psd,pksf->kdf", n3_pair, grad_hidden, preferred_element_type=F32)
-    in_bias_grad = jnp.sum(grad_hidden.astype(F32), axis=(0, 2))
-    dn3_part = jnp.einsum("pksf,kdf->psd", grad_hidden, mi, preferred_element_type=F32)
-    dn3 = dn3_part[0] + swap_pairs(dn3_part[1].astype(BF), n).astype(F32)
-    residual = grad_rows + norm_back(dn3, normal3, inverse3, gain3)
-    r2 = residual.astype(BF)
-    co_grad = tn(cross, r2)
-    dcross = split_heads(nt(r2, co).astype(BF))
-    dweights = jnp.einsum("qhe,khe->hqk", dcross, values, preferred_element_type=F32)
-    dscores = weights * (dweights - jnp.sum(weights * dweights, axis=-1, keepdims=True)) * SCALE
-    dscores = dscores.astype(BF)
-    dquery = jnp.einsum("hqk,khe->qhe", dscores, keys, preferred_element_type=F32).astype(BF).reshape(size, -1)
-    dkeys = jnp.einsum("hqk,qhe->khe", dscores, query, preferred_element_type=F32).reshape(keys.shape[0], -1)
-    dvalues = jnp.einsum("hqk,qhe->khe", rounded, dcross, preferred_element_type=F32).reshape(keys.shape[0], -1)
-    dtext = jnp.concatenate(
-        [t[:, g * local : (g + 1) * local] for g in range(n) for t in (dkeys, dvalues)], axis=1
-    ).astype(BF)
-    cq_grad = tn(n2, dquery)
-    dn2 = nt(dquery, cq)
-    residual = residual + norm_back(dn2, normal2, inverse2, gain2)
-    r1 = residual.astype(BF)
-    so_grad = tn(mixed, r1)
-    dmixed = nt(r1, so).astype(BF)
-    dmixed = jnp.stack([dmixed[:, g * local : (g + 1) * local] for g in range(n)])
-    dmixed = lax.all_to_all(dmixed, "mp", 0, 0)
-    vectors = [
-        jnp.sum(dn2 * normal2, axis=0), jnp.sum(dn2, axis=0), jnp.sum(dn3 * normal3, axis=0), jnp.sum(dn3, axis=0),
-        jnp.sum(grad_rows, axis=0),
-    ]
-    return (out.astype(BF), residual, dmixed.reshape(-1, local), dtext, so_grad, cq_grad, co_grad, mi_grad, mo_grad,
-            in_bias_grad, vectors)
 
 
 def attention_back(n, projected, totals, dmixed, local):
@@ -458,30 +670,28 @@
     sizes = dict(sizes, share=share_of(local, sizes["dp"]))
     qkv, kv = qkv.reshape(width, 3 * local), kv.reshape(width, 2 * local)
     own = lambda value: lax.dynamic_slice_in_dim(value, m * size, size, 0)
-    (projected, normed1, mixed, totals, mixed_rows, text_proj, so_full, cq_full, co_full, mi_full, mo_full) = attention(
-        sizes, image, gain1[None], shift1[None], qkv, text, kv, so, cq, co, mi, mo)
-    bias_full = lax.all_gather(in_bias, "mp").reshape(n // 2, 2, -1)[:, m % 2]
+    row = lambda value: value[None]
     image_rows = own(image).astype(F32)
-    grad_rows = own(grad_out)
-    other = lax.dynamic_slice_in_dim(grad_out, (m + 1 - 2 * (m % 2)) * size, size, 0)
-    (out, residual, dmixed, dtext, so_grad, cq_grad, co_grad, mi_grad, mo_grad, in_bias_grad, vectors) = middle(
-        n, image_rows, grad_rows.astype(F32), jnp.stack([grad_rows, other]), lengths[0], mixed_rows, text_proj,
-        so_full, cq_full, co_full, mi_full, mo_full, bias_full, out_bias, gain2, shift2, gain3, shift3)
+    (projected, normed1, mixed, totals, out, residual, dmixed, dtext, so_grad, cq_grad, co_grad, mi_grad, mo_grad,
+     in_bias_grad, vectors) = layer(
+        sizes, image, row(gain1), row(shift1), qkv, text, kv, row(lengths), row(gain2), row(shift2), row(gain3),
+        row(shift3), row(in_bias), row(out_bias), so, cq, co, mi, mo, grad_out)
+    in_bias_grad = in_bias_grad[:, 0]
+    vectors = [vectors[t] for t in range(2, 7)]
     dprojected = attention_back(n, projected, totals, dmixed, local)
     qkv_grad = tn(normed1, dprojected)
     dn1 = lax.psum_scatter(nt(dprojected, qkv).astype(BF), "mp", scatter_dimension=0, tiled=True).astype(F32)
     normal1, inverse1 = norm_parts(image_rows)
     image_grad = residual + norm_back(dn1, normal1, inverse1, gain1)
-    dtext = lax.psum_scatter(dtext, "mp", scatter_dimension=1, tiled=True)
     kv_grad = tn(text, dtext)
     text_grad = lax.psum_scatter(nt(dtext, kv).astype(BF), "mp", scatter_dimension=0, tiled=True).astype(F32)
-    scatter = lambda value, dim: lax.psum_scatter(value.astype(BF), "mp", scatter_dimension=dim, tiled=True)
-    so_grad, co_grad, cq_grad = scatter(so_grad, 0), scatter(co_grad, 0), scatter(cq_grad, 1)
+    scatter = lambda value: lax.psum_scatter(value, "mp", scatter_dimension=0, tiled=True)[0]
+    so_grad, co_grad, cq_grad = scatter(so_grad).T, scatter(co_grad).T, scatter(cq_grad)
 
     def own_shard(value):
         total = jnp.zeros((n,) + value.shape[1:], F32)
         for j in range(n // 2):
-            total = lax.dynamic_update_index_in_dim(total, value[j], 2 * j + m % 2, 0)
+            total = lax.dynamic_update_index_in_dim(total, value[j].astype(F32), 2 * j + m % 2, 0)
         return lax.psum_scatter(total.astype(BF), "mp", scatter_dimension=0, tiled=True)[0]
 
     mi_grad, mo_grad, in_bias_grad = own_shard(mi_grad), own_shard(mo_grad), own_shard(in_bias_grad)

time: 983 us -> 826 us (0.84)
  matrix products: 149 us -> 72 us
  Pallas kernels: 187 us -> 153 us
  blocking collectives: 85.5 us -> 64.9 us
  local copies, waits for them, and re-layouts: 49.7 us -> 36.6 us
    dot_general x14 -> x0, matrix products: 50.5 us -> none  [the longest x1 13.1 us: middle(): jnp.einsum('psd,kdf->pksf', n3_pair, mi, preferred_element_type=F32)]
    pallas_call x1, Pallas kernels: 187 us -> 153 us  [layer(): pl.pallas_call(partial(layer_kernel, sizes), out_shape=[shape((rows, 3 *...]
    all_gather x1 -> x0, blocking collectives: 20.9 us -> none  [body(): bias_full = lax.all_gather(in_bias, 'mp').reshape(n // 2, 2, -1)[:, m % 2]]
    reduce_scatter x4 -> x3, waiting for transfers between devices: 9.22 us -> 28.4 us  [body(): lax.psum_scatter(value, 'mp', scatter_dimension=0, tiled=True)[0]]
    ppermute x3 -> x0, waiting for transfers between devices: 16 us -> none  [swap_pairs(): lax.ppermute(value, 'mp', [(s, s + 1 - 2 * (s % 2)) for s in range(n)])]
  transfers between devices with their start and end apart: 13 -> 8, of which waited for: 8 -> 5; matrix products, arithmetic and copies ran while one was open for 16% -> 13% of each run, Pallas kernels for 0% -> 0%
where the time goes in v2:
time: 826 us; the launch traced here: 821 us
  waiting for transfers between devices  454 us (55%)
  Pallas kernels  153 us (19%)
  matrix products  72 us (9%)
  blocking collectives  64.9 us (8%)
  local copies, waits for them, and re-layouts  36.6 us (4%)
  other arithmetic  24.9 us (3%)
  between operations  15.5 us (2%)
    reduce_scatter x2, waiting for transfers between devices, own_shard(): lax.psum_scatter(total.astype(BF), 'mp', scatter_dimension=0, tiled=True)[0]  294 us
    pallas_call x1, Pallas kernels, layer(): pl.pallas_call(partial(layer_kernel, sizes), out_shape=[shape((rows, 3 *...  153 us
    psum x1, waiting for transfers between devices, body(): total = lambda value: lax.psum(value.astype(BF), 'dp').astype(F32)  90.6 us
    psum x1, blocking collectives, body(): g1, s1, g2, s2, g3, s3, ob = lax.psum(tuple(vectors), ('dp', 'mp'))  41.1 us
    reduce_scatter x1, waiting for transfers between devices, body(): lax.psum_scatter(nt(dprojected, qkv).astype(BF), 'mp', scatter_dimension=...  39.7 us
    reduce_scatter x3, waiting for transfers between devices, body(): lax.psum_scatter(value, 'mp', scatter_dimension=0, tiled=True)[0]  28.4 us
    dot_general x1, matrix products, attention_back(): dk = jnp.einsum('hqk,qhe->khe', dscores, q, preferred_element_type=F32)  23 us
    dot_general x1, matrix products, attention_back(): dq = jnp.einsum('hqk,khe->qhe', dscores, k, preferred_element_type=F32)  22.9 us
  transfers between devices with their start and end apart: 8, of which 5 were waited for; matrix products, arithmetic and copies ran while one was open for 13% of the time, Pallas kernels for 0%

profile of v2, /device:TPU:0, one launch (start us, length us, event | category | flops | bytes accessed | tf_op | source)
XLA Modules:
  0.0 821.4 jit_solution(4780906840025528386)
XLA Ops:
  7.9 2.4 copy.83
  10.3 1.7 copy.66
  12.0 1.6 copy.67.qkv
  13.6 152.6 %shard_map.322 = (bf16[1024,768]{1,0:T(8,128)(2,1)}, bf16[1024,1024]{1,0:T(8,128)(2,1)}, bf16[1024,256]{1,0:T(8,128)(2,1)}, f32[2,4,1,512]{3,2,1,0:T(1,128)}, bf...) custom-call(bf16[1024,1024]{1,0:T(8,128)(2,1)} %bitcast.114, ...), custom_call_target="tpu_custom_call" | custom-call | flops 23622320128 | bytes 50331648 | tf_op jit(solution)/shard_map/pallas_call | solution.py:601
  166.3 0.7 reduce-scatter.14.cloned.1.call-update
  167.1 0.7 reduce-scatter.16.cloned.1.call-update
  168.0 4.5 broadcast.43.clone.1
  172.5 1.5 convert_dynamic-update-slice_fusion.1
  174.0 1.5 convert_dynamic-update-slice_fusion
  175.6 4.3 broadcast.43.clone
  179.9 1.5 convert_dynamic-update-slice_fusion.3
  181.4 1.5 convert_dynamic-update-slice_fusion.2
  182.9 1.2 copy-done.3
  184.1 1.2 convolution_convert_fusion.3
  185.4 1.3 iota_compare_fusion
  186.9 2.4 fusion.42
  189.4 1.2 copy.72
  190.6 2.0 copy.69
  192.7 1.0 copy.68
  193.7 5.9 subtract_exponential_fusion
  199.6 2.7 fusion.15
  202.2 3.0 copy-done
  205.3 8.1 fusion.44
  213.4 22.9 %fusion.18 = bf16[4,64,1024]{2,1,0:T(8,128)(2,1)S(1)} fusion(bf16[1024,4,64]{0,2,1:T(8,128)(2,1)} %bitcast.128, f32[4,1024,1024]{1,2,0:T(8,128)} %copy-done, f32[4,1024,1024]{1,2,0:T(8,128)} %fusion.44), kind=kOutput, calls=%fused_computation.27 | convolution fusion | flops 558109696 | bytes 34603008 | tf_op jit(solution)/shard_map/hqk,khe->qhe/dot_general | solution.py:656
  236.3 23.0 %fusion.21 = bf16[4,64,1024]{2,1,0:T(8,128)(2,1)} fusion(bf16[1024,4,64]{0,2,1:T(8,128)(2,1)S(1)} %bitcast.126, f32[4,1024,1024]{1,2,0:T(8,128)} %copy-done, f32[4,1024,1024]{1,2,0:T(8,128)} %fusion.44), kind=kOutput, calls=%fused_computation.28 | convolution fusion | flops 558109696 | bytes 34603008 | tf_op jit(solution)/shard_map/hqk,qhe->khe/dot_general | solution.py:657
  259.4 4.2 convolution_convert_fusion
  264.4 2.0 copy.77
  266.4 3.6 convolution_convert_fusion.1
  270.0 1.6 copy.76
  271.6 28.4 %reduce-scatter.16.cloned.1.call-done = bf16[1,1024,256]{2,1,0:T(8,128)(2,1)} async-done(((bf16[4,1024,256]{2,1,0:T(8,128)(2,1)}), bf16[1,1024,256]{2,1,0:T(8,128)(2,1)}) %reduce-scatter.16.cloned.1.call-update) | async-done | bytes 524304 | tf_op jit(solution)/shard_map/reduce_scatter | solution.py:688
  300.0 146.2 %reduce-scatter.20.cloned.1.call-done = bf16[1,1024,1024]{2,1,0:T(8,128)(2,1)} async-done(((bf16[4,1024,1024]{2,1,0:T(8,128)(2,1)}), bf16[1,1024,1024]{2,1,0:T(8,128)(2,1)}) %reduce-scatter.20.cloned.1.call-update) | async-done | bytes 2097168 | tf_op jit(solution)/shard_map/reduce_scatter | solution.py:695
  446.1 147.6 %reduce-scatter.18.cloned.1.call-done = bf16[1,1024,1024]{2,1,0:T(8,128)(2,1)} async-done(((bf16[4,1024,1024]{2,1,0:T(8,128)(2,1)}), bf16[1,1024,1024]{2,1,0:T(8,128)(2,1)}) %reduce-scatter.18.cloned.1.call-update) | async-done | bytes 2097168 | tf_op jit(solution)/shard_map/reduce_scatter | solution.py:695
  595.1 11.4 %all-reduce = bf16[4,1024]{1,0:T(4,128)(2,1)S(1)} all-reduce(bf16[4,1024]{1,0:T(4,128)(2,1)S(1)} %dynamic_update_slice.23), channel_id=8, replica_groups=mesh['dp'=8,'mp'=4] {'mp'}, use_global_device_ids=true, to_apply=%region_25.26.clone | all-reduce | flops 4096 | bytes 16384
  607.2 12.4 %psum.117 = bf16[1024]{0:T(1024)(128)(2,1)S(1)} all-reduce(bf16[1024]{0:T(1024)(128)(2,1)S(1)} %dynamic-slice_reduce_fusion), channel_id=1, replica_groups=mesh['dp'=8,'mp'=4] {'dp'}, use_global_device_ids=true, to_apply=%region_26.27 | all-reduce | flops 1024 | bytes 4096 | tf_op jit(solution)/shard_map/psum | solution.py:698
  620.7 1.5 bitcast_convert_fusion
  622.2 39.7 %reduce-scatter.8.cloned.1.call-done = bf16[256,1024]{1,0:T(8,128)(2,1)} async-done(((bf16[1024,1024]{1,0:T(8,128)(2,1)}), bf16[256,1024]{1,0:T(8,128)(2,1)}) %reduce-scatter.8.cloned.1.call-update) | async-done | bytes 524304 | tf_op jit(solution)/shard_map/reduce_scatter | solution.py:683
  661.9 1.6 fusion.34
  663.5 41.1 %all-reduce.1 = (f32[1024]{0:T(1024)}, f32[1024]{0:T(1024)}, f32[1024]{0:T(1024)}, f32[1024]{0:T(1024)}, f32[1024]{0:T(1024)}, /*index=5*/f32[1024]{0:T(1024)}, f32[1024]{0:T(1024)}) all-reduce(f32[1024]{0:T(1024)S(1)} %get-tuple-element.100, f32[1024]{0:T(1024)S(1)} %get-tuple-element.103, ...), channel_id=1, replica_groups=mesh['dp'=8,'mp'=4] {'dp','mp'}, use_global_device_ids=true, to_apply=%region_8.9 | all-reduce | flops 7168 | bytes 57344 | tf_op jit(solution)/shard_map/psum | solution.py:700
  704.6 2.4 fusion.31
  707.0 90.6 %all-reduce.5.cloned.1.call-done = (bf16[256,1024]{0,1:T(8,128)(2,1)}, bf16[256,1024]{0,1:T(8,128)(2,1)}, bf16[1024,3,256]{2,0,1:T(8,128)(2,1)}, bf16[1024,256]{...) async-done(((bf16[256,1024]{0,1:T(8,128)(2,1)}, bf16[256,1024]{0,1:T(8,128)(2,1)}, ...) | async-done | bytes 8388624 | tf_op jit(solution)/shard_map/psum | solution.py:698
  797.7 2.4 copy.78
  800.0 2.2 copy.79
  802.3 2.1 convert_element_type.86
  804.3 2.0 reshape.121
  806.4 1.9 reshape.119
  808.3 2.5 convert_element_type.93
  810.8 2.5 convert_element_type.99
  813.3 0.8 copy.100
  (72 shorter events, 4.7 us)
Async XLA Ops:
  7.2 264.4 %reduce-scatter.12.cloned.1.call-start = ((), (), s32[]{:S(2)}) async-start(), calls=%async_computation.9 | async-start | bytes 2621440 | tf_op jit(solution)/shard_map/reduce_scatter | solution.py:688
  166.3 105.3 %reduce-scatter.14.cloned.1.call-start = ((), (), s32[]{:S(2)}) async-start(), calls=%async_computation.10 | async-start | bytes 2621440 | tf_op jit(solution)/shard_map/reduce_scatter | solution.py:688
  167.0 133.0 %reduce-scatter.16.cloned.1.call-start = ((), (), s32[]{:S(2)}) async-start(), calls=%async_computation.11 | async-start | bytes 2621440 | tf_op jit(solution)/shard_map/reduce_scatter | solution.py:688
  167.8 278.4 %reduce-scatter.20.cloned.1.call-start = ((), (), s32[]{:S(2)}) async-start(), calls=%async_computation.13 | async-start | bytes 10485760 | tf_op jit(solution)/shard_map/reduce_scatter | solution.py:695
  168.0 4.5 copy-start.2
  175.6 418.1 %reduce-scatter.18.cloned.1.call-start = ((), (), s32[]{:S(2)}) async-start(), calls=%async_computation.12 | async-start | bytes 10485760 | tf_op jit(solution)/shard_map/reduce_scatter | solution.py:695
  175.6 4.3 copy-start.1
  182.9 1.2 copy-start.3
  182.9 1.2 copy-start.13
  182.9 3.8 copy-start.16
  182.9 3.8 copy-start.11
  182.9 437.8 %reduce-scatter.10.cloned.1.call-start = ((), (), s32[]{:S(2)}) async-start(), calls=%async_computation.8 | async-start | bytes 327680 | tf_op jit(solution)/shard_map/reduce_scatter | solution.py:687
  185.3 476.6 %reduce-scatter.8.cloned.1.call-start = ((), (), s32[]{:S(2)}) async-start(), calls=%async_computation.7 | async-start | bytes 2621440 | tf_op jit(solution)/shard_map/reduce_scatter | solution.py:683
  199.6 5.7 copy-start
  213.4 22.9 %copy-start.12 = (bf16[1024,256]{0,1:T(8,128)(2,1)S(1)}, bf16[1024,256]{0,1:T(8,128)(2,1)}, u32[]{:S(2)}) copy-start(bf16[1024,256]{0,1:T(8,128)(2,1)} %copy.69) | copy-start | bytes 1572868
  259.4 4.6 copy-start.14
  263.6 534.0 %all-reduce.5.cloned.1.call-start = ((), (), s32[]{:S(2)}) async-start(), calls=%async_computation.14 | async-start | bytes 16777216 | tf_op jit(solution)/shard_map/psum | solution.py:698
  593.7 0.7 copy-start.19
  593.7 1.2 copy-start.18
  593.7 26.5 %copy-start.6 = (bf16[1,1024,1024]{2,1,0:T(8,128)(2,1)S(1)}, bf16[1,1024,1024]{2,1,0:T(8,128)(2,1)}, u32[]{:S(2)}) copy-start(bf16[1,1024,1024]{2,1,0:T(8,128)(2,1)} %param.19) | copy-start | bytes 6291460
  593.7 26.9 %copy-start.17 = (f32[8,1024]{1,0:T(8,128)S(1)}, f32[8,1024]{1,0:T(8,128)}, u32[]{:S(2)}) copy-start(f32[8,1024]{1,0:T(8,128)} %get-tuple-element.40) | copy-start | bytes 98308
  593.7 68.2 %copy-start.15 = (f32[1024]{0:T(1024)S(1)}, f32[1024]{0:T(1024)}, u32[]{:S(2)}) copy-start(f32[1024]{0:T(1024)} %param.23) | copy-start | bytes 12292
  593.7 110.9 %copy-start.9 = (f32[256,1024]{1,0:T(8,128)S(1)}, f32[256,1024]{1,0:T(8,128)}, u32[]{:S(2)}) copy-start(f32[256,1024]{1,0:T(8,128)} %get-tuple-element.33) | copy-start | bytes 3145732
  797.7 6.7 copy-start.8
  797.7 8.7 %copy-start.7 = (bf16[1024,3,256]{2,0,1:T(8,128)(2,1)S(1)}, bf16[1024,3,256]{2,0,1:T(8,128)(2,1)}, u32[]{:S(2)}) copy-start(bf16[1024,3,256]{2,0,1:T(8,128)(2,1)} %get-tuple-element.113) | copy-start | bytes 4718596
  804.3 4.0 copy-start.5
  808.3 2.5 copy-start.4
  810.8 2.5 copy-start.10
Sparse Core Ops, SparseCore 0:
  166.4 42.3 reduce-scatter.11
  211.2 43.1 reduce-scatter.13
  256.7 43.1 reduce-scatter.15
  302.3 143.7 reduce-scatter.19
  448.5 145.1 reduce-scatter.17
  596.5 20.3 reduce-scatter.9
  619.7 42.1 reduce-scatter.7
  668.5 129.0 all-reduce.4

commit v3 on v2

--- a/solution.py
+++ b/solution.py
@@ -636,27 +636,428 @@
       so, cq, co, mi, mo, grad_out)
 
 
-def split_heads(value):
-    return value.reshape(value.shape[0], -1, HEAD_DIM)
-
-
-def attention_back(n, projected, totals, dmixed, local):
-    rows = projected.shape[0]
-    heads = local // HEAD_DIM
-    q, k, v = (split_heads(projected[:, t * local : (t + 1) * local]) for t in range(3))
+class Reduce:
+    def __init__(self, place, ref, recv, pieces, other, final, whole, rule, sems):
+        self.place, self.ref, self.recv, self.pieces, self.other, self.final, self.whole = (
+            place, ref, recv, pieces, other, final, whole)
+        self.slots, self.rows, self.columns = ref.shape
+        self.half = self.rows // 2
+        self.part = self.half // 2
+        self.bits = (place.dp // 2).bit_length() - 1
+        self.count = self.part >> self.bits
+        self.rule, (self.send, self.recv_sem, self.keep) = rule, sems
+        self.chip = place.d // 2
+        if rule == "all":
+            self.hops = [(k, place.along(k)) for k in range(1, place.n)]
+            self.slot = place.m
+        elif rule == "parity":
+            half = place.n // 2
+            self.hops = [(2 * k, lax.rem(place.m // 2 + k, half)) for k in range(1, half)]
+            self.slot = place.m // 2
+        else:
+            self.hops, self.slot = [], 0
+
+    def bit(self, p, k):
+        b = k if p == 0 else self.bits - 1 - k
+        value = lax.rem(self.chip // (1 << b), 2)
+        chip = self.chip + (1 - 2 * value) * (1 << b)
+        return value, (2 * chip + self.place.core, self.place.m)
+
+    def region(self, p, k):
+        start = self.place.core * self.half + p * self.part
+        for t in range(k):
+            start = start + self.bit(p, t)[0] * (self.part >> (t + 1))
+        return start
+
+    def span(self, start, count):
+        return pl.ds(pl.multiple_of(start, self.count), count)
+
+    def copy(self, src, dst, index, device):
+        return pltpu.make_async_remote_copy(
+            src_ref=src, dst_ref=dst, send_sem=self.send.at[index], recv_sem=self.recv_sem.at[index],
+            device_id=device, device_id_type=MESH,
+        )
+
+    def core_copy(self):
+        away = self.span((1 - self.place.core) * self.half, self.half)
+        return self.copy(self.ref.at[:, away, :], self.recv.at[:, pl.ds(0, self.half), :], 0, self.place.partner)
+
+    def offset(self, p, k):
+        return self.half + p * (self.part - self.count) + sum(self.part >> (t + 1) for t in range(k))
+
+    def chip_copy(self, p, k):
+        value, device = self.bit(p, k)
+        count = self.part >> (k + 1)
+        away = self.span(self.region(p, k) + (1 - value) * count, count)
+        return self.copy(
+            self.ref.at[:, away, :], self.recv.at[:, pl.ds(self.offset(p, k), count), :], 1 + p * self.bits + k, device)
+
+    def far_copy(self, index):
+        hop, slot = self.hops[index]
+        return self.copy(self.pieces.at[slot], self.other.at[self.slot], 1 + 4 * self.bits + index, self.place.peer(hop))
+
+    def spread_copy(self, p, k):
+        _, device = self.bit(p, k)
+        count = self.part >> (k + 1)
+        rows = self.span(self.region(p, k + 1), count)
+        block = self.whole.at[rows, :]
+        src = self.final.at[pl.ds(p * self.count, self.count), :] if k == self.bits - 1 else block
+        return self.copy(src, block, 1 + 2 * self.bits + p * self.bits + k, device)
+
+    def keep_copy(self, p):
+        rows = self.span(self.region(p, self.bits), self.count)
+        return pltpu.make_async_copy(self.final.at[pl.ds(p * self.count, self.count), :], self.whole.at[rows, :], self.keep.at[p])
+
+    def core_spread(self):
+        block = self.whole.at[self.span(self.place.core * self.half, self.half), :]
+        return self.copy(block, block, 1 + 4 * self.bits + self.place.n, self.place.partner)
+
+    def add(self, start, offset, count, target, target_start):
+        chunk = min(32, count)
+
+        def run(t, _):
+            at = t * chunk
+            for s in range(self.slots):
+                mine = self.ref[s, self.span_of(start + at, chunk), :].astype(F32)
+                theirs = self.recv[s, self.span_of(offset + at, chunk), :].astype(F32)
+                target[s, self.span_of(target_start + at, chunk), :] = (mine + theirs).astype(BF)
+            return 0
+
+        lax.fori_loop(0, count // chunk, run, 0)
+
+    def span_of(self, start, chunk):
+        return pl.ds(pl.multiple_of(start, 16), chunk)
+
+    def phases(self):
+        bits = self.bits
+
+        def begin():
+            self.core_copy().start()
+
+        def core_sum():
+            self.core_copy().wait()
+            self.add(self.place.core * self.half, 0, self.half, self.ref, self.place.core * self.half)
+            for p in range(2):
+                self.chip_copy(p, 0).start()
+
+        def chip_sum(k):
+            for p in range(2):
+                self.chip_copy(p, k).wait()
+                last = k == bits - 1
+                start = self.region(p, k + 1)
+                self.add(start, self.offset(p, k), self.part >> (k + 1), self.pieces if last else self.ref,
+                         p * self.count if last else start)
+                if not last:
+                    self.chip_copy(p, k + 1).start()
+            if k == bits - 1:
+                for index in range(len(self.hops)):
+                    self.far_copy(index).start()
+
+        def far_sum():
+            total = self.pieces[self.slot].astype(F32)
+            for index, (hop, _) in enumerate(self.hops):
+                self.far_copy(index).wait()
+                source = self.place.along(self.place.n - hop)
+                total += self.other[source if self.rule == "all" else source // 2].astype(F32)
+            self.final[...] = total.astype(BF)
+            for p in range(2):
+                self.keep_copy(p).start()
+                self.spread_copy(p, bits - 1).start()
+            for p in range(2):
+                self.keep_copy(p).wait()
+
+        def spread(k):
+            for p in range(2):
+                self.spread_copy(p, k).wait()
+                if k > 0:
+                    self.spread_copy(p, k - 1).start()
+            if k == 0:
+                self.core_spread().start()
+
+        def end():
+            self.core_spread().wait()
+
+        steps = [begin, core_sum] + [partial(chip_sum, k) for k in range(bits)] + [far_sum]
+        return steps + [partial(spread, k) for k in reversed(range(bits))] + [end]
+
+
+def back_kernel(
+    sizes,
+    gain1, qkv, kv, text, residual, projected, normed, mixed, totals, dmixed, dtext, early,
+    image, mi_grad, mo_grad, so_grad, cq_grad, co_grad,
+    image_grad, text_grad, early_out, late_out, mi_out, mo_out, small_out, joint_out,
+    image_rows, stacked, above, delta, dquery, dprojected, dn1_send, dn1_recv, dn1_own,
+    mi_ref, mi_recv, mi_pieces, mi_other, mi_final, mo_ref, mo_recv, mo_pieces, mo_other, mo_final,
+    small_ref, small_recv, small_pieces, small_other, small_final, joint_ref, joint_recv, joint_pieces, joint_final,
+    early_dp, early_mp, early_own, late, late_dp, late_mp, late_own, text_send, text_recv,
+    reduce_send, reduce_recv, reduce_keep, load_sem, dn1_ssem, dn1_rsem, text_ssem, text_rsem,
+    vec_ssem, vec_rsem, vec_zsend, vec_zrecv,
+):
+    place = Place(sizes)
+    n, dp = place.n, place.dp
+    rows, width = normed.shape
+    local = mixed.shape[1]
     size = rows // n
-    log_total = totals.reshape(heads // 2, n, 2, size).transpose(0, 2, 1, 3).reshape(heads, rows)
-    scores = jnp.einsum("qhe,khe->hqk", q, k, preferred_element_type=F32) * SCALE
-    keep = lax.iota(jnp.int32, rows)[:, None] >= lax.iota(jnp.int32, rows)[None, :]
-    weights = jnp.exp(jnp.where(keep, scores, MASKED) - log_total[:, :, None])
-    do = split_heads(dmixed)
-    dweights = jnp.einsum("qhe,khe->hqk", do, v, preferred_element_type=F32)
-    dscores = weights * (dweights - jnp.sum(weights * dweights, axis=-1, keepdims=True)) * SCALE
-    dscores = dscores.astype(BF)
-    dq = jnp.einsum("hqk,khe->qhe", dscores, k, preferred_element_type=F32)
-    dk = jnp.einsum("hqk,qhe->khe", dscores, q, preferred_element_type=F32)
-    dv = jnp.einsum("hqk,qhe->khe", weights.astype(BF), do, preferred_element_type=F32)
-    return jnp.concatenate([t.reshape(rows, local) for t in (dq, dk, dv)], axis=1).astype(BF)
+    pairs = local // PAIR
+    offsets = list(range(1, n))
+    everyone = [lax.rem(place.d + k, dp) for k in range(1, dp)]
+    barrier([place.peer(k) for k in offsets] + [(device, place.m) for device in everyone])
+
+    def remote(src, dst, send, recv, device):
+        return pltpu.make_async_remote_copy(
+            src_ref=src, dst_ref=dst, send_sem=send, recv_sem=recv, device_id=device, device_id_type=MESH
+        )
+
+    def block_of(index):
+        return pl.ds(pl.multiple_of(index * size, size), size)
+
+    loads = [
+        pltpu.make_async_copy(src, dst, load_sem.at[t])
+        for t, (src, dst) in enumerate((
+            (mi_grad, mi_ref), (mo_grad, mo_ref), (so_grad, small_ref.at[:, :, 0:local]),
+            (cq_grad, small_ref.at[:, :, local : 2 * local]), (co_grad, small_ref.at[:, :, 2 * local : 3 * local]),
+            (image.at[block_of(place.m), :], image_rows),
+        ))
+    ]
+    for load in loads:
+        load.start()
+
+    def unit(t, ref, recv, pieces, other, final, whole, rule):
+        sems = (reduce_send.at[t], reduce_recv.at[t], reduce_keep.at[t])
+        return Reduce(place, ref, recv, pieces, other, final, whole, rule, sems).phases()
+
+    mi_steps = unit(0, mi_ref, mi_recv, mi_pieces, mi_other, mi_final, mi_out, "parity")
+    mo_steps = unit(1, mo_ref, mo_recv, mo_pieces, mo_other, mo_final, mo_out, "parity")
+    small_steps = unit(2, small_ref, small_recv, small_pieces, small_other, small_final, small_out, "all")
+    joint_steps = unit(3, joint_ref, joint_recv, joint_pieces, None, joint_final, joint_out, "own")
+
+    class Vectors:
+        def __init__(self, value, over_dp, own, over_mp, base):
+            self.value, self.over_dp, self.own, self.over_mp, self.base = value, over_dp, own, over_mp, base
+
+        def first(self, k):
+            return remote(self.value, self.over_dp.at[place.d], vec_ssem.at[self.base, k], vec_rsem.at[self.base, k],
+                          (everyone[k - 1], place.m))
+
+        def second(self, k):
+            return remote(self.own, self.over_mp.at[place.m], vec_zsend.at[self.base, k], vec_zrecv.at[self.base, k],
+                          place.peer(k))
+
+        def begin(self):
+            self.over_dp[place.d] = self.value[...]
+            for k in range(1, dp):
+                self.first(k).start()
+
+        def turn(self):
+            for k in range(1, dp):
+                self.first(k).wait()
+            total = self.over_dp[0]
+            for j in range(1, dp):
+                total += self.over_dp[j]
+            self.own[...] = total
+            self.over_mp[place.m] = total
+            for k in offsets:
+                self.second(k).start()
+
+        def end(self):
+            for k in offsets:
+                self.second(k).wait()
+
+        def total(self):
+            value = self.over_mp[0]
+            for j in range(1, n):
+                value += self.over_mp[j]
+            return value
+
+    early_sum = Vectors(early, early_dp, early_own, early_mp, 0)
+    late_sum = Vectors(late, late_dp, late_own, late_mp, 1)
+    early_sum.begin()
+
+    part = text_grad.shape[0]
+    spread_text = nt(dtext[...], kv[...]).astype(BF)
+    for g in range(n):
+        text_send[g] = spread_text[g * part : (g + 1) * part, :]
+
+    def text_copy(k):
+        return remote(text_send.at[place.along(k)], text_recv.at[place.m], text_ssem.at[k], text_rsem.at[k], place.peer(k))
+
+    for k in offsets:
+        text_copy(k).start()
+    joint_ref[0, :, 3 * local :] = tn(text[...], dtext[...]).astype(BF)
+
+    loads[0].wait()
+    mi_steps[0]()
+    loads[1].wait()
+    mo_steps[0]()
+    for load in loads[2:5]:
+        load.wait()
+    small_steps[0]()
+
+    def prepare(i, _):
+        block = block_of(i)
+        for hp in range(pairs):
+            columns = slice(hp * PAIR, (hp + 1) * PAIR)
+            stacked[hp, i] = stack_heads(projected[block, columns], SCALE)
+            above[hp, i] = stack_heads(dmixed[block, columns])
+            product = (dmixed[block, columns].astype(F32) * mixed[block, columns].astype(F32)).T
+            delta[hp, i] = jnp.concatenate(
+                [jnp.sum(product[:HEAD_DIM], axis=0, keepdims=True), jnp.sum(product[HEAD_DIM:], axis=0, keepdims=True)],
+                axis=1,
+            )
+            dquery[hp, i] = jnp.zeros_like(dquery[hp, i])
+        return 0
+
+    lax.fori_loop(0, n, prepare, 0)
+    plan = [mi_steps[1], mo_steps[1], small_steps[1], mi_steps[2], mo_steps[2], early_sum.turn, small_steps[2], mi_steps[3]]
+    each = -(-len(plan) // (n * pairs))
+
+    def dn1_copy(j):
+        gap = lax.rem(j - place.m + n, n)
+        return remote(dn1_send.at[j], dn1_recv.at[place.m], dn1_ssem.at[gap], dn1_rsem.at[gap], (place.d, j))
+
+    point = 0
+    for j in range(n):
+        keys = slice(j * size, (j + 1) * size)
+        for hp in range(pairs):
+            columns = slice(hp * PAIR, (hp + 1) * PAIR)
+            key = projected[keys, local + hp * PAIR : local + (hp + 1) * PAIR]
+            value = projected[keys, 2 * local + hp * PAIR : 2 * local + (hp + 1) * PAIR]
+
+            def tile(i, carry, diagonal):
+                dkey, dvalue = carry
+                query, over = stacked[hp, i], above[hp, i]
+                scores = nt(key, query)
+                if diagonal:
+                    scores = jnp.where(causal(size, size), scores, MASKED)
+                weights = jnp.exp(scores - totals[hp, i])
+                dscores = (weights * (nt(value, over) - delta[hp, i])).astype(BF)
+                dvalue = dvalue + nn(weights.astype(BF), over)
+                dkey = dkey + nn(dscores, query)
+                turned = tn(key, dscores)
+                dquery[hp, i] += jnp.concatenate([turned[:HEAD_DIM, :size], turned[HEAD_DIM:, size:]], axis=0)
+                return dkey, dvalue
+
+            carry = (jnp.zeros((size, PAIR), F32), jnp.zeros((size, PAIR), F32))
+            carry = tile(j, carry, True)
+            dkey, dvalue = lax.fori_loop(j + 1, n, lambda i, c: tile(i, c, False), carry)
+            dprojected[keys, columns] = (dquery[hp, j].T * SCALE).astype(BF)
+            dprojected[keys, local + hp * PAIR : local + (hp + 1) * PAIR] = dkey.astype(BF)
+            dprojected[keys, 2 * local + hp * PAIR : 2 * local + (hp + 1) * PAIR] = dvalue.astype(BF)
+            for phase in plan[point * each : (point + 1) * each]:
+                phase()
+            point += 1
+        partial_sum = nt(dprojected[keys, :], qkv[...])
+
+        @pl.when(place.m == j)
+        def _():
+            dn1_own[...] = partial_sum
+
+        @pl.when(place.m != j)
+        def _():
+            dn1_send[j] = partial_sum.astype(BF)
+            dn1_copy(j).start()
+
+    tile_rows = min(256, width)
+
+    def qkv_grad(t, _):
+        at = pl.ds(pl.multiple_of(t * tile_rows, tile_rows), tile_rows)
+        joint_ref[0, at, 0 : 3 * local] = tn(normed[:, at], dprojected[...]).astype(BF)
+        return 0
+
+    lax.fori_loop(0, width // tile_rows, qkv_grad, 0)
+    done = 3 + (len(mi_steps) - 8)
+    joint_steps[0]()
+    mo_steps[3]()
+    small_steps[3]()
+    joint_steps[1]()
+    for k in range(4, len(mi_steps) - 1):
+        mi_steps[k]()
+        mo_steps[k]()
+        small_steps[k]()
+        joint_steps[k - 2]()
+
+    for k in offsets:
+        dn1_copy(place.along(k)).wait()
+        dn1_own[...] += dn1_recv[place.along(n - k)].astype(F32)
+    loads[5].wait()
+    late[...] = jnp.zeros_like(late)
+
+    def last_back(chunk):
+        grad = dn1_own[chunk, :]
+        normal, inverse = norm_parts(image_rows[chunk, :].astype(F32))
+        add_rows(late, 0, grad * normal)
+        add_rows(late, 1, grad)
+        image_grad[chunk, :] = residual[chunk, :] + norm_back(grad, normal, inverse, gain1[...])
+
+    in_chunks(size, ROWS_AT_ONCE, last_back)
+    late_sum.begin()
+    for k in range(len(mi_steps) - 3, len(mi_steps) - 1):
+        joint_steps[k]()
+    for k in offsets:
+        text_copy(k).wait()
+    total = text_send[place.m].astype(F32)
+    for k in offsets:
+        total += text_recv[place.along(k)].astype(F32)
+    text_grad[...] = total
+    late_sum.turn()
+    early_sum.end()
+    early_out[...] = early_sum.total()
+    shared = early_out[pl.ds(8 + place.m // 2, 1), :] * 0.0
+    for j in range(n):
+        take = jnp.where(lax.rem(place.m + j, 2) == 0, 1.0, 0.0)
+        shared += early_mp[j, pl.ds(8 + place.m // 2, 1), :] * take
+    early_out[7:8, :] = shared
+    late_sum.end()
+    late_out[...] = late_sum.total()
+    for steps in (mi_steps, mo_steps, small_steps, joint_steps):
+        steps[-1]()
+
+
+def back(sizes, gain1, qkv, kv, text, residual, projected, normed, mixed, totals, dmixed, dtext, early,
+         image, mi_grad, mo_grad, so_grad, cq_grad, co_grad):
+    n, dp = sizes["mp"], sizes["dp"]
+    rows, width = normed.shape
+    slots = text.shape[0]
+    local, hidden = mixed.shape[1], mi_grad.shape[2]
+    size, pairs, half = rows // n, local // PAIR, n // 2
+    bits = (dp // 2).bit_length() - 1
+    vmem, hbm = pl.BlockSpec(memory_space=pltpu.VMEM), pl.BlockSpec(memory_space=pl.ANY)
+    dma, mem = pltpu.SemaphoreType.DMA, pltpu.VMEM
+    shape = jax.ShapeDtypeStruct
+
+    def unit(count, height, columns, rule):
+        piece = 2 * (height // 4 >> bits)
+        scratch = [mem((count, height, columns), BF), mem((count, height - piece, columns), BF), mem((count, piece, columns), BF)]
+        if rule != "own":
+            scratch.append(mem((count, piece, columns), BF))
+        return scratch + [mem((piece, columns), BF)]
+
+    few = early.shape[0]
+    each = 2 + 4 * bits + n
+    return pl.pallas_call(
+        partial(back_kernel, sizes),
+        out_shape=[
+            shape((size, width), F32), shape((slots // n, width), F32), shape((few, width), F32), shape((2, width), F32),
+            shape((width, hidden), BF), shape((hidden, width), BF), shape((width, 3 * local), BF), shape((width, 5 * local), BF),
+        ],
+        in_specs=[vmem] * 12 + [hbm] * 6,
+        out_specs=[vmem] * 4 + [hbm] * 4,
+        scratch_shapes=[
+            mem((size, width), BF), mem((pairs, n, 2 * size, PAIR), BF), mem((pairs, n, 2 * size, PAIR), BF),
+            mem((pairs, n, 1, 2 * size), F32), mem((pairs, n, PAIR, size), F32), mem((rows, 3 * local), BF),
+            mem((n, size, width), BF), mem((n, size, width), BF), mem((size, width), F32),
+            *unit(half, width, hidden, "parity"), *unit(half, hidden, width, "parity"),
+            *unit(n, width, 3 * local, "all"), *unit(1, width, 5 * local, "own"),
+            mem((dp, few, width), F32), mem((n, few, width), F32), mem((few, width), F32),
+            mem((2, width), F32), mem((dp, 2, width), F32), mem((n, 2, width), F32), mem((2, width), F32),
+            mem((n, slots // n, width), BF), mem((n, slots // n, width), BF),
+            dma((4, each)), dma((4, each)), dma((4, 2)), dma((6,)), dma((n,)), dma((n,)), dma((n,)), dma((n,)),
+            dma((2, dp)), dma((2, dp)), dma((2, n)), dma((2, n)),
+        ],
+        compiler_params=pltpu.CompilerParams(collective_id=2, has_side_effects=True, vmem_limit_bytes=60 << 20),
+        cost_estimate=pl.CostEstimate(flops=8 << 30, bytes_accessed=48 << 20, transcendentals=4 << 20),
+    )(gain1, qkv, kv, text, residual, projected, normed, mixed, totals, dmixed, dtext, early,
+      image, mi_grad, mo_grad, so_grad, cq_grad, co_grad)
 
 
 def body(sizes, image, text, grad_out, lengths, gain1, shift1, qkv, so, gain2, shift2, cq, kv, co, gain3, shift3, mi,
@@ -664,44 +1065,27 @@
     n = sizes["mp"]
     image, text, grad_out = image[0], text[0], grad_out[0]
     rows, width = image.shape
-    size = rows // n
     local = so.shape[0]
-    m = lax.axis_index("mp")
     sizes = dict(sizes, share=share_of(local, sizes["dp"]))
     qkv, kv = qkv.reshape(width, 3 * local), kv.reshape(width, 2 * local)
-    own = lambda value: lax.dynamic_slice_in_dim(value, m * size, size, 0)
     row = lambda value: value[None]
-    image_rows = own(image).astype(F32)
     (projected, normed1, mixed, totals, out, residual, dmixed, dtext, so_grad, cq_grad, co_grad, mi_grad, mo_grad,
      in_bias_grad, vectors) = layer(
         sizes, image, row(gain1), row(shift1), qkv, text, kv, row(lengths), row(gain2), row(shift2), row(gain3),
         row(shift3), row(in_bias), row(out_bias), so, cq, co, mi, mo, grad_out)
-    in_bias_grad = in_bias_grad[:, 0]
-    vectors = [vectors[t] for t in range(2, 7)]
-    dprojected = attention_back(n, projected, totals, dmixed, local)
-    qkv_grad = tn(normed1, dprojected)
-    dn1 = lax.psum_scatter(nt(dprojected, qkv).astype(BF), "mp", scatter_dimension=0, tiled=True).astype(F32)
-    normal1, inverse1 = norm_parts(image_rows)
-    image_grad = residual + norm_back(dn1, normal1, inverse1, gain1)
-    kv_grad = tn(text, dtext)
-    text_grad = lax.psum_scatter(nt(dtext, kv).astype(BF), "mp", scatter_dimension=0, tiled=True).astype(F32)
-    scatter = lambda value: lax.psum_scatter(value, "mp", scatter_dimension=0, tiled=True)[0]
-    so_grad, co_grad, cq_grad = scatter(so_grad).T, scatter(co_grad).T, scatter(cq_grad)
-
-    def own_shard(value):
-        total = jnp.zeros((n,) + value.shape[1:], F32)
-        for j in range(n // 2):
-            total = lax.dynamic_update_index_in_dim(total, value[j].astype(F32), 2 * j + m % 2, 0)
-        return lax.psum_scatter(total.astype(BF), "mp", scatter_dimension=0, tiled=True)[0]
-
-    mi_grad, mo_grad, in_bias_grad = own_shard(mi_grad), own_shard(mo_grad), own_shard(in_bias_grad)
-    total = lambda value: lax.psum(value.astype(BF), "dp").astype(F32)
-    vectors = [jnp.sum(dn1 * normal1, axis=0), jnp.sum(dn1, axis=0)] + vectors
-    g1, s1, g2, s2, g3, s3, ob = lax.psum(tuple(vectors), ("dp", "mp"))
+    early = jnp.zeros((8 + -(-n // 2 // 8) * 8, width), F32)
+    early = lax.dynamic_update_slice(early, vectors, (0, 0))
+    early = lax.dynamic_update_slice(early, in_bias_grad[:, 0], (8, 0))
+    image_grad, text_grad, early, late, mi_sum, mo_sum, small_sum, joint_sum = back(
+        sizes, row(gain1), qkv, kv, text, residual, projected, normed1, mixed, totals, dmixed, dtext, early,
+        image, mi_grad, mo_grad, so_grad, cq_grad, co_grad)
+    hidden = mi.shape[1]
+    small = lambda t: small_sum[:, t * local : (t + 1) * local].astype(F32)
     return (
-        out[None], image_grad[None], text_grad[None], g1, s1, total(qkv_grad).reshape(width, 3, local), total(so_grad),
-        g2, s2, total(cq_grad), total(kv_grad).reshape(width, 2, local), total(co_grad), g3, s3, total(mi_grad),
-        total(in_bias_grad), total(mo_grad), ob,
+        out[None], image_grad[None], text_grad[None], late[0], late[1],
+        joint_sum[:, : 3 * local].astype(F32).reshape(width, 3, local), small(0).T, early[2], early[3], small(1),
+        joint_sum[:, 3 * local :].astype(F32).reshape(width, 2, local), small(2).T, early[4], early[5],
+        mi_sum.astype(F32), early[7, :hidden], mo_sum.astype(F32), early[6],
     )
 
 

time: 826 us -> 363 us (0.44)
  waiting for transfers between devices: 454 us -> 0 us
  Pallas kernels: 153 us -> 327 us
  matrix products: 72 us -> 0 us
  blocking collectives: 64.9 us -> 0 us
  other arithmetic: 24.9 us -> 10.7 us
  between operations: 15.5 us -> 1.49 us
  local copies, waits for them, and re-layouts: 36.6 us -> 22.6 us
    reduce_scatter x7 -> x0, waiting for transfers between devices: 362 us -> none  [the longest x2 294 us: own_shard(): lax.psum_scatter(total.astype(BF), 'mp', scatter_dimension=0, tiled=True)[0]]
    pallas_call x0 -> x1, Pallas kernels: none -> 175 us  [back(): pl.pallas_call(partial(back_kernel, sizes), out_shape=[shape((size, width...]
    psum x1 -> x0, waiting for transfers between devices: 90.6 us -> none  [body(): total = lambda value: lax.psum(value.astype(BF), 'dp').astype(F32)]
    dot_general x9 -> x0, matrix products: 72 us -> none  [the longest x1 23 us: attention_back(): dk = jnp.einsum('hqk,qhe->khe', dscores, q, preferred_element_type=F32)]
    psum x2 -> x0, blocking collectives: 53.5 us -> none  [the longest x1 41.1 us: body(): g1, s1, g2, s2, g3, s3, ob = lax.psum(tuple(vectors), ('dp', 'mp'))]
    unnamed x1 -> x0, blocking collectives: 11.4 us -> none
    another operation x2 -> x0, local copies, waits for them, and re-layouts: 8.73 us -> none
  transfers between devices with their start and end apart: 8 -> 0, of which waited for: 5 -> 0; matrix products, arithmetic and copies ran while one was open for 13% -> 0% of each run, Pallas kernels for 0% -> 0%
where the time goes in v3:
time: 363 us; the launch traced here: 362 us
  Pallas kernels  327 us (90%)
  local copies, waits for them, and re-layouts  22.6 us (6%)
  other arithmetic  10.7 us (3%)
    pallas_call x1, Pallas kernels, back(): pl.pallas_call(partial(back_kernel, sizes), out_shape=[shape((size, width...  175 us
    pallas_call x1, Pallas kernels, layer(): pl.pallas_call(partial(layer_kernel, sizes), out_shape=[shape((rows, 3 *...  152 us
    unnamed x22, local copies, waits for them, and re-layouts  13.2 us

profile of v3, /device:TPU:0, one launch (start us, length us, event | category | flops | bytes accessed | tf_op | source)
XLA Modules:
  0.0 362.2 jit_solution(14051342735810446257)
XLA Ops:
  0.7 0.0 copy-start.2
  1.4 2.4 copy.49
  3.9 0.0 copy-done.2
  3.9 0.9 copy.41
  4.7 1.6 copy.42.qkv
  6.3 152.1 %shard_map.322 = (bf16[1024,768]{1,0:T(8,128)(2,1)}, bf16[1024,1024]{1,0:T(8,128)(2,1)}, bf16[1024,256]{1,0:T(8,128)(2,1)}, f32[2,4,1,512]{3,2,1,0:T(1,128)}, bf...) custom-call(bf16[1024,1024]{1,0:T(8,128)(2,1)} %bitcast.51, ...), custom_call_target="tpu_custom_call" | custom-call | flops 23622320128 | bytes 50331648 | tf_op jit(solution)/shard_map/pallas_call | solution.py:601
  158.4 0.8 dynamic_update_slice.6
  159.2 0.7 bitcast_dynamic-update-slice_fusion.early
  159.9 0.0 copy-start.6
  159.9 0.6 copy-done.6
  160.5 175.2 %shard_map.323 = (f32[256,1024]{1,0:T(8,128)}, f32[32,1024]{1,0:T(8,128)}, f32[16,1024]{1,0:T(8,128)}, f32[2,1024]{1,0:T(2,128)}, bf16[1024,1024]{1,0:T(8,128)(2...) custom-call(f32[1,1024]{1,0:T(1,128)} %bitcast.63, ...), custom_call_target="tpu_custom_call" | custom-call | flops 8589934592 | bytes 50331648 | tf_op jit(solution)/shard_map/pallas_call | solution.py:1037
  335.8 1.7 fusion
  337.5 1.5 slice_convert_fusion.1
  339.0 2.4 reshape.63
  341.3 1.6 slice_convert_fusion
  343.0 2.4 copy.44
  345.4 3.5 copy.45
  348.9 2.6 convert_bitcast_fusion
  351.5 1.3 copy.47
  352.8 0.0 copy-start.1
  352.8 1.3 copy.46
  354.1 0.7 copy-done.1
  354.8 0.0 copy-start
  354.8 2.5 convert_element_type.14
  357.2 0.0 copy-done
  357.2 0.0 copy-start.4
  357.3 0.0 copy-start.3
  357.3 2.5 convert_element_type.15
  359.7 0.0 copy-done.4
  359.7 0.0 copy-start.5
  359.7 0.8 copy.56
  360.5 0.0 copy-done.3
  360.5 1.0 copy.57
  361.5 0.0 copy-done.5
  361.5 0.7 copy.58
Async XLA Ops:
  0.7 3.2 copy-start.2
  159.9 0.6 copy-start.6
  352.8 2.0 copy-start.1
  354.8 2.5 copy-start
  357.2 2.5 copy-start.4
  357.3 3.3 copy-start.3
  359.7 1.8 copy-start.5

commit v4 on v3

--- a/solution.py
+++ b/solution.py
@@ -15,7 +15,7 @@
 BF = jnp.bfloat16
 F32 = jnp.float32
 MESH = pl.DeviceIdType.MESH
-VMEM_LIMIT = 56 << 20
+VMEM_LIMIT = 60 << 20
 
 
 def nn(a, b):
@@ -71,6 +71,7 @@
         self.d = lax.axis_index("dp")
         self.m = lax.axis_index("mp")
         self.core = lax.rem(self.d, 2)
+        self.mate = self.m + 1 - 2 * lax.rem(self.m, 2)
         self.partner = (self.d + 1 - 2 * self.core, self.m)
         self.member = lax.rem(self.d, self.share)
         self.chip = self.member // 2
@@ -80,6 +81,9 @@
     def along(self, offset):
         return lax.rem(self.m + offset, self.n)
 
+    def mate_along(self, offset):
+        return lax.rem(self.mate + offset, self.n)
+
     def peer(self, offset):
         return (self.d, self.along(offset))
 
@@ -96,82 +100,86 @@
 
 
 class Gather:
-    def __init__(self, place, own, full, offsets, slot_of, sems):
-        self.place, self.own, self.full, self.offsets, self.slot_of = place, own, full, offsets, slot_of
-        self.rows = own.shape[0]
-        self.count = self.rows // place.share
+    def __init__(self, place, own, full, everyone, slot_of, sems):
+        self.place, self.own, self.full, self.slot_of = place, own, full, slot_of
+        self.count = own.shape[0] // place.share
         self.sems = sems
+        self.even = list(range(2, place.n, 2))
+        self.sources = [place.along(place.n - k) for k in self.even]
+        if everyone:
+            self.sources.append(place.mate)
+            self.sources += [place.mate_along(place.n - k) for k in self.even]
+        self.everyone = everyone
 
     def rows_of(self, slot, piece, pieces=1):
         start = pl.multiple_of(piece * self.count, self.count)
         return self.full.at[slot, pl.ds(start, pieces * self.count), :]
 
+    def copy(self, src, dst, index, hop, device):
+        return pltpu.make_async_remote_copy(
+            src_ref=src, dst_ref=dst, send_sem=self.sems[0].at[index, hop], recv_sem=self.sems[1].at[index, hop],
+            device_id=device, device_id_type=MESH,
+        )
+
     def first(self, index):
-        place, offset = self.place, self.offsets[index]
-        start = pl.multiple_of(place.piece * self.count, self.count)
-        return pltpu.make_async_remote_copy(
-            src_ref=self.own.at[pl.ds(start, self.count), :],
-            dst_ref=self.rows_of(self.slot_of(place.m), place.piece),
-            send_sem=self.sems[0].at[index, 0],
-            recv_sem=self.sems[1].at[index, 0],
-            device_id=place.peer(offset),
-            device_id_type=MESH,
-        )
-
-    def slot(self, index):
-        place = self.place
-        return self.slot_of(place.along(place.n - self.offsets[index]))
+        place, parity = self.place, len(self.even)
+        mine = self.own.at[pl.ds(pl.multiple_of(place.piece * self.count, self.count), self.count), :]
+        slot = self.slot_of(place.m)
+        if index < parity:
+            device = place.peer(self.even[index])
+        else:
+            device = (place.d, place.mate)
+        if index > parity:
+            slot = self.slot_of(self.sources[index - parity - 1])
+            mine = self.rows_of(slot, place.piece)
+        return self.copy(mine, self.rows_of(slot, place.piece), index, 0, device)
 
     def second(self, index, hop):
-        place = self.place
-        device, _ = place.chip_peer(hop)
-        block = self.rows_of(self.slot(index), place.piece)
-        return pltpu.make_async_remote_copy(
-            src_ref=block,
-            dst_ref=block,
-            send_sem=self.sems[0].at[index, hop],
-            recv_sem=self.sems[1].at[index, hop],
-            device_id=device,
-            device_id_type=MESH,
-        )
+        block = self.rows_of(self.slot_of(self.sources[index]), self.place.piece)
+        return self.copy(block, block, index, hop, self.place.chip_peer(hop)[0])
 
     def third(self, index):
-        place = self.place
-        half = place.share // 2
-        block = self.rows_of(self.slot(index), place.core * half, half)
-        return pltpu.make_async_remote_copy(
-            src_ref=block,
-            dst_ref=block,
-            send_sem=self.sems[0].at[index, half],
-            recv_sem=self.sems[1].at[index, half],
-            device_id=place.partner,
-            device_id_type=MESH,
-        )
+        half = self.place.share // 2
+        block = self.rows_of(self.slot_of(self.sources[index]), self.place.core * half, half)
+        return self.copy(block, block, index, half, self.place.partner)
 
     def local(self):
         return pltpu.make_async_copy(self.own, self.full.at[self.slot_of(self.place.m)], self.sems[2])
 
     def step(self, number):
         hops = range(1, self.place.share // 2)
-        for index in range(len(self.offsets)):
-            if number == 0:
-                self.first(index).start()
-            elif number == 1:
+        parity = len(self.even)
+        everything = range(len(self.sources))
+        if number == 0:
+            for index in everything:
+                if index <= parity:
+                    self.first(index).start()
+        elif number == 1:
+            for index in range(parity):
+                self.first(index).wait_recv()
+                if self.everyone:
+                    self.first(parity + 1 + index).start()
+                for hop in hops:
+                    self.second(index, hop).start()
+        elif number == 2:
+            for index in everything[parity:]:
                 self.first(index).wait_recv()
                 for hop in hops:
                     self.second(index, hop).start()
-            elif number == 2:
+        elif number == 3:
+            for index in everything:
                 for hop in hops:
                     self.second(index, hop).wait_recv()
                 self.third(index).start()
-            else:
+        else:
+            for index in everything:
                 self.third(index).wait()
                 self.first(index).wait_send()
                 for hop in hops:
                     self.second(index, hop).wait_send()
 
     def finish(self):
-        self.step(3)
+        self.step(4)
         self.local().wait()
 
 
@@ -213,6 +221,205 @@
     return share
 
 
+def halvings(rows, bits):
+    left = [rows // 4]
+    for _ in range(bits):
+        left.append(left[-1] // 2 if left[-1] % 32 == 0 else left[-1])
+    return left
+
+
+def arrivals(rows, bits):
+    left = halvings(rows, bits)
+    return left[1:]
+
+
+class Rows:
+    def __init__(self, place, rows):
+        self.place = place
+        self.half = rows // 2
+        self.bits = (place.dp // 2).bit_length() - 1
+        self.left = halvings(rows, self.bits)
+        self.count = self.left[-1]
+        self.chip = place.d // 2
+
+    def bit(self, p, k):
+        b = k if p == 0 else self.bits - 1 - k
+        value = lax.rem(self.chip // (1 << b), 2)
+        chip = self.chip + (1 - 2 * value) * (1 << b)
+        return value, (2 * chip + self.place.core, self.place.m)
+
+    def cut(self, k):
+        return self.left[k + 1] < self.left[k]
+
+    def region(self, p, k):
+        start = self.place.core * self.half + p * self.left[0]
+        for t in range(k):
+            if self.cut(t):
+                start = start + self.bit(p, t)[0] * self.left[t + 1]
+        return start
+
+    def span(self, start, count):
+        return pl.ds(pl.multiple_of(start, 16), count)
+
+
+class Reduce:
+    def __init__(self, place, ref, recv, pieces, sems):
+        self.place, self.ref, self.recv, self.pieces = place, ref, recv, pieces
+        self.rows = Rows(place, ref.shape[1])
+        self.send, self.recv_sem = sems
+
+    def copy(self, src, dst, index, device):
+        return pltpu.make_async_remote_copy(
+            src_ref=src, dst_ref=dst, send_sem=self.send.at[index], recv_sem=self.recv_sem.at[index],
+            device_id=device, device_id_type=MESH,
+        )
+
+    def core_copy(self):
+        half = self.rows.half
+        away = self.rows.span((1 - self.place.core) * half, half)
+        return self.copy(self.ref.at[:, away, :], self.recv.at[:, pl.ds(0, half), :], 0, self.place.partner)
+
+    def offset(self, p, k):
+        into = self.rows.left[1:]
+        return self.rows.half + p * sum(into) + sum(into[:k])
+
+    def chip_copy(self, p, k):
+        rows = self.rows
+        value, device = rows.bit(p, k)
+        count = rows.left[k + 1]
+        start = rows.region(p, k)
+        if rows.cut(k):
+            start = start + (1 - value) * count
+        return self.copy(
+            self.ref.at[:, rows.span(start, count), :], self.recv.at[:, pl.ds(self.offset(p, k), count), :],
+            1 + p * rows.bits + k, device)
+
+    def add(self, start, offset, count, target, target_start):
+        chunk = min(32, count)
+        span = self.rows.span
+
+        def run(t, _):
+            at = t * chunk
+            for s in range(self.ref.shape[0]):
+                mine = self.ref[s, span(start + at, chunk), :].astype(F32)
+                theirs = self.recv[s, span(offset + at, chunk), :].astype(F32)
+                target[s, span(target_start + at, chunk), :] = (mine + theirs).astype(BF)
+            return 0
+
+        lax.fori_loop(0, count // chunk, run, 0)
+
+    def phases(self):
+        rows = self.rows
+
+        def begin():
+            self.core_copy().start()
+
+        def core_sum():
+            self.core_copy().wait()
+            self.add(self.place.core * rows.half, 0, rows.half, self.ref, self.place.core * rows.half)
+            for p in range(2):
+                self.chip_copy(p, 0).start()
+
+        def chip_sum(k):
+            last = k == rows.bits - 1
+            for p in range(2):
+                self.chip_copy(p, k).wait()
+                start = rows.region(p, k + 1)
+                self.add(start, self.offset(p, k), rows.left[k + 1], self.pieces if last else self.ref,
+                         p * rows.count if last else start)
+                if not last:
+                    self.chip_copy(p, k + 1).start()
+
+        return [begin, core_sum] + [partial(chip_sum, k) for k in range(rows.bits)]
+
+
+class Spread:
+    def __init__(self, place, rows, pieces, other, final, whole, rule, sems):
+        self.place, self.pieces, self.other, self.final, self.whole = place, pieces, other, final, whole
+        self.rows = Rows(place, rows)
+        self.rule, (self.send, self.recv_sem, self.keep) = rule, sems
+        if rule == "all":
+            self.hops = [(k, place.along(k)) for k in range(1, place.n)]
+            self.slot = place.m
+        elif rule == "parity":
+            half = place.n // 2
+            self.hops = [(2 * k, lax.rem(place.m // 2 + k, half)) for k in range(1, half)]
+            self.slot = place.m // 2
+        else:
+            self.hops, self.slot = [], 0
+
+    def copy(self, src, dst, index, device):
+        return pltpu.make_async_remote_copy(
+            src_ref=src, dst_ref=dst, send_sem=self.send.at[index], recv_sem=self.recv_sem.at[index],
+            device_id=device, device_id_type=MESH,
+        )
+
+    def far_copy(self, index):
+        hop, slot = self.hops[index]
+        return self.copy(self.pieces.at[slot], self.other.at[self.slot], 1 + 2 * self.rows.bits + index, self.place.peer(hop))
+
+    def spread_copy(self, p, k):
+        rows = self.rows
+        count = rows.left[k + 1]
+        block = self.whole.at[rows.span(rows.region(p, k + 1), count), :]
+        first = not any(rows.cut(t) for t in range(k + 1, rows.bits))
+        src = self.final.at[pl.ds(p * rows.count, rows.count), :] if first else block
+        return self.copy(src, block, 1 + p * rows.bits + k, rows.bit(p, k)[1])
+
+    def keep_copy(self, p):
+        rows = self.rows
+        block = self.whole.at[rows.span(rows.region(p, rows.bits), rows.count), :]
+        return pltpu.make_async_copy(self.final.at[pl.ds(p * rows.count, rows.count), :], block, self.keep.at[p])
+
+    def core_spread(self):
+        half = self.rows.half
+        block = self.whole.at[self.rows.span(self.place.core * half, half), :]
+        return self.copy(block, block, 0, self.place.partner)
+
+    def phases(self):
+        rows = self.rows
+        cuts = [k for k in reversed(range(rows.bits)) if rows.cut(k)]
+
+        def far():
+            for index in range(len(self.hops)):
+                self.far_copy(index).start()
+
+        def far_sum():
+            total = self.pieces[self.slot].astype(F32)
+            for index, (hop, _) in enumerate(self.hops):
+                self.far_copy(index).wait()
+                source = self.place.along(self.place.n - hop)
+                total += self.other[source if self.rule == "all" else source // 2].astype(F32)
+            self.final[...] = total.astype(BF)
+            for p in range(2):
+                self.keep_copy(p).start()
+                self.spread_copy(p, cuts[0]).start()
+            for p in range(2):
+                self.keep_copy(p).wait()
+
+        def spread(t):
+            for p in range(2):
+                self.spread_copy(p, cuts[t]).wait()
+                if t + 1 < len(cuts):
+                    self.spread_copy(p, cuts[t + 1]).start()
+            if t + 1 == len(cuts):
+                self.core_spread().start()
+
+        def end():
+            self.core_spread().wait()
+
+        nothing = [lambda: None] * (rows.bits - len(cuts))
+        return [far, far_sum] + [partial(spread, t) for t in range(len(cuts))] + nothing + [end]
+
+
+def recv_space(count, rows, columns, bits):
+    return pltpu.VMEM((count, rows // 2 + 2 * sum(arrivals(rows, bits)), columns), BF)
+
+
+def piece_shape(count, rows, columns, bits):
+    return jax.ShapeDtypeStruct((count, 2 * halvings(rows, bits)[-1], columns), BF)
+
+
 def norm_back(grad, normal, inverse, gain):
     scaled = grad * gain
     return inverse * (
@@ -254,15 +461,15 @@
     sizes,
     image, gain1, shift1, qkv, text, kv, length, gain2, shift2, gain3, shift3, in_bias, out_bias,
     so, cq, co, mi, mo, grad_out,
-    projected, normed, mixed, totals, out, residual, dmixed, dtext, so_grad, cq_grad, co_grad, mi_grad, mo_grad,
+    projected, normed, mixed, totals, out, residual, dmixed, dtext, so_grad, cq_grad, co_grad, mi_pieces, mo_pieces,
     bias_grad, vectors,
     mixed_rows, text_proj, so_full, cq_full, co_full, mi_full, mo_full, bias_full,
     grad_pair, mixed_all, first, second, work, grad2, out_part,
     n2, query, cross, cross_totals, dquery, n3_pair, active, dhidden,
     dn3_send, dn3_recv, out_send, out_recv, r2, dcross, r1, dmixed_send, dtext_send, dtext_recv,
-    text_own, so_keep, co_keep, small_send, small_recv, small_own, wide_send, wide_recv, wide_own,
+    text_own, mi_recv, mo_recv, small_send, small_recv, small_own, wide_send, wide_recv, wide_own,
     mix_send, mix_recv, mix_own, text_send, text_recv, bias_send, bias_recv, load_sem,
-    pair_send, pair_recv, dmix_send, dmix_recv, dtext_ssem, dtext_rsem, store_sem,
+    pair_send, pair_recv, dmix_send, dmix_recv, dtext_ssem, dtext_rsem, store_sem, reduce_send, reduce_recv,
 ):
     place = Place(sizes)
     n, share = place.n, place.share
@@ -271,12 +478,11 @@
     local, hidden = so.shape[0], mi.shape[1]
     half = n // 2
     offsets = list(range(1, n))
-    parity = lax.rem(place.m, 2)
-    mate = (place.d, place.m + 1 - 2 * parity)
+    mate = (place.d, place.mate)
     mine = place.m // 2
-    greet = [place.peer(k) for k in offsets]
-    greet += [place.chip_peer(k)[0] for k in range(1, share // 2)]
-    greet.append(place.partner)
+    chips = place.dp // 2
+    greet = [place.peer(k) for k in offsets] + [place.partner]
+    greet += [(2 * lax.rem(place.d // 2 + k, chips) + place.core, place.m) for k in range(1, chips)]
     barrier(greet)
 
     def remote(src, dst, send, recv, device):
@@ -285,11 +491,11 @@
         )
 
     small = [
-        Gather(place, own, full, offsets, lambda s: s, (small_send.at[t], small_recv.at[t], small_own.at[t]))
+        Gather(place, own, full, True, lambda s: s, (small_send.at[t], small_recv.at[t], small_own.at[t]))
         for t, (own, full) in enumerate(((so, so_full), (cq, cq_full), (co, co_full)))
     ]
     wide = [
-        Gather(place, own, full, list(range(2, n, 2)), lambda s: s // 2, (wide_send.at[t], wide_recv.at[t], wide_own.at[t]))
+        Gather(place, own, full, False, lambda s: s // 2, (wide_send.at[t], wide_recv.at[t], wide_own.at[t]))
         for t, (own, full) in enumerate(((mi, mi_full), (mo, mo_full)))
     ]
     for item in small:
@@ -331,10 +537,16 @@
     text_own[...] = nn(text[...], kv[...]).astype(BF)
     text_proj[place.m] = text_own[...]
 
+    even = list(range(2, n, 2))
+
     def text_copy(k):
-        return remote(text_own, text_proj.at[place.m], text_send.at[k], text_recv.at[k], place.peer(k))
-
-    for k in offsets:
+        return remote(text_own, text_proj.at[place.m], text_send.at[k], text_recv.at[k], place.peer(k) if k else mate)
+
+    def text_pass(k):
+        block = text_proj.at[place.along(n - k)]
+        return remote(block, block, text_send.at[k + 1], text_recv.at[k + 1], mate)
+
+    for k in [0] + even:
         text_copy(k).start()
 
     def mix_copy(i):
@@ -342,9 +554,12 @@
         return remote(mixed.at[block_of(i), :], mixed_rows.at[place.m], mix_send.at[gap], mix_recv.at[gap], (place.d, i))
 
     mix_keep = pltpu.make_async_copy(mixed.at[own_rows, :], mixed_rows.at[place.m], mix_own)
-    plan = [(small[0], 1), (small[1], 1), (small[0], 2), (small[2], 1), (small[1], 2), (small[2], 2)]
-    plan += [(wide[0], 0), (wide[1], 0)]
-    each = -(-len(plan) // n)
+    for item in small:
+        item.step(1)
+    plan = [[] for _ in range(n)]
+    plan[1] = [small[0]]
+    plan[2] = [small[1]]
+    plan[n - 1] += [small[2]]
     for i in range(n):
         lax.fori_loop(0, local // PAIR, lambda hp, _: (attend_block(projected, mixed, totals, i, hp, size, local), 0)[1], 0)
 
@@ -356,13 +571,21 @@
         def _():
             mix_keep.start()
 
-        for item, number in plan[i * each : (i + 1) * each]:
-            item.step(number)
+        for item in plan[i]:
+            item.step(2)
+
+    for item in wide:
+        item.step(0)
+    for k in even:
+        text_copy(k).wait_recv()
+        text_pass(k).start()
+    small[0].step(3)
 
     for k in offsets:
         mix_copy(place.along(k)).wait()
     mix_keep.wait()
     small[0].finish()
+    small[1].step(3)
     for g in range(n):
         mixed_all[:, g * local : (g + 1) * local] = mixed_rows[g]
     first[...] = nn(mixed_all[...], so_full[...].reshape(n * local, width))
@@ -375,10 +598,13 @@
 
     in_chunks(size, ROWS_AT_ONCE, first_norm)
     small[1].finish()
+    small[2].step(3)
     for g in range(n):
         query[:, g * local : (g + 1) * local] = nn(n2[...], cq_full[g]).astype(BF)
-    for k in offsets:
-        text_copy(k).wait()
+    text_copy(0).wait()
+    for k in even:
+        text_copy(k).wait_send()
+        text_pass(k).wait()
     for item in wide:
         item.step(1)
     limit = length[0, 0]
@@ -438,9 +664,9 @@
     n3_copy.wait()
     feed(1, mine)
     for item in wide:
-        item.step(2)
+        item.step(3)
     for item in wide:
-        item.step(3)
+        item.step(4)
     others = [lax.rem(mine + k, half) for k in range(1, half)]
     for slot in others:
         feed(1, slot)
@@ -454,6 +680,35 @@
         feed(0, slot)
     work[...] = sum_slots(lambda slot: nt(dhidden[slot, 0], mi_full[slot]))
     out_part[...] = sum_slots(lambda slot: nn(active[slot, 0], mo_full[slot]))
+    tile = min(256, width)
+
+    def wide_grads(slot):
+        inner = n3_pair.shape[0] * size
+        hidden_grad = dhidden[slot].reshape(inner, hidden)
+        grads = grad_pair[...].reshape(inner, width)
+        bias_grad[slot] = jnp.sum(hidden_grad.astype(F32), axis=0, keepdims=True)
+
+        def into(t, _):
+            at = pl.ds(pl.multiple_of(t * tile, tile), tile)
+            mi_full[slot, at, :] = tn(n3_pair[:, :, at].reshape(inner, tile), hidden_grad).astype(BF)
+            return 0
+
+        lax.fori_loop(0, width // tile, into, 0)
+
+        def back(t, _):
+            at = pl.ds(pl.multiple_of(t * step, step), step)
+            mo_full[slot, at, :] = tn(active[slot, :, :, at].reshape(inner, step), grads).astype(BF)
+            return 0
+
+        lax.fori_loop(0, hidden // step, back, 0)
+
+    for slot in range(half):
+        wide_grads(slot)
+    mi_steps = Reduce(place, mi_full, mi_recv, mi_pieces, (reduce_send.at[0], reduce_recv.at[0])).phases()
+    mo_steps = Reduce(place, mo_full, mo_recv, mo_pieces, (reduce_send.at[1], reduce_recv.at[1])).phases()
+    wide_steps = [step for pair in zip(mi_steps, mo_steps) for step in pair]
+    for run in wide_steps[:2]:
+        run()
     dn3_copy.wait()
 
     vectors[...] = jnp.zeros_like(vectors)
@@ -470,6 +725,7 @@
         r2[chunk, :] = value.astype(BF)
 
     in_chunks(size, ROWS_AT_ONCE, third_back)
+    wide_steps[2]()
     dcross[...] = nt(r2[...], co_full[...].reshape(n * local, width)).astype(BF)
 
     def cross_back(idx, _):
@@ -484,6 +740,7 @@
         return 0
 
     lax.fori_loop(0, all_pairs, cross_back, 0)
+    wide_steps[3]()
 
     def dtext_copy(k):
         return remote(dtext_send.at[place.along(k)], dtext_recv.at[place.m], dtext_ssem.at[k], dtext_rsem.at[k], place.peer(k))
@@ -516,55 +773,26 @@
         dmixed_send[k] = nt(r1[...], so_full[place.along(k)]).astype(BF)
         dmix_copy(k).start()
     dmixed[own_rows, :] = nt(r1[...], so_full[place.m]).astype(BF)
-
-    tile = min(256, width)
-
-    def wide_grads(slot):
-        inner = n3_pair.shape[0] * size
-        hidden_grad = dhidden[slot].reshape(inner, hidden)
-        grads = grad_pair[...].reshape(inner, width)
-        bias_grad[slot] = jnp.sum(hidden_grad.astype(F32), axis=0, keepdims=True)
-
-        def into(t, _):
-            at = pl.ds(pl.multiple_of(t * tile, tile), tile)
-            mi_full[slot, at, :] = tn(n3_pair[:, :, at].reshape(inner, tile), hidden_grad).astype(BF)
-            return 0
-
-        lax.fori_loop(0, width // tile, into, 0)
-
-        def back(t, _):
-            at = pl.ds(pl.multiple_of(t * step, step), step)
-            mo_full[slot, at, :] = tn(active[slot, :, :, at].reshape(inner, step), grads).astype(BF)
-            return 0
-
-        lax.fori_loop(0, hidden // step, back, 0)
-
-    for slot in range(half):
-        wide_grads(slot)
-    stores = [
-        pltpu.make_async_copy(mi_full, mi_grad, store_sem.at[0]),
-        pltpu.make_async_copy(mo_full, mo_grad, store_sem.at[1]),
-    ]
-    for store in stores:
-        store.start()
+    wide_steps[4]()
+
+    stores = []
 
     def small_grad(left, right, keep, target, index):
-        def into(t, _):
-            at = pl.ds(pl.multiple_of(t * tile, tile), tile)
-            turned = left[:, at]
-            for g in range(n):
-                keep[g, at, :] = tn(turned, right[:, g * local : (g + 1) * local]).astype(BF)
-            return 0
-
-        lax.fori_loop(0, width // tile, into, 0)
+        for g in range(n):
+            heads = slice(g * local, (g + 1) * local)
+            if keep.shape[1] == local:
+                keep[g] = tn(left[:, heads], right[...]).astype(BF)
+            else:
+                keep[g] = tn(left[...], right[:, heads]).astype(BF)
         copy = pltpu.make_async_copy(keep, target, store_sem.at[index])
         copy.start()
         stores.append(copy)
 
-    small_grad(n2, dquery, cq_full, cq_grad, 2)
-    small_grad(r1, mixed_all, so_keep, so_grad, 3)
-    small_grad(r2, cross, co_keep, co_grad, 4)
-
+    small_grad(n2, dquery, cq_full, cq_grad, 0)
+    small_grad(mixed_all, r1, so_full, so_grad, 1)
+    small_grad(cross, r2, co_full, co_grad, 2)
+
+    wide_steps[5]()
     out_copy.wait()
 
     def finish_out(chunk):
@@ -572,6 +800,8 @@
         out[chunk, :] = value.astype(BF)
 
     in_chunks(size, ROWS_AT_ONCE, finish_out)
+    for run in wide_steps[6:]:
+        run()
     for k in offsets:
         dtext_copy(k).wait()
     total = dtext_send[place.m].astype(F32)
@@ -598,18 +828,19 @@
     dma, mem = pltpu.SemaphoreType.DMA, pltpu.VMEM
     shape = jax.ShapeDtypeStruct
     few = max(half - 1, 1)
+    bits = (sizes["dp"] // 2).bit_length() - 1
     return pl.pallas_call(
         partial(layer_kernel, sizes),
         out_shape=[
             shape((rows, 3 * local), BF), shape((rows, width), BF), shape((rows, local), BF),
             shape((pairs, n, 1, 2 * size), F32), shape((size, width), BF), shape((size, width), F32),
             shape((rows, local), BF), shape((slots, 2 * local), BF),
-            shape((n, width, local), BF), shape((n, width, local), BF), shape((n, width, local), BF),
-            shape((half, width, hidden), BF), shape((half, hidden, width), BF),
+            shape((n, local, width), BF), shape((n, width, local), BF), shape((n, local, width), BF),
+            piece_shape(half, width, hidden, bits), piece_shape(half, hidden, width, bits),
             shape((half, 1, hidden), F32), shape((8, width), F32),
         ],
         in_specs=[vmem] * 6 + [pl.BlockSpec(memory_space=pltpu.SMEM)] + [vmem] * 6 + [hbm] * 6,
-        out_specs=[vmem] * 8 + [hbm] * 5 + [vmem] * 2,
+        out_specs=[vmem] * 8 + [hbm] * 3 + [vmem] * 4,
         scratch_shapes=[
             mem((n, size, local), BF), mem((n, slots, 2 * local), BF),
             mem((n, local, width), BF), mem((n, width, local), BF), mem((n, local, width), BF),
@@ -623,12 +854,12 @@
             mem((size, width), BF), mem((size, width), BF), mem((size, width), BF), mem((size, width), BF),
             mem((size, width), BF), mem((size, n * local), BF), mem((size, width), BF),
             mem((n, size, local), BF), mem((n, slots, 2 * local), BF), mem((n, slots, 2 * local), BF),
-            mem((slots, 2 * local), BF), mem((n, width, local), BF), mem((n, width, local), BF),
+            mem((slots, 2 * local), BF), recv_space(half, width, hidden, bits), recv_space(half, hidden, width, bits),
             dma((3, n - 1, hops)), dma((3, n - 1, hops)), dma((3,)),
             dma((2, few, hops)), dma((2, few, hops)), dma((2,)),
             dma((n,)), dma((n,)), dma(()),
-            dma((n,)), dma((n,)), dma((half,)), dma((half,)), dma((2,)),
-            dma((3,)), dma((3,)), dma((n,)), dma((n,)), dma((n,)), dma((n,)), dma((5,)),
+            dma((n + 1,)), dma((n + 1,)), dma((half,)), dma((half,)), dma((2,)),
+            dma((3,)), dma((3,)), dma((n,)), dma((n,)), dma((n,)), dma((n,)), dma((3,)), dma((2, 1 + 2 * bits)), dma((2, 1 + 2 * bits)),
         ],
         compiler_params=pltpu.CompilerParams(collective_id=1, has_side_effects=True, vmem_limit_bytes=VMEM_LIMIT),
         cost_estimate=pl.CostEstimate(flops=22 << 30, bytes_accessed=48 << 20, transcendentals=8 << 20),
@@ -636,168 +867,26 @@
       so, cq, co, mi, mo, grad_out)
 
 
-class Reduce:
-    def __init__(self, place, ref, recv, pieces, other, final, whole, rule, sems):
-        self.place, self.ref, self.recv, self.pieces, self.other, self.final, self.whole = (
-            place, ref, recv, pieces, other, final, whole)
-        self.slots, self.rows, self.columns = ref.shape
-        self.half = self.rows // 2
-        self.part = self.half // 2
-        self.bits = (place.dp // 2).bit_length() - 1
-        self.count = self.part >> self.bits
-        self.rule, (self.send, self.recv_sem, self.keep) = rule, sems
-        self.chip = place.d // 2
-        if rule == "all":
-            self.hops = [(k, place.along(k)) for k in range(1, place.n)]
-            self.slot = place.m
-        elif rule == "parity":
-            half = place.n // 2
-            self.hops = [(2 * k, lax.rem(place.m // 2 + k, half)) for k in range(1, half)]
-            self.slot = place.m // 2
-        else:
-            self.hops, self.slot = [], 0
-
-    def bit(self, p, k):
-        b = k if p == 0 else self.bits - 1 - k
-        value = lax.rem(self.chip // (1 << b), 2)
-        chip = self.chip + (1 - 2 * value) * (1 << b)
-        return value, (2 * chip + self.place.core, self.place.m)
-
-    def region(self, p, k):
-        start = self.place.core * self.half + p * self.part
-        for t in range(k):
-            start = start + self.bit(p, t)[0] * (self.part >> (t + 1))
-        return start
-
-    def span(self, start, count):
-        return pl.ds(pl.multiple_of(start, self.count), count)
-
-    def copy(self, src, dst, index, device):
-        return pltpu.make_async_remote_copy(
-            src_ref=src, dst_ref=dst, send_sem=self.send.at[index], recv_sem=self.recv_sem.at[index],
-            device_id=device, device_id_type=MESH,
-        )
-
-    def core_copy(self):
-        away = self.span((1 - self.place.core) * self.half, self.half)
-        return self.copy(self.ref.at[:, away, :], self.recv.at[:, pl.ds(0, self.half), :], 0, self.place.partner)
-
-    def offset(self, p, k):
-        return self.half + p * (self.part - self.count) + sum(self.part >> (t + 1) for t in range(k))
-
-    def chip_copy(self, p, k):
-        value, device = self.bit(p, k)
-        count = self.part >> (k + 1)
-        away = self.span(self.region(p, k) + (1 - value) * count, count)
-        return self.copy(
-            self.ref.at[:, away, :], self.recv.at[:, pl.ds(self.offset(p, k), count), :], 1 + p * self.bits + k, device)
-
-    def far_copy(self, index):
-        hop, slot = self.hops[index]
-        return self.copy(self.pieces.at[slot], self.other.at[self.slot], 1 + 4 * self.bits + index, self.place.peer(hop))
-
-    def spread_copy(self, p, k):
-        _, device = self.bit(p, k)
-        count = self.part >> (k + 1)
-        rows = self.span(self.region(p, k + 1), count)
-        block = self.whole.at[rows, :]
-        src = self.final.at[pl.ds(p * self.count, self.count), :] if k == self.bits - 1 else block
-        return self.copy(src, block, 1 + 2 * self.bits + p * self.bits + k, device)
-
-    def keep_copy(self, p):
-        rows = self.span(self.region(p, self.bits), self.count)
-        return pltpu.make_async_copy(self.final.at[pl.ds(p * self.count, self.count), :], self.whole.at[rows, :], self.keep.at[p])
-
-    def core_spread(self):
-        block = self.whole.at[self.span(self.place.core * self.half, self.half), :]
-        return self.copy(block, block, 1 + 4 * self.bits + self.place.n, self.place.partner)
-
-    def add(self, start, offset, count, target, target_start):
-        chunk = min(32, count)
-
-        def run(t, _):
-            at = t * chunk
-            for s in range(self.slots):
-                mine = self.ref[s, self.span_of(start + at, chunk), :].astype(F32)
-                theirs = self.recv[s, self.span_of(offset + at, chunk), :].astype(F32)
-                target[s, self.span_of(target_start + at, chunk), :] = (mine + theirs).astype(BF)
-            return 0
-
-        lax.fori_loop(0, count // chunk, run, 0)
-
-    def span_of(self, start, chunk):
-        return pl.ds(pl.multiple_of(start, 16), chunk)
-
-    def phases(self):
-        bits = self.bits
-
-        def begin():
-            self.core_copy().start()
-
-        def core_sum():
-            self.core_copy().wait()
-            self.add(self.place.core * self.half, 0, self.half, self.ref, self.place.core * self.half)
-            for p in range(2):
-                self.chip_copy(p, 0).start()
-
-        def chip_sum(k):
-            for p in range(2):
-                self.chip_copy(p, k).wait()
-                last = k == bits - 1
-                start = self.region(p, k + 1)
-                self.add(start, self.offset(p, k), self.part >> (k + 1), self.pieces if last else self.ref,
-                         p * self.count if last else start)
-                if not last:
-                    self.chip_copy(p, k + 1).start()
-            if k == bits - 1:
-                for index in range(len(self.hops)):
-                    self.far_copy(index).start()
-
-        def far_sum():
-            total = self.pieces[self.slot].astype(F32)
-            for index, (hop, _) in enumerate(self.hops):
-                self.far_copy(index).wait()
-                source = self.place.along(self.place.n - hop)
-                total += self.other[source if self.rule == "all" else source // 2].astype(F32)
-            self.final[...] = total.astype(BF)
-            for p in range(2):
-                self.keep_copy(p).start()
-                self.spread_copy(p, bits - 1).start()
-            for p in range(2):
-                self.keep_copy(p).wait()
-
-        def spread(k):
-            for p in range(2):
-                self.spread_copy(p, k).wait()
-                if k > 0:
-                    self.spread_copy(p, k - 1).start()
-            if k == 0:
-                self.core_spread().start()
-
-        def end():
-            self.core_spread().wait()
-
-        steps = [begin, core_sum] + [partial(chip_sum, k) for k in range(bits)] + [far_sum]
-        return steps + [partial(spread, k) for k in reversed(range(bits))] + [end]
-
-
 def back_kernel(
     sizes,
-    gain1, qkv, kv, text, residual, projected, normed, mixed, totals, dmixed, dtext, early,
-    image, mi_grad, mo_grad, so_grad, cq_grad, co_grad,
-    image_grad, text_grad, early_out, late_out, mi_out, mo_out, small_out, joint_out,
-    image_rows, stacked, above, delta, dquery, dprojected, dn1_send, dn1_recv, dn1_own,
-    mi_ref, mi_recv, mi_pieces, mi_other, mi_final, mo_ref, mo_recv, mo_pieces, mo_other, mo_final,
-    small_ref, small_recv, small_pieces, small_other, small_final, joint_ref, joint_recv, joint_pieces, joint_final,
+    gain1, qkv, kv, text, residual, projected, normed, mixed, totals, dmixed, dtext, early, mi_pieces, mo_pieces,
+    image, so_grad, cq_grad, co_grad,
+    image_grad, text_grad, early_out, late_out, mi_out, mo_out, so_out, cq_out, co_out, joint_out,
+    image_rows, stacked, above, delta, dquery, dprojected,
+    near_hold, near_send, near_recv, far_send, far_recv, dn1_own,
+    mi_other, mi_final, mo_other, mo_final,
+    so_ref, so_recv, so_pieces, so_other, so_final, cq_ref, cq_recv, cq_pieces, cq_other, cq_final,
+    co_ref, co_recv, co_pieces, co_other, co_final, joint_ref, joint_recv, joint_pieces, joint_final,
     early_dp, early_mp, early_own, late, late_dp, late_mp, late_own, text_send, text_recv,
-    reduce_send, reduce_recv, reduce_keep, load_sem, dn1_ssem, dn1_rsem, text_ssem, text_rsem,
-    vec_ssem, vec_rsem, vec_zsend, vec_zrecv,
+    reduce_send, reduce_recv, spread_send, spread_recv, spread_keep, load_sem,
+    near_ssem, near_rsem, far_ssem, far_rsem, text_ssem, text_rsem, vec_ssem, vec_rsem, vec_zsend, vec_zrecv,
 ):
     place = Place(sizes)
     n, dp = place.n, place.dp
     rows, width = normed.shape
     local = mixed.shape[1]
     size = rows // n
+    half = n // 2
     pairs = local // PAIR
     offsets = list(range(1, n))
     everyone = [lax.rem(place.d + k, dp) for k in range(1, dp)]
@@ -814,22 +903,28 @@
     loads = [
         pltpu.make_async_copy(src, dst, load_sem.at[t])
         for t, (src, dst) in enumerate((
-            (mi_grad, mi_ref), (mo_grad, mo_ref), (so_grad, small_ref.at[:, :, 0:local]),
-            (cq_grad, small_ref.at[:, :, local : 2 * local]), (co_grad, small_ref.at[:, :, 2 * local : 3 * local]),
-            (image.at[block_of(place.m), :], image_rows),
+            (so_grad, so_ref), (cq_grad, cq_ref), (co_grad, co_ref), (image.at[block_of(place.m), :], image_rows),
         ))
     ]
     for load in loads:
         load.start()
 
-    def unit(t, ref, recv, pieces, other, final, whole, rule):
-        sems = (reduce_send.at[t], reduce_recv.at[t], reduce_keep.at[t])
-        return Reduce(place, ref, recv, pieces, other, final, whole, rule, sems).phases()
-
-    mi_steps = unit(0, mi_ref, mi_recv, mi_pieces, mi_other, mi_final, mi_out, "parity")
-    mo_steps = unit(1, mo_ref, mo_recv, mo_pieces, mo_other, mo_final, mo_out, "parity")
-    small_steps = unit(2, small_ref, small_recv, small_pieces, small_other, small_final, small_out, "all")
-    joint_steps = unit(3, joint_ref, joint_recv, joint_pieces, None, joint_final, joint_out, "own")
+    def reduce(t, ref, recv, pieces):
+        return Reduce(place, ref, recv, pieces, (reduce_send.at[t], reduce_recv.at[t])).phases()
+
+    def spread(t, rows, pieces, other, final, whole, rule):
+        sems = (spread_send.at[t], spread_recv.at[t], spread_keep.at[t])
+        return Spread(place, rows, pieces, other, final, whole, rule, sems).phases()
+
+    mi_steps = spread(0, width, mi_pieces, mi_other, mi_final, mi_out, "parity")
+    mo_steps = spread(1, mo_out.shape[0], mo_pieces, mo_other, mo_final, mo_out, "parity")
+    so_steps = reduce(0, so_ref, so_recv, so_pieces) + spread(2, local, so_pieces, so_other, so_final, so_out, "all")
+    cq_steps = reduce(1, cq_ref, cq_recv, cq_pieces) + spread(3, width, cq_pieces, cq_other, cq_final, cq_out, "all")
+    co_steps = reduce(2, co_ref, co_recv, co_pieces) + spread(4, local, co_pieces, co_other, co_final, co_out, "all")
+    joint_steps = reduce(3, joint_ref, joint_recv, joint_pieces)
+    joint_steps += spread(5, width, joint_pieces, None, joint_final, joint_out, "own")
+    mi_steps[0]()
+    mo_steps[0]()
 
     class Vectors:
         def __init__(self, value, over_dp, own, over_mp, base):
@@ -885,13 +980,9 @@
         text_copy(k).start()
     joint_ref[0, :, 3 * local :] = tn(text[...], dtext[...]).astype(BF)
 
-    loads[0].wait()
-    mi_steps[0]()
-    loads[1].wait()
-    mo_steps[0]()
-    for load in loads[2:5]:
+    for load, steps in zip(loads, (so_steps, cq_steps, co_steps)):
         load.wait()
-    small_steps[0]()
+        steps[0]()
 
     def prepare(i, _):
         block = block_of(i)
@@ -908,12 +999,30 @@
         return 0
 
     lax.fori_loop(0, n, prepare, 0)
-    plan = [mi_steps[1], mo_steps[1], small_steps[1], mi_steps[2], mo_steps[2], early_sum.turn, small_steps[2], mi_steps[3]]
+    plan = [[so_steps[1]], [cq_steps[1]], [co_steps[1]], [mi_steps[1]], [so_steps[2]], [mo_steps[1]], [cq_steps[2]], [co_steps[2]]]
     each = -(-len(plan) // (n * pairs))
-
-    def dn1_copy(j):
-        gap = lax.rem(j - place.m + n, n)
-        return remote(dn1_send.at[j], dn1_recv.at[place.m], dn1_ssem.at[gap], dn1_rsem.at[gap], (place.d, j))
+    parity = lax.rem(place.m, 2)
+    mine = place.m // 2
+
+    def near_copy(t):
+        return remote(near_send.at[t], near_recv.at[t], near_ssem.at[t], near_rsem.at[t], (place.d, place.mate))
+
+    def far_copy(t):
+        gap = lax.rem(t - mine + half, half)
+        return remote(far_send.at[t], far_recv.at[mine], far_ssem.at[gap], far_rsem.at[gap], (place.d, 2 * t + parity))
+
+    def pass_on(t):
+        near_copy(t).wait()
+        total = near_hold[t] + near_recv[t].astype(F32)
+
+        @pl.when(mine == t)
+        def _():
+            dn1_own[...] = total
+
+        @pl.when(mine != t)
+        def _():
+            far_send[t] = total.astype(BF)
+            far_copy(t).start()
 
     point = 0
     for j in range(n):
@@ -943,19 +1052,23 @@
             dprojected[keys, columns] = (dquery[hp, j].T * SCALE).astype(BF)
             dprojected[keys, local + hp * PAIR : local + (hp + 1) * PAIR] = dkey.astype(BF)
             dprojected[keys, 2 * local + hp * PAIR : 2 * local + (hp + 1) * PAIR] = dvalue.astype(BF)
-            for phase in plan[point * each : (point + 1) * each]:
-                phase()
+            for phases in plan[point * each : (point + 1) * each]:
+                for phase in phases:
+                    phase()
             point += 1
         partial_sum = nt(dprojected[keys, :], qkv[...])
 
-        @pl.when(place.m == j)
+        @pl.when(parity == j % 2)
         def _():
-            dn1_own[...] = partial_sum
-
-        @pl.when(place.m != j)
+            near_hold[j // 2] = partial_sum
+
+        @pl.when(parity != j % 2)
         def _():
-            dn1_send[j] = partial_sum.astype(BF)
-            dn1_copy(j).start()
+            near_send[j // 2] = partial_sum.astype(BF)
+            near_copy(j // 2).start()
+
+        if j % 2 and j > 1:
+            pass_on(j // 2 - 1)
 
     tile_rows = min(256, width)
 
@@ -965,21 +1078,37 @@
         return 0
 
     lax.fori_loop(0, width // tile_rows, qkv_grad, 0)
-    done = 3 + (len(mi_steps) - 8)
+    bits = (dp // 2).bit_length() - 1
     joint_steps[0]()
-    mo_steps[3]()
-    small_steps[3]()
+    early_sum.turn()
+    pass_on(half - 1)
+    mi_steps[2]()
+    small_steps = (so_steps, cq_steps, co_steps)
+    for k in range(1, bits):
+        for steps in small_steps:
+            steps[2 + k]()
+    for steps in small_steps:
+        steps[2 + bits]()
     joint_steps[1]()
-    for k in range(4, len(mi_steps) - 1):
-        mi_steps[k]()
-        mo_steps[k]()
-        small_steps[k]()
-        joint_steps[k - 2]()
-
-    for k in offsets:
-        dn1_copy(place.along(k)).wait()
-        dn1_own[...] += dn1_recv[place.along(n - k)].astype(F32)
-    loads[5].wait()
+    mo_steps[2]()
+    for k in range(1, bits):
+        mi_steps[2 + k]()
+        mo_steps[2 + k]()
+    for k in range(bits):
+        joint_steps[2 + k]()
+        if k == 0:
+            for steps in small_steps:
+                steps[3 + bits]()
+    joint_steps[2 + bits]()
+    joint_steps[3 + bits]()
+    for k in range(bits - 1):
+        for steps in small_steps:
+            steps[4 + bits + k]()
+
+    for k in range(1, half):
+        far_copy(lax.rem(mine + k, half)).wait()
+        dn1_own[...] += far_recv[lax.rem(mine + half - k, half)].astype(F32)
+    loads[3].wait()
     late[...] = jnp.zeros_like(late)
 
     def last_back(chunk):
@@ -991,8 +1120,9 @@
 
     in_chunks(size, ROWS_AT_ONCE, last_back)
     late_sum.begin()
-    for k in range(len(mi_steps) - 3, len(mi_steps) - 1):
-        joint_steps[k]()
+    for steps in small_steps:
+        steps[3 + 2 * bits]()
+    joint_steps[4 + bits]()
     for k in offsets:
         text_copy(k).wait()
     total = text_send[place.m].astype(F32)
@@ -1007,18 +1137,20 @@
         take = jnp.where(lax.rem(place.m + j, 2) == 0, 1.0, 0.0)
         shared += early_mp[j, pl.ds(8 + place.m // 2, 1), :] * take
     early_out[7:8, :] = shared
+    for k in range(1, bits):
+        joint_steps[4 + bits + k]()
     late_sum.end()
     late_out[...] = late_sum.total()
-    for steps in (mi_steps, mo_steps, small_steps, joint_steps):
+    for steps in (mi_steps, mo_steps, *small_steps, joint_steps):
         steps[-1]()
 
 
-def back(sizes, gain1, qkv, kv, text, residual, projected, normed, mixed, totals, dmixed, dtext, early,
-         image, mi_grad, mo_grad, so_grad, cq_grad, co_grad):
+def back(sizes, gain1, qkv, kv, text, residual, projected, normed, mixed, totals, dmixed, dtext, early, mi_pieces, mo_pieces,
+         image, so_grad, cq_grad, co_grad, hidden):
     n, dp = sizes["mp"], sizes["dp"]
     rows, width = normed.shape
     slots = text.shape[0]
-    local, hidden = mixed.shape[1], mi_grad.shape[2]
+    local = mixed.shape[1]
     size, pairs, half = rows // n, local // PAIR, n // 2
     bits = (dp // 2).bit_length() - 1
     vmem, hbm = pl.BlockSpec(memory_space=pltpu.VMEM), pl.BlockSpec(memory_space=pl.ANY)
@@ -1026,38 +1158,42 @@
     shape = jax.ShapeDtypeStruct
 
     def unit(count, height, columns, rule):
-        piece = 2 * (height // 4 >> bits)
-        scratch = [mem((count, height, columns), BF), mem((count, height - piece, columns), BF), mem((count, piece, columns), BF)]
+        pieces = piece_shape(count, height, columns, bits).shape
+        scratch = []
+        if rule != "parity":
+            scratch += [mem((count, height, columns), BF), recv_space(count, height, columns, bits), mem(pieces, BF)]
         if rule != "own":
-            scratch.append(mem((count, piece, columns), BF))
-        return scratch + [mem((piece, columns), BF)]
+            scratch.append(mem(pieces, BF))
+        return scratch + [mem(pieces[1:], BF)]
 
     few = early.shape[0]
-    each = 2 + 4 * bits + n
+    whole = [(width, hidden), (hidden, width), (local, width), (width, local), (local, width), (width, 5 * local)]
+    block = mem((half, size, width), BF)
     return pl.pallas_call(
         partial(back_kernel, sizes),
         out_shape=[
             shape((size, width), F32), shape((slots // n, width), F32), shape((few, width), F32), shape((2, width), F32),
-            shape((width, hidden), BF), shape((hidden, width), BF), shape((width, 3 * local), BF), shape((width, 5 * local), BF),
-        ],
-        in_specs=[vmem] * 12 + [hbm] * 6,
-        out_specs=[vmem] * 4 + [hbm] * 4,
+        ] + [shape(extent, BF) for extent in whole],
+        in_specs=[vmem] * 14 + [hbm] * 4,
+        out_specs=[vmem] * 4 + [hbm] * 6,
         scratch_shapes=[
             mem((size, width), BF), mem((pairs, n, 2 * size, PAIR), BF), mem((pairs, n, 2 * size, PAIR), BF),
             mem((pairs, n, 1, 2 * size), F32), mem((pairs, n, PAIR, size), F32), mem((rows, 3 * local), BF),
-            mem((n, size, width), BF), mem((n, size, width), BF), mem((size, width), F32),
+            mem((half, size, width), F32), block, block, block, block, mem((size, width), F32),
             *unit(half, width, hidden, "parity"), *unit(half, hidden, width, "parity"),
-            *unit(n, width, 3 * local, "all"), *unit(1, width, 5 * local, "own"),
+            *unit(n, local, width, "all"), *unit(n, width, local, "all"), *unit(n, local, width, "all"),
+            *unit(1, width, 5 * local, "own"),
             mem((dp, few, width), F32), mem((n, few, width), F32), mem((few, width), F32),
             mem((2, width), F32), mem((dp, 2, width), F32), mem((n, 2, width), F32), mem((2, width), F32),
             mem((n, slots // n, width), BF), mem((n, slots // n, width), BF),
-            dma((4, each)), dma((4, each)), dma((4, 2)), dma((6,)), dma((n,)), dma((n,)), dma((n,)), dma((n,)),
+            dma((4, 1 + 2 * bits)), dma((4, 1 + 2 * bits)), dma((6, 1 + 2 * bits + n)), dma((6, 1 + 2 * bits + n)), dma((6, 2)),
+            dma((4,)), dma((half,)), dma((half,)), dma((half,)), dma((half,)), dma((n,)), dma((n,)),
             dma((2, dp)), dma((2, dp)), dma((2, n)), dma((2, n)),
         ],
-        compiler_params=pltpu.CompilerParams(collective_id=2, has_side_effects=True, vmem_limit_bytes=60 << 20),
+        compiler_params=pltpu.CompilerParams(collective_id=2, has_side_effects=True, vmem_limit_bytes=VMEM_LIMIT),
         cost_estimate=pl.CostEstimate(flops=8 << 30, bytes_accessed=48 << 20, transcendentals=4 << 20),
-    )(gain1, qkv, kv, text, residual, projected, normed, mixed, totals, dmixed, dtext, early,
-      image, mi_grad, mo_grad, so_grad, cq_grad, co_grad)
+    )(gain1, qkv, kv, text, residual, projected, normed, mixed, totals, dmixed, dtext, early, mi_pieces, mo_pieces,
+      image, so_grad, cq_grad, co_grad)
 
 
 def body(sizes, image, text, grad_out, lengths, gain1, shift1, qkv, so, gain2, shift2, cq, kv, co, gain3, shift3, mi,
@@ -1069,23 +1205,22 @@
     sizes = dict(sizes, share=share_of(local, sizes["dp"]))
     qkv, kv = qkv.reshape(width, 3 * local), kv.reshape(width, 2 * local)
     row = lambda value: value[None]
-    (projected, normed1, mixed, totals, out, residual, dmixed, dtext, so_grad, cq_grad, co_grad, mi_grad, mo_grad,
+    (projected, normed1, mixed, totals, out, residual, dmixed, dtext, so_grad, cq_grad, co_grad, mi_pieces, mo_pieces,
      in_bias_grad, vectors) = layer(
         sizes, image, row(gain1), row(shift1), qkv, text, kv, row(lengths), row(gain2), row(shift2), row(gain3),
         row(shift3), row(in_bias), row(out_bias), so, cq, co, mi, mo, grad_out)
     early = jnp.zeros((8 + -(-n // 2 // 8) * 8, width), F32)
     early = lax.dynamic_update_slice(early, vectors, (0, 0))
     early = lax.dynamic_update_slice(early, in_bias_grad[:, 0], (8, 0))
-    image_grad, text_grad, early, late, mi_sum, mo_sum, small_sum, joint_sum = back(
+    hidden = mi.shape[1]
+    image_grad, text_grad, early, late, mi_sum, mo_sum, so_sum, cq_sum, co_sum, joint_sum = back(
         sizes, row(gain1), qkv, kv, text, residual, projected, normed1, mixed, totals, dmixed, dtext, early,
-        image, mi_grad, mo_grad, so_grad, cq_grad, co_grad)
-    hidden = mi.shape[1]
-    small = lambda t: small_sum[:, t * local : (t + 1) * local].astype(F32)
+        mi_pieces, mo_pieces, image, so_grad, cq_grad, co_grad, hidden)
     return (
         out[None], image_grad[None], text_grad[None], late[0], late[1],
-        joint_sum[:, : 3 * local].astype(F32).reshape(width, 3, local), small(0).T, early[2], early[3], small(1),
-        joint_sum[:, 3 * local :].astype(F32).reshape(width, 2, local), small(2).T, early[4], early[5],
-        mi_sum.astype(F32), early[7, :hidden], mo_sum.astype(F32), early[6],
+        joint_sum[:, : 3 * local].astype(F32).reshape(width, 3, local), so_sum.astype(F32), early[2], early[3],
+        cq_sum.astype(F32), joint_sum[:, 3 * local :].astype(F32).reshape(width, 2, local), co_sum.astype(F32),
+        early[4], early[5], mi_sum.astype(F32), early[7, :hidden], mo_sum.astype(F32), early[6],
     )
 
 

time: 363 us -> 306 us (0.84); the launches traced: 362 us -> 301 us
  Pallas kernels: 327 us -> 267 us
    pallas_call x1, Pallas kernels: 175 us -> 124 us  [back(): pl.pallas_call(partial(back_kernel, sizes), out_shape=[shape((size, width...]
    pallas_call x1, Pallas kernels: 152 us -> 143 us  [layer(): pl.pallas_call(partial(layer_kernel, sizes), out_shape=[shape((rows, 3 *...]
    convert_element_type x0 -> x3, other arithmetic: none -> 5.3 us  [the longest x1 2.13 us: body(): so_sum.astype(F32)]
where the time goes in v4:
time: 306 us; the launch traced here: 301 us
  Pallas kernels  267 us (87%)
  local copies, waits for them, and re-layouts  19.5 us (6%)
  other arithmetic  13.4 us (4%)
    pallas_call x1, Pallas kernels, layer(): pl.pallas_call(partial(layer_kernel, sizes), out_shape=[shape((rows, 3 *...  143 us
    pallas_call x1, Pallas kernels, back(): pl.pallas_call(partial(back_kernel, sizes), out_shape=[shape((size, width...  124 us
    unnamed x22, local copies, waits for them, and re-layouts  10 us

profile of v4, /device:TPU:0, one launch (start us, length us, event | category | flops | bytes accessed | tf_op | source)
XLA Modules:
  0.0 301.4 jit_solution(13140162719416830850)
XLA Ops:
  0.7 0.0 copy-start.2
  1.4 2.4 copy.45
  3.9 0.0 copy-done.2
  3.9 0.9 copy.39
  4.7 1.6 copy.40.qkv
  6.3 142.9 %shard_map.322 = (bf16[1024,768]{1,0:T(8,128)(2,1)}, bf16[1024,1024]{1,0:T(8,128)(2,1)}, bf16[1024,256]{1,0:T(8,128)(2,1)}, f32[2,4,1,512]{3,2,1,0:T(1,128)}, bf...) custom-call(bf16[1024,1024]{1,0:T(8,128)(2,1)} %bitcast.47, ...), custom_call_target="tpu_custom_call" | custom-call | flops 23622320128 | bytes 50331648 | tf_op jit(solution)/shard_map/pallas_call | solution.py:832
  149.2 0.8 dynamic_update_slice.6
  149.9 0.7 bitcast_dynamic-update-slice_fusion.early
  150.6 0.0 copy-start.7
  150.6 0.6 copy-done.7
  151.3 124.2 %shard_map.323 = (f32[256,1024]{1,0:T(8,128)}, f32[32,1024]{1,0:T(8,128)}, f32[16,1024]{1,0:T(8,128)}, f32[2,1024]{1,0:T(2,128)}, bf16[1024,1024]{1,0:T(8,128)(2...) custom-call(f32[1,1024]{1,0:T(1,128)} %bitcast.59, ...), custom_call_target="tpu_custom_call" | custom-call | flops 8589934592 | bytes 50331648 | tf_op jit(solution)/shard_map/pallas_call | solution.py:1172
  275.5 0.0 copy-start.4
  275.5 1.7 fusion
  277.2 2.1 convert_element_type.17
  279.3 2.1 convert_element_type.18
  281.4 0.0 copy-done.4
  281.4 1.1 convert_element_type.19
  282.5 1.5 slice_convert_fusion.1
  284.0 2.4 reshape.63
  286.3 1.6 slice_convert_fusion
  288.0 2.4 copy.42
  290.3 0.0 copy-start.1
  290.4 3.7 %copy.43 = f32[1024,3,256]{2,0,1:T(8,128)} copy(f32[1024,3,256]{0,2,1:T(8,128)} %bitcast.30) | data formatting | bytes 6291456
  294.0 0.0 copy-done.1
  294.0 0.0 copy-start
  294.0 2.5 convert_element_type.20
  296.5 0.0 copy-done
  296.5 0.0 copy-start.5
  296.5 0.0 copy-start.3
  296.5 2.5 convert_element_type.21
  299.0 0.0 copy-done.5
  299.0 0.0 copy-start.6
  299.0 0.8 copy.52
  299.8 0.0 copy-done.3
  299.8 1.0 copy.53
  300.8 0.0 copy-done.6
  300.8 0.7 copy.54
Async XLA Ops:
  0.7 3.2 %copy-start.2 = (bf16[1024,3,256]{2,0,1:T(8,128)(2,1)S(1)}, bf16[1024,3,256]{2,0,1:T(8,128)(2,1)}, u32[]{:S(2)}) copy-start(bf16[1024,3,256]{2,0,1:T(8,128)(2,1)} %param.25) | copy-start | bytes 4718596
  150.6 0.6 copy-start.7
  275.5 5.9 %copy-start.4 = (bf16[256,1024]{1,0:T(8,128)(2,1)S(1)}, bf16[256,1024]{1,0:T(8,128)(2,1)}, u32[]{:S(2)}) copy-start(bf16[256,1024]{1,0:T(8,128)(2,1)} %get-tuple-element.65) | copy-start | bytes 1572868
  290.3 3.7 %copy-start.1 = (bf16[1024,1024]{1,0:T(8,128)(2,1)S(1)}, bf16[1024,1024]{1,0:T(8,128)(2,1)}, u32[]{:S(2)}) copy-start(bf16[1024,1024]{1,0:T(8,128)(2,1)} %get-tuple-element.66) | copy-start | bytes 6291460
  294.0 2.5 copy-start
  296.5 2.5 copy-start.5
  296.5 3.3 %copy-start.3 = (f32[256,1024]{1,0:T(8,128)S(1)}, f32[256,1024]{1,0:T(8,128)}, u32[]{:S(2)}) copy-start(f32[256,1024]{1,0:T(8,128)} %get-tuple-element.58) | copy-start | bytes 3145732
  299.0 1.8 copy-start.6

commit v5 on v4

--- a/solution.py
+++ b/solution.py
@@ -92,11 +92,13 @@
         return (self.base + 2 * chip + self.core, self.m), self.core * (self.share // 2) + chip
 
 
-def barrier(devices):
-    sem = pltpu.get_barrier_semaphore()
+def greet(devices):
     for device in devices:
-        pl.semaphore_signal(sem, inc=1, device_id=device, device_id_type=MESH)
-    pl.semaphore_wait(sem, len(devices))
+        pl.semaphore_signal(pltpu.get_barrier_semaphore(), inc=1, device_id=device, device_id_type=MESH)
+
+
+def meet(devices):
+    pl.semaphore_wait(pltpu.get_barrier_semaphore(), len(devices))
 
 
 class Gather:
@@ -358,22 +360,26 @@
         hop, slot = self.hops[index]
         return self.copy(self.pieces.at[slot], self.other.at[self.slot], 1 + 2 * self.rows.bits + index, self.place.peer(hop))
 
+    def view(self, ref, start, count):
+        span = self.rows.span(start, count)
+        return ref.at[:, span, :] if self.rule == "own" else ref.at[span, :]
+
     def spread_copy(self, p, k):
         rows = self.rows
         count = rows.left[k + 1]
-        block = self.whole.at[rows.span(rows.region(p, k + 1), count), :]
+        block = self.view(self.whole, rows.region(p, k + 1), count)
         first = not any(rows.cut(t) for t in range(k + 1, rows.bits))
-        src = self.final.at[pl.ds(p * rows.count, rows.count), :] if first else block
+        src = self.view(self.final, p * rows.count, rows.count) if first else block
         return self.copy(src, block, 1 + p * rows.bits + k, rows.bit(p, k)[1])
 
     def keep_copy(self, p):
         rows = self.rows
-        block = self.whole.at[rows.span(rows.region(p, rows.bits), rows.count), :]
-        return pltpu.make_async_copy(self.final.at[pl.ds(p * rows.count, rows.count), :], block, self.keep.at[p])
+        block = self.view(self.whole, rows.region(p, rows.bits), rows.count)
+        return pltpu.make_async_copy(self.view(self.final, p * rows.count, rows.count), block, self.keep.at[p])
 
     def core_spread(self):
         half = self.rows.half
-        block = self.whole.at[self.rows.span(self.place.core * half, half), :]
+        block = self.view(self.whole, self.place.core * half, half)
         return self.copy(block, block, 0, self.place.partner)
 
     def phases(self):
@@ -385,12 +391,13 @@
                 self.far_copy(index).start()
 
         def far_sum():
-            total = self.pieces[self.slot].astype(F32)
-            for index, (hop, _) in enumerate(self.hops):
-                self.far_copy(index).wait()
-                source = self.place.along(self.place.n - hop)
-                total += self.other[source if self.rule == "all" else source // 2].astype(F32)
-            self.final[...] = total.astype(BF)
+            if self.hops:
+                total = self.pieces[self.slot].astype(F32)
+                for index, (hop, _) in enumerate(self.hops):
+                    self.far_copy(index).wait()
+                    source = self.place.along(self.place.n - hop)
+                    total += self.other[source if self.rule == "all" else source // 2].astype(F32)
+                self.final[...] = total.astype(BF)
             for p in range(2):
                 self.keep_copy(p).start()
                 self.spread_copy(p, cuts[0]).start()
@@ -462,7 +469,7 @@
     image, gain1, shift1, qkv, text, kv, length, gain2, shift2, gain3, shift3, in_bias, out_bias,
     so, cq, co, mi, mo, grad_out,
     projected, normed, mixed, totals, out, residual, dmixed, dtext, so_grad, cq_grad, co_grad, mi_pieces, mo_pieces,
-    bias_grad, vectors,
+    vectors,
     mixed_rows, text_proj, so_full, cq_full, co_full, mi_full, mo_full, bias_full,
     grad_pair, mixed_all, first, second, work, grad2, out_part,
     n2, query, cross, cross_totals, dquery, n3_pair, active, dhidden,
@@ -481,9 +488,10 @@
     mate = (place.d, place.mate)
     mine = place.m // 2
     chips = place.dp // 2
-    greet = [place.peer(k) for k in offsets] + [place.partner]
-    greet += [(2 * lax.rem(place.d // 2 + k, chips) + place.core, place.m) for k in range(1, chips)]
-    barrier(greet)
+    partners = [place.peer(k) for k in offsets] + [place.partner]
+    partners += [(2 * lax.rem(place.d // 2 + k, chips) + place.core, place.m) for k in range(1, chips)]
+    greet(partners)
+    meet(partners)
 
     def remote(src, dst, send, recv, device):
         return pltpu.make_async_remote_copy(
@@ -502,6 +510,7 @@
         item.step(0)
     for item in small + wide:
         item.local().start()
+    wide[0].step(0)
 
     def block_of(index):
         return pl.ds(pl.multiple_of(index * size, size), size)
@@ -530,7 +539,8 @@
             normed[at, :] = (normal * gain1[...] + shift1[...]).astype(BF)
 
         in_chunks(size, ROWS_AT_ONCE, norm)
-        projected[block, :] = nn(normed[block, :], qkv[...]).astype(BF)
+        for t in range(3):
+            projected[block, t * local : (t + 1) * local] = nn(normed[block, :], qkv[t]).astype(BF)
         return 0
 
     lax.fori_loop(0, n, project, 0)
@@ -574,8 +584,7 @@
         for item in plan[i]:
             item.step(2)
 
-    for item in wide:
-        item.step(0)
+    wide[1].step(0)
     for k in even:
         text_copy(k).wait_recv()
         text_pass(k).start()
@@ -686,7 +695,7 @@
         inner = n3_pair.shape[0] * size
         hidden_grad = dhidden[slot].reshape(inner, hidden)
         grads = grad_pair[...].reshape(inner, width)
-        bias_grad[slot] = jnp.sum(hidden_grad.astype(F32), axis=0, keepdims=True)
+        vectors[8 + slot : 9 + slot, 0:hidden] = jnp.sum(hidden_grad.astype(F32), axis=0, keepdims=True)
 
         def into(t, _):
             at = pl.ds(pl.multiple_of(t * tile, tile), tile)
@@ -702,6 +711,7 @@
 
         lax.fori_loop(0, hidden // step, back, 0)
 
+    vectors[...] = jnp.zeros_like(vectors)
     for slot in range(half):
         wide_grads(slot)
     mi_steps = Reduce(place, mi_full, mi_recv, mi_pieces, (reduce_send.at[0], reduce_recv.at[0])).phases()
@@ -711,7 +721,6 @@
         run()
     dn3_copy.wait()
 
-    vectors[...] = jnp.zeros_like(vectors)
 
     def third_back(chunk):
         grad = work[chunk, :] + dn3_recv[chunk, :].astype(F32)
@@ -837,10 +846,10 @@
             shape((rows, local), BF), shape((slots, 2 * local), BF),
             shape((n, local, width), BF), shape((n, width, local), BF), shape((n, local, width), BF),
             piece_shape(half, width, hidden, bits), piece_shape(half, hidden, width, bits),
-            shape((half, 1, hidden), F32), shape((8, width), F32),
+            shape((8 + -(-half // 8) * 8, width), F32),
         ],
         in_specs=[vmem] * 6 + [pl.BlockSpec(memory_space=pltpu.SMEM)] + [vmem] * 6 + [hbm] * 6,
-        out_specs=[vmem] * 8 + [hbm] * 3 + [vmem] * 4,
+        out_specs=[vmem] * 8 + [hbm] * 3 + [vmem] * 3,
         scratch_shapes=[
             mem((n, size, local), BF), mem((n, slots, 2 * local), BF),
             mem((n, local, width), BF), mem((n, width, local), BF), mem((n, local, width), BF),
@@ -876,7 +885,7 @@
     near_hold, near_send, near_recv, far_send, far_recv, dn1_own,
     mi_other, mi_final, mo_other, mo_final,
     so_ref, so_recv, so_pieces, so_other, so_final, cq_ref, cq_recv, cq_pieces, cq_other, cq_final,
-    co_ref, co_recv, co_pieces, co_other, co_final, joint_ref, joint_recv, joint_pieces, joint_final,
+    co_ref, co_recv, co_pieces, co_other, co_final, joint_ref, joint_recv, joint_pieces,
     early_dp, early_mp, early_own, late, late_dp, late_mp, late_own, text_send, text_recv,
     reduce_send, reduce_recv, spread_send, spread_recv, spread_keep, load_sem,
     near_ssem, near_rsem, far_ssem, far_rsem, text_ssem, text_rsem, vec_ssem, vec_rsem, vec_zsend, vec_zrecv,
@@ -890,7 +899,8 @@
     pairs = local // PAIR
     offsets = list(range(1, n))
     everyone = [lax.rem(place.d + k, dp) for k in range(1, dp)]
-    barrier([place.peer(k) for k in offsets] + [(device, place.m) for device in everyone])
+    partners = [place.peer(k) for k in offsets] + [(device, place.m) for device in everyone]
+    greet(partners)
 
     def remote(src, dst, send, recv, device):
         return pltpu.make_async_remote_copy(
@@ -922,10 +932,7 @@
     cq_steps = reduce(1, cq_ref, cq_recv, cq_pieces) + spread(3, width, cq_pieces, cq_other, cq_final, cq_out, "all")
     co_steps = reduce(2, co_ref, co_recv, co_pieces) + spread(4, local, co_pieces, co_other, co_final, co_out, "all")
     joint_steps = reduce(3, joint_ref, joint_recv, joint_pieces)
-    joint_steps += spread(5, width, joint_pieces, None, joint_final, joint_out, "own")
-    mi_steps[0]()
-    mo_steps[0]()
-
+    joint_steps += spread(5, width, joint_pieces, None, joint_pieces, joint_out, "own")
     class Vectors:
         def __init__(self, value, over_dp, own, over_mp, base):
             self.value, self.over_dp, self.own, self.over_mp, self.base = value, over_dp, own, over_mp, base
@@ -966,8 +973,6 @@
 
     early_sum = Vectors(early, early_dp, early_own, early_mp, 0)
     late_sum = Vectors(late, late_dp, late_own, late_mp, 1)
-    early_sum.begin()
-
     part = text_grad.shape[0]
     spread_text = nt(dtext[...], kv[...]).astype(BF)
     for g in range(n):
@@ -976,13 +981,8 @@
     def text_copy(k):
         return remote(text_send.at[place.along(k)], text_recv.at[place.m], text_ssem.at[k], text_rsem.at[k], place.peer(k))
 
-    for k in offsets:
-        text_copy(k).start()
-    joint_ref[0, :, 3 * local :] = tn(text[...], dtext[...]).astype(BF)
-
-    for load, steps in zip(loads, (so_steps, cq_steps, co_steps)):
-        load.wait()
-        steps[0]()
+    for t in range(2):
+        joint_ref[3 + t] = tn(text[...], dtext[:, t * local : (t + 1) * local]).astype(BF)
 
     def prepare(i, _):
         block = block_of(i)
@@ -999,7 +999,17 @@
         return 0
 
     lax.fori_loop(0, n, prepare, 0)
-    plan = [[so_steps[1]], [cq_steps[1]], [co_steps[1]], [mi_steps[1]], [so_steps[2]], [mo_steps[1]], [cq_steps[2]], [co_steps[2]]]
+    meet(partners)
+    mi_steps[0]()
+    mo_steps[0]()
+    for load, steps in zip(loads, (so_steps, cq_steps, co_steps)):
+        load.wait()
+        steps[0]()
+    early_sum.begin()
+    for k in offsets:
+        text_copy(k).start()
+
+    plan = [[so_steps[1]], [cq_steps[1]], [co_steps[1]]]
     each = -(-len(plan) // (n * pairs))
     parity = lax.rem(place.m, 2)
     mine = place.m // 2
@@ -1056,7 +1066,7 @@
                 for phase in phases:
                     phase()
             point += 1
-        partial_sum = nt(dprojected[keys, :], qkv[...])
+        partial_sum = sum(nt(dprojected[keys, t * local : (t + 1) * local], qkv[t]) for t in range(3))
 
         @pl.when(parity == j % 2)
         def _():
@@ -1067,40 +1077,45 @@
             near_send[j // 2] = partial_sum.astype(BF)
             near_copy(j // 2).start()
 
-        if j % 2 and j > 1:
-            pass_on(j // 2 - 1)
-
     tile_rows = min(256, width)
 
     def qkv_grad(t, _):
         at = pl.ds(pl.multiple_of(t * tile_rows, tile_rows), tile_rows)
-        joint_ref[0, at, 0 : 3 * local] = tn(normed[:, at], dprojected[...]).astype(BF)
+        total = tn(normed[:, at], dprojected[...]).astype(BF)
+        for t in range(3):
+            joint_ref[t, at, :] = total[:, t * local : (t + 1) * local]
         return 0
 
     lax.fori_loop(0, width // tile_rows, qkv_grad, 0)
     bits = (dp // 2).bit_length() - 1
+    small_steps = (so_steps, cq_steps, co_steps)
     joint_steps[0]()
     early_sum.turn()
+    for steps in small_steps:
+        steps[2]()
+    joint_steps[1]()
+    for t in range(half - 1):
+        pass_on(t)
+    mi_steps[1]()
+    mo_steps[1]()
     pass_on(half - 1)
-    mi_steps[2]()
-    small_steps = (so_steps, cq_steps, co_steps)
     for k in range(1, bits):
         for steps in small_steps:
             steps[2 + k]()
     for steps in small_steps:
         steps[2 + bits]()
-    joint_steps[1]()
+    for k in range(bits):
+        joint_steps[2 + k]()
+    joint_steps[2 + bits]()
+    joint_steps[3 + bits]()
+    mi_steps[2]()
     mo_steps[2]()
+    for steps in small_steps:
+        steps[3 + bits]()
     for k in range(1, bits):
         mi_steps[2 + k]()
         mo_steps[2 + k]()
-    for k in range(bits):
-        joint_steps[2 + k]()
-        if k == 0:
-            for steps in small_steps:
-                steps[3 + bits]()
-    joint_steps[2 + bits]()
-    joint_steps[3 + bits]()
+    joint_steps[4 + bits]()
     for k in range(bits - 1):
         for steps in small_steps:
             steps[4 + bits + k]()
@@ -1122,7 +1137,6 @@
     late_sum.begin()
     for steps in small_steps:
         steps[3 + 2 * bits]()
-    joint_steps[4 + bits]()
     for k in offsets:
         text_copy(k).wait()
     total = text_send[place.m].astype(F32)
@@ -1163,11 +1177,11 @@
         if rule != "parity":
             scratch += [mem((count, height, columns), BF), recv_space(count, height, columns, bits), mem(pieces, BF)]
         if rule != "own":
-            scratch.append(mem(pieces, BF))
-        return scratch + [mem(pieces[1:], BF)]
+            scratch += [mem(pieces, BF), mem(pieces[1:], BF)]
+        return scratch
 
     few = early.shape[0]
-    whole = [(width, hidden), (hidden, width), (local, width), (width, local), (local, width), (width, 5 * local)]
+    whole = [(width, hidden), (hidden, width), (local, width), (width, local), (local, width), (5, width, local)]
     block = mem((half, size, width), BF)
     return pl.pallas_call(
         partial(back_kernel, sizes),
@@ -1182,7 +1196,7 @@
             mem((half, size, width), F32), block, block, block, block, mem((size, width), F32),
             *unit(half, width, hidden, "parity"), *unit(half, hidden, width, "parity"),
             *unit(n, local, width, "all"), *unit(n, width, local, "all"), *unit(n, local, width, "all"),
-            *unit(1, width, 5 * local, "own"),
+            *unit(5, width, local, "own"),
             mem((dp, few, width), F32), mem((n, few, width), F32), mem((few, width), F32),
             mem((2, width), F32), mem((dp, 2, width), F32), mem((n, 2, width), F32), mem((2, width), F32),
             mem((n, slots // n, width), BF), mem((n, slots // n, width), BF),
@@ -1196,6 +1210,54 @@
       image, so_grad, cq_grad, co_grad)
 
 
+def finish_kernel(slots, out, image_grad, text_grad, early, late, mi, mo, so, cq, co, joint,
+                  to_out, to_image, to_text, to_mi, to_mo, to_so, to_cq, to_co, to_qkv, to_kv, to_bias, *to_vectors):
+    to_out[...] = out[...]
+    to_image[...] = image_grad[...]
+    to_text[...] = text_grad[...]
+    for source, target in ((mi, to_mi), (mo, to_mo), (so, to_so), (cq, to_cq), (co, to_co)):
+        target[...] = source[...].astype(F32)
+    for t in range(3):
+        to_qkv[t] = joint[t].astype(F32)
+    for t in range(2):
+        to_kv[:, t, :] = joint[3 + t].astype(F32)
+    for t in range(2):
+        to_vectors[t][...] = late[t : t + 1, :]
+    for t in range(2, 7):
+        to_vectors[t][...] = early[t : t + 1, :]
+    to_bias[...] = early[7:8, 0 : to_bias.shape[1]]
+
+
+def finish(out, image_grad, text_grad, early, late, mi, mo, so, cq, co, joint):
+    steps = 8
+    width, hidden = mi.shape
+    local = so.shape[0]
+
+    def cut(value, axis=0):
+        shape = list(value.shape)
+        shape[axis] //= steps
+        return pl.BlockSpec(tuple(shape), lambda i: tuple(i if t == axis else 0 for t in range(len(shape))))
+
+    def whole(shape):
+        return pl.BlockSpec(tuple(shape), lambda i: (0,) * len(shape))
+
+    shape = jax.ShapeDtypeStruct
+    sums = [shape(value.shape, F32) for value in (mi, mo, so, cq, co)]
+    qkv, kv = shape((3, width, local), F32), shape((width, 2, local), F32)
+    return pl.pallas_call(
+        partial(finish_kernel, steps),
+        grid=(steps,),
+        out_shape=[shape(out.shape, BF), shape(image_grad.shape, F32), shape(text_grad.shape, F32), *sums, qkv, kv,
+                   shape((1, hidden), F32)] + [shape((1, width), F32)] * 7,
+        in_specs=[cut(out), cut(image_grad), whole(text_grad.shape), whole(early.shape), whole(late.shape)]
+        + [cut(value) for value in (mi, mo, so, cq, co)] + [cut(joint, 1)],
+        out_specs=[cut(out), cut(image_grad), whole(text_grad.shape)] + [cut(value) for value in sums]
+        + [cut(qkv, 1), cut(kv), whole((1, hidden))] + [whole((1, width))] * 7,
+        compiler_params=pltpu.CompilerParams(vmem_limit_bytes=VMEM_LIMIT),
+        cost_estimate=pl.CostEstimate(flops=1 << 22, bytes_accessed=28 << 20, transcendentals=0),
+    )(out, image_grad, text_grad, early, late, mi, mo, so, cq, co, joint)
+
+
 def body(sizes, image, text, grad_out, lengths, gain1, shift1, qkv, so, gain2, shift2, cq, kv, co, gain3, shift3, mi,
          in_bias, mo, out_bias):
     n = sizes["mp"]
@@ -1203,24 +1265,21 @@
     rows, width = image.shape
     local = so.shape[0]
     sizes = dict(sizes, share=share_of(local, sizes["dp"]))
-    qkv, kv = qkv.reshape(width, 3 * local), kv.reshape(width, 2 * local)
+    qkv, kv = jnp.transpose(qkv, (1, 0, 2)), kv.reshape(width, 2 * local)
     row = lambda value: value[None]
     (projected, normed1, mixed, totals, out, residual, dmixed, dtext, so_grad, cq_grad, co_grad, mi_pieces, mo_pieces,
-     in_bias_grad, vectors) = layer(
+     early) = layer(
         sizes, image, row(gain1), row(shift1), qkv, text, kv, row(lengths), row(gain2), row(shift2), row(gain3),
         row(shift3), row(in_bias), row(out_bias), so, cq, co, mi, mo, grad_out)
-    early = jnp.zeros((8 + -(-n // 2 // 8) * 8, width), F32)
-    early = lax.dynamic_update_slice(early, vectors, (0, 0))
-    early = lax.dynamic_update_slice(early, in_bias_grad[:, 0], (8, 0))
-    hidden = mi.shape[1]
     image_grad, text_grad, early, late, mi_sum, mo_sum, so_sum, cq_sum, co_sum, joint_sum = back(
         sizes, row(gain1), qkv, kv, text, residual, projected, normed1, mixed, totals, dmixed, dtext, early,
-        mi_pieces, mo_pieces, image, so_grad, cq_grad, co_grad, hidden)
+        mi_pieces, mo_pieces, image, so_grad, cq_grad, co_grad, mi.shape[1])
+    (out, image_grad, text_grad, mi_sum, mo_sum, so_sum, cq_sum, co_sum, qkv_sum, kv_sum, bias_sum, *vectors) = finish(
+        out, image_grad, text_grad, early, late, mi_sum, mo_sum, so_sum, cq_sum, co_sum, joint_sum)
+    g1, s1, g2, s2, g3, s3, ob = (value[0] for value in vectors)
     return (
-        out[None], image_grad[None], text_grad[None], late[0], late[1],
-        joint_sum[:, : 3 * local].astype(F32).reshape(width, 3, local), so_sum.astype(F32), early[2], early[3],
-        cq_sum.astype(F32), joint_sum[:, 3 * local :].astype(F32).reshape(width, 2, local), co_sum.astype(F32),
-        early[4], early[5], mi_sum.astype(F32), early[7, :hidden], mo_sum.astype(F32), early[6],
+        out[None], image_grad[None], text_grad[None], g1, s1, jnp.transpose(qkv_sum, (1, 0, 2)), so_sum, g2, s2, cq_sum,
+        kv_sum, co_sum, g3, s3, mi_sum, bias_sum[0], mo_sum, ob,
     )
 
 

time: 306 us -> 278 us (0.908); the launches traced: 301 us -> 277 us
  local copies, waits for them, and re-layouts: 19.5 us -> 2.42 us
  other arithmetic: 13.4 us -> 0 us
  Pallas kernels: 267 us -> 274 us
    pallas_call x0 -> x1, Pallas kernels: none -> 11.4 us  [finish(): pl.pallas_call(partial(finish_kernel, steps), grid=(steps,), out_shape=[s...]
    convert_element_type x5 -> x0, other arithmetic: 10.3 us -> none  [the longest x1 2.48 us: body(): mo_sum.astype(F32)]
    unnamed x22 -> x1, local copies, waits for them, and re-layouts: 10 us -> 2.42 us
    reshape x3 -> x0, local copies, waits for them, and re-layouts: 6.28 us -> none  [the longest x1 2.36 us: body(): joint_sum[:, :3 * local].astype(F32).reshape(width, 3, local)]
    pallas_call x1, Pallas kernels: 124 us -> 119 us  [back(): pl.pallas_call(partial(back_kernel, sizes), out_shape=[shape((size, width...]
    reshape x2 -> x0, other arithmetic: 3.14 us -> none  [the longest x1 1.64 us: body(): joint_sum[:, :3 * local].astype(F32).reshape(width, 3, local)]
where the time goes in v5:
time: 278 us; the launch traced here: 277 us
  Pallas kernels  274 us (99%)
    pallas_call x1, Pallas kernels, layer(): pl.pallas_call(partial(layer_kernel, sizes), out_shape=[shape((rows, 3 *...  143 us
    pallas_call x1, Pallas kernels, back(): pl.pallas_call(partial(back_kernel, sizes), out_shape=[shape((size, width...  119 us
    pallas_call x1, Pallas kernels, finish(): pl.pallas_call(partial(finish_kernel, steps), grid=(steps,), out_shape=[s...  11.4 us

profile of v5, /device:TPU:0, one launch (start us, length us, event | category | flops | bytes accessed | tf_op | source)
XLA Modules:
  0.0 277.5 jit_solution(8852065733808086597)
XLA Ops:
  1.3 2.4 copy.37
  3.7 142.7 %shard_map.322 = (bf16[1024,768]{1,0:T(8,128)(2,1)}, bf16[1024,1024]{1,0:T(8,128)(2,1)}, bf16[1024,256]{1,0:T(8,128)(2,1)}, f32[2,4,1,512]{3,2,1,0:T(1,128)}, bf...) custom-call(bf16[1024,1024]{1,0:T(8,128)(2,1)} %bitcast.33, ...), custom_call_target="tpu_custom_call" | custom-call | flops 23622320128 | bytes 50331648 | tf_op jit(solution)/shard_map/pallas_call | solution.py:841
  146.5 119.5 %shard_map.323 = (f32[256,1024]{1,0:T(8,128)}, f32[32,1024]{1,0:T(8,128)}, f32[16,1024]{1,0:T(8,128)}, f32[2,1024]{1,0:T(2,128)}, bf16[1024,1024]{1,0:T(8,128)(2...) custom-call(f32[1,1024]{1,0:T(1,128)} %bitcast.50, ...), custom_call_target="tpu_custom_call" | custom-call | flops 8589934592 | bytes 50331648 | tf_op jit(solution)/shard_map/pallas_call | solution.py:1186
  265.9 11.4 %shard_map.324 = (bf16[256,1024]{1,0:T(8,128)(2,1)}, f32[256,1024]{1,0:T(8,128)}, f32[32,1024]{1,0:T(8,128)}, f32[1024,1024]{1,0:T(8,128)}, f32[1024,1024]{1,0:T...) custom-call(bf16[256,1024]{1,0:T(8,128)(2,1)} %get-tuple-element.60., ...), custom_call_target="tpu_custom_call" | custom-call | flops 4194304 | bytes 29360128 | tf_op jit(solution)/shard_map/pallas_call | solution.py:1247

commit v6 on v5

--- a/solution.py
+++ b/solution.py
@@ -670,10 +670,10 @@
         return total
 
     feed(0, mine)
+    for item in wide:
+        item.step(3)
     n3_copy.wait()
     feed(1, mine)
-    for item in wide:
-        item.step(3)
     for item in wide:
         item.step(4)
     others = [lax.rem(mine + k, half) for k in range(1, half)]
@@ -1089,21 +1089,20 @@
     lax.fori_loop(0, width // tile_rows, qkv_grad, 0)
     bits = (dp // 2).bit_length() - 1
     small_steps = (so_steps, cq_steps, co_steps)
-    joint_steps[0]()
-    early_sum.turn()
+    for t in range(half - 1):
+        pass_on(t)
     for steps in small_steps:
         steps[2]()
-    joint_steps[1]()
-    for t in range(half - 1):
-        pass_on(t)
-    mi_steps[1]()
-    mo_steps[1]()
-    pass_on(half - 1)
+    joint_steps[0]()
     for k in range(1, bits):
         for steps in small_steps:
             steps[2 + k]()
     for steps in small_steps:
         steps[2 + bits]()
+    joint_steps[1]()
+    pass_on(half - 1)
+    mi_steps[1]()
+    mo_steps[1]()
     for k in range(bits):
         joint_steps[2 + k]()
     joint_steps[2 + bits]()
@@ -1120,6 +1119,7 @@
         for steps in small_steps:
             steps[4 + bits + k]()
 
+    early_sum.turn()
     for k in range(1, half):
         far_copy(lax.rem(mine + k, half)).wait()
         dn1_own[...] += far_recv[lax.rem(mine + half - k, half)].astype(F32)
@@ -1229,7 +1229,7 @@
 
 
 def finish(out, image_grad, text_grad, early, late, mi, mo, so, cq, co, joint):
-    steps = 8
+    steps = 2
     width, hidden = mi.shape
     local = so.shape[0]
 

time: 278 us -> 264 us (0.950)
  Pallas kernels: 274 us -> 260 us
    pallas_call x1, Pallas kernels: 119 us -> 108 us  [back(): pl.pallas_call(partial(back_kernel, sizes), out_shape=[shape((size, width...]
where the time goes in v6:
time: 264 us
  Pallas kernels  260 us (98%)
    pallas_call x1, Pallas kernels, layer(): pl.pallas_call(partial(layer_kernel, sizes), out_shape=[shape((rows, 3 *...  142 us
    pallas_call x1, Pallas kernels, back(): pl.pallas_call(partial(back_kernel, sizes), out_shape=[shape((size, width...  108 us
    pallas_call x1, Pallas kernels, finish(): pl.pallas_call(partial(finish_kernel, steps), grid=(steps,), out_shape=[s...  9.22 us

profile of v6, /device:TPU:0, one launch (start us, length us, event | category | flops | bytes accessed | tf_op | source)
XLA Modules:
  0.0 263.7 jit_solution(6350613057585699746)
XLA Ops:
  1.3 2.4 copy.37
  3.7 142.2 %shard_map.322 = (bf16[1024,768]{1,0:T(8,128)(2,1)}, bf16[1024,1024]{1,0:T(8,128)(2,1)}, bf16[1024,256]{1,0:T(8,128)(2,1)}, f32[2,4,1,512]{3,2,1,0:T(1,128)}, bf...) custom-call(bf16[1024,1024]{1,0:T(8,128)(2,1)} %bitcast.33, ...), custom_call_target="tpu_custom_call" | custom-call | flops 23622320128 | bytes 50331648 | tf_op jit(solution)/shard_map/pallas_call | solution.py:841
  145.9 108.4 %shard_map.323 = (f32[256,1024]{1,0:T(8,128)}, f32[32,1024]{1,0:T(8,128)}, f32[16,1024]{1,0:T(8,128)}, f32[2,1024]{1,0:T(2,128)}, bf16[1024,1024]{1,0:T(8,128)(2...) custom-call(f32[1,1024]{1,0:T(1,128)} %bitcast.50, ...), custom_call_target="tpu_custom_call" | custom-call | flops 8589934592 | bytes 50331648 | tf_op jit(solution)/shard_map/pallas_call | solution.py:1186
  254.3 9.2 %shard_map.324 = (bf16[256,1024]{1,0:T(8,128)(2,1)}, f32[256,1024]{1,0:T(8,128)}, f32[32,1024]{1,0:T(8,128)}, f32[1024,1024]{1,0:T(8,128)}, f32[1024,1024]{1,0:T...) custom-call(bf16[256,1024]{1,0:T(8,128)(2,1)} %get-tuple-element.60., ...), custom_call_target="tpu_custom_call" | custom-call | flops 4194304 | bytes 29360128 | tf_op jit(solution)/shard_map/pallas_call | solution.py:1247

commit v7 on v6

--- a/solution.py
+++ b/solution.py
@@ -682,27 +682,26 @@
     dn3_send[...] = sum_slots(lambda slot: nt(dhidden[slot, 1], mi_full[slot])).astype(BF)
     dn3_copy = remote(dn3_send, dn3_recv, pair_send.at[1], pair_recv.at[1], mate)
     dn3_copy.start()
-    out_send[...] = sum_slots(lambda slot: nn(active[slot, 1], mo_full[slot])).astype(BF)
-    out_copy = remote(out_send, out_recv, pair_send.at[2], pair_recv.at[2], mate)
-    out_copy.start()
     for slot in others:
         feed(0, slot)
     work[...] = sum_slots(lambda slot: nt(dhidden[slot, 0], mi_full[slot]))
-    out_part[...] = sum_slots(lambda slot: nn(active[slot, 0], mo_full[slot]))
     tile = min(256, width)
 
-    def wide_grads(slot):
+    def wide_grads(slot, first):
         inner = n3_pair.shape[0] * size
         hidden_grad = dhidden[slot].reshape(inner, hidden)
         grads = grad_pair[...].reshape(inner, width)
-        vectors[8 + slot : 9 + slot, 0:hidden] = jnp.sum(hidden_grad.astype(F32), axis=0, keepdims=True)
+        if first:
+            vectors[8 + slot : 9 + slot, 0:hidden] = jnp.sum(hidden_grad.astype(F32), axis=0, keepdims=True)
 
         def into(t, _):
             at = pl.ds(pl.multiple_of(t * tile, tile), tile)
             mi_full[slot, at, :] = tn(n3_pair[:, :, at].reshape(inner, tile), hidden_grad).astype(BF)
             return 0
 
-        lax.fori_loop(0, width // tile, into, 0)
+        if first:
+            lax.fori_loop(0, width // tile, into, 0)
+            return
 
         def back(t, _):
             at = pl.ds(pl.multiple_of(t * step, step), step)
@@ -711,14 +710,21 @@
 
         lax.fori_loop(0, hidden // step, back, 0)
 
-    vectors[...] = jnp.zeros_like(vectors)
-    for slot in range(half):
-        wide_grads(slot)
     mi_steps = Reduce(place, mi_full, mi_recv, mi_pieces, (reduce_send.at[0], reduce_recv.at[0])).phases()
     mo_steps = Reduce(place, mo_full, mo_recv, mo_pieces, (reduce_send.at[1], reduce_recv.at[1])).phases()
     wide_steps = [step for pair in zip(mi_steps, mo_steps) for step in pair]
-    for run in wide_steps[:2]:
-        run()
+    vectors[...] = jnp.zeros_like(vectors)
+    for slot in range(half):
+        wide_grads(slot, True)
+    wide_steps[0]()
+    out_send[...] = sum_slots(lambda slot: nn(active[slot, 1], mo_full[slot])).astype(BF)
+    out_copy = remote(out_send, out_recv, pair_send.at[2], pair_recv.at[2], mate)
+    out_copy.start()
+    out_part[...] = sum_slots(lambda slot: nn(active[slot, 0], mo_full[slot]))
+    for slot in range(half):
+        wide_grads(slot, False)
+    wide_steps[1]()
+    wide_steps[2]()
     dn3_copy.wait()
 
 
@@ -734,7 +740,7 @@
         r2[chunk, :] = value.astype(BF)
 
     in_chunks(size, ROWS_AT_ONCE, third_back)
-    wide_steps[2]()
+    wide_steps[3]()
     dcross[...] = nt(r2[...], co_full[...].reshape(n * local, width)).astype(BF)
 
     def cross_back(idx, _):
@@ -749,7 +755,7 @@
         return 0
 
     lax.fori_loop(0, all_pairs, cross_back, 0)
-    wide_steps[3]()
+    wide_steps[4]()
 
     def dtext_copy(k):
         return remote(dtext_send.at[place.along(k)], dtext_recv.at[place.m], dtext_ssem.at[k], dtext_rsem.at[k], place.peer(k))
@@ -782,7 +788,7 @@
         dmixed_send[k] = nt(r1[...], so_full[place.along(k)]).astype(BF)
         dmix_copy(k).start()
     dmixed[own_rows, :] = nt(r1[...], so_full[place.m]).astype(BF)
-    wide_steps[4]()
+    wide_steps[5]()
 
     stores = []
 
@@ -801,7 +807,6 @@
     small_grad(mixed_all, r1, so_full, so_grad, 1)
     small_grad(cross, r2, co_full, co_grad, 2)
 
-    wide_steps[5]()
     out_copy.wait()
 
     def finish_out(chunk):

time: 264 us -> 262 us (level)
  no operation moved by 1% of the time
where the time goes in v7:
time: 262 us; the launch traced here: 261 us
  Pallas kernels  258 us (98%)
    pallas_call x1, Pallas kernels, layer(): pl.pallas_call(partial(layer_kernel, sizes), out_shape=[shape((rows, 3 *...  140 us
    pallas_call x1, Pallas kernels, back(): pl.pallas_call(partial(back_kernel, sizes), out_shape=[shape((size, width...  108 us
    pallas_call x1, Pallas kernels, finish(): pl.pallas_call(partial(finish_kernel, steps), grid=(steps,), out_shape=[s...  9.22 us

profile of v7, /device:TPU:0, one launch (start us, length us, event | category | flops | bytes accessed | tf_op | source)
XLA Modules:
  0.0 261.5 jit_solution(5332709036246141325)
XLA Ops:
  1.3 2.4 copy.37
  3.7 139.8 %shard_map.322 = (bf16[1024,768]{1,0:T(8,128)(2,1)}, bf16[1024,1024]{1,0:T(8,128)(2,1)}, bf16[1024,256]{1,0:T(8,128)(2,1)}, f32[2,4,1,512]{3,2,1,0:T(1,128)}, bf...) custom-call(bf16[1024,1024]{1,0:T(8,128)(2,1)} %bitcast.33, ...), custom_call_target="tpu_custom_call" | custom-call | flops 23622320128 | bytes 50331648 | tf_op jit(solution)/shard_map/pallas_call | solution.py:846
  143.6 108.4 %shard_map.323 = (f32[256,1024]{1,0:T(8,128)}, f32[32,1024]{1,0:T(8,128)}, f32[16,1024]{1,0:T(8,128)}, f32[2,1024]{1,0:T(2,128)}, bf16[1024,1024]{1,0:T(8,128)(2...) custom-call(f32[1,1024]{1,0:T(1,128)} %bitcast.50, ...), custom_call_target="tpu_custom_call" | custom-call | flops 8589934592 | bytes 50331648 | tf_op jit(solution)/shard_map/pallas_call | solution.py:1191
  252.0 9.2 %shard_map.324 = (bf16[256,1024]{1,0:T(8,128)(2,1)}, f32[256,1024]{1,0:T(8,128)}, f32[32,1024]{1,0:T(8,128)}, f32[1024,1024]{1,0:T(8,128)}, f32[1024,1024]{1,0:T...) custom-call(bf16[256,1024]{1,0:T(8,128)(2,1)} %get-tuple-element.60., ...), custom_call_target="tpu_custom_call" | custom-call | flops 4194304 | bytes 29360128 | tf_op jit(solution)/shard_map/pallas_call | solution.py:1252

commit v8 on v7

--- a/solution.py
+++ b/solution.py
@@ -1003,7 +1003,6 @@
             dquery[hp, i] = jnp.zeros_like(dquery[hp, i])
         return 0
 
-    lax.fori_loop(0, n, prepare, 0)
     meet(partners)
     mi_steps[0]()
     mo_steps[0]()
@@ -1013,6 +1012,7 @@
     early_sum.begin()
     for k in offsets:
         text_copy(k).start()
+    lax.fori_loop(0, n, prepare, 0)
 
     plan = [[so_steps[1]], [cq_steps[1]], [co_steps[1]]]
     each = -(-len(plan) // (n * pairs))

time: 262 us -> 260 us (level)
  no operation moved by 1% of the time
where the time goes in v8:
time: 260 us
  Pallas kernels  256 us (98%)
    pallas_call x1, Pallas kernels, layer(): pl.pallas_call(partial(layer_kernel, sizes), out_shape=[shape((rows, 3 *...  140 us
    pallas_call x1, Pallas kernels, back(): pl.pallas_call(partial(back_kernel, sizes), out_shape=[shape((size, width...  107 us
    pallas_call x1, Pallas kernels, finish(): pl.pallas_call(partial(finish_kernel, steps), grid=(steps,), out_shape=[s...  9.22 us

profile of v8, /device:TPU:0, one launch (start us, length us, event | category | flops | bytes accessed | tf_op | source)
XLA Modules:
  0.0 259.9 jit_solution(5626383293558036595)
XLA Ops:
  1.3 2.4 copy.37
  3.7 139.8 %shard_map.322 = (bf16[1024,768]{1,0:T(8,128)(2,1)}, bf16[1024,1024]{1,0:T(8,128)(2,1)}, bf16[1024,256]{1,0:T(8,128)(2,1)}, f32[2,4,1,512]{3,2,1,0:T(1,128)}, bf...) custom-call(bf16[1024,1024]{1,0:T(8,128)(2,1)} %bitcast.33, ...), custom_call_target="tpu_custom_call" | custom-call | flops 23622320128 | bytes 50331648 | tf_op jit(solution)/shard_map/pallas_call | solution.py:846
  143.6 106.9 %shard_map.323 = (f32[256,1024]{1,0:T(8,128)}, f32[32,1024]{1,0:T(8,128)}, f32[16,1024]{1,0:T(8,128)}, f32[2,1024]{1,0:T(2,128)}, bf16[1024,1024]{1,0:T(8,128)(2...) custom-call(f32[1,1024]{1,0:T(1,128)} %bitcast.50, ...), custom_call_target="tpu_custom_call" | custom-call | flops 8589934592 | bytes 50331648 | tf_op jit(solution)/shard_map/pallas_call | solution.py:1191
  250.5 9.2 %shard_map.324 = (bf16[256,1024]{1,0:T(8,128)(2,1)}, f32[256,1024]{1,0:T(8,128)}, f32[32,1024]{1,0:T(8,128)}, f32[1024,1024]{1,0:T(8,128)}, f32[1024,1024]{1,0:T...) custom-call(bf16[256,1024]{1,0:T(8,128)(2,1)} %get-tuple-element.60., ...), custom_call_target="tpu_custom_call" | custom-call | flops 4194304 | bytes 29360128 | tf_op jit(solution)/shard_map/pallas_call | solution.py:1252
